TPU v7x, 32 devices: a whole 2x2x4 slice. The times are simulated.
32 devices in a mesh: hst: 8 (over z, x), tp: 4 (over y, core).
Axes of the slice: x: 2, y: 2, z: 4, core: 2. Of those that a mesh axis runs over, the one named last changes fastest.
Arguments:
- queries: bfloat16 [512, 4096], P('hst', 'tp')
- key_page_cache: bfloat16 [4096, 16, 1024], P('hst', None, 'tp')
- value_page_cache: bfloat16 [4096, 16, 1024], P('hst', None, 'tp'), may hold values from -5 to 5
- request_pages: int32 [512, 8], P('hst'), may hold values from 0 to 511, as said below
- context_length: int32 [512], P('hst'), may hold values from 2 to 128, as said below
- output_weight: bfloat16 [4096, 4096], P('tp'), may hold values from -0.09375 to 0.09375
- adapter_down_weight: bfloat16 [256, 64, 4096], P('hst', None, 'tp'), may hold values from -0.09375 to 0.09375
- adapter_up_weight: bfloat16 [256, 64, 4096], P('hst', None, 'tp'), may hold values from -0.75 to 0.75
- residual: bfloat16 [512, 4096], P('hst', 'tp'), may hold values from -6 to 6
- host_slot_adapter: int32 [256], P('hst'), may hold values from 0 to 255, as said below
- request_slot: int32 [512, 1], P('hst'), may hold values from 0 to 31; in each aligned block of 64 rows (0 to 63, 64 to 127, ...) at most 4 rows name the same one
Outputs:
- hidden_out: bfloat16 [512, 4096], P('hst', 'tp')
Inputs may be any that keep to these rules, and one draw needn't show every extreme that they name: `request_pages`: entries of one host are its pages 512 in some order: every page of the host belongs to exactly one request. `context_length`: some request of every host has exactly 128 cached tokens. `host_slot_adapter`: A host's 32 entries name different adapters; adapter a is owned by host a // 32. No owner serves more than 8 slots of one host, and some owner serves exactly 8 slots of every host. `request_slot`: at most 4 of the rows of one host name one slot.
All inputs are finite; a program needn't handle non-finite values.
Results may differ from a plain program's by a relative error of at most 0.0085.
Values may be sent and summed in bfloat16 or wider, within the bound.
No kernel may reach another device: no remote copies, remote signals or barrier semaphores. Data moves between devices by JAX's collectives and lax.ppermute only.
A program may use at most 128 MiB of HBM per device.

v0:
```python
import math

import jax
import jax.numpy as jnp
from jax import lax
from jax.sharding import PartitionSpec as P

HD = 128


ADAPTER_SCALE = 2.0


def attend_rows(queries, key_page_cache, value_page_cache, request_pages, context_length):
    row_count = queries.shape[0]
    kv_here = key_page_cache.shape[2] // HD
    heads_here = queries.shape[1] // HD
    group_size = heads_here // kv_here
    key_rows = key_page_cache[request_pages].reshape(row_count, -1, kv_here, HD)
    value_rows = value_page_cache[request_pages].reshape(row_count, -1, kv_here, HD)
    query_rows = queries.reshape(row_count, kv_here, group_size, HD)
    query_match_logits = jnp.einsum(
        "rkgd,rtkd->rkgt", query_rows, key_rows, preferred_element_type=jnp.float32
    ) / math.sqrt(HD)
    live_mask = jnp.arange(key_rows.shape[1])[None, :] < context_length[:, None]
    query_match_logits = jnp.where(live_mask[:, None, None, :], query_match_logits, -jnp.inf)
    attn_weights = jax.nn.softmax(query_match_logits, axis=-1).astype(jnp.bfloat16)
    attended = jnp.einsum(
        "rkgt,rtkd->rkgd", attn_weights, value_rows, preferred_element_type=jnp.float32
    )
    return attended.astype(jnp.bfloat16).reshape(row_count, heads_here * HD)


def slot_dispatch(request_slot, slot_total, slot_capacity):
    chosen = request_slot[:, 0]
    row_order = jnp.arange(chosen.shape[0])
    same_slot = chosen[:, None] == chosen[None, :]
    earlier = row_order[None, :] < row_order[:, None]
    before = jnp.sum(same_slot & earlier, axis=1)
    target = chosen * slot_capacity + before
    return jnp.arange(slot_total * slot_capacity)[:, None] == target[None, :]


def owner_slots(host_slot_adapter, owned_total):
    owners = host_slot_adapter // owned_total
    slot_order = jnp.arange(owners.shape[0])
    same_owner = owners[:, None] == owners[None, :]
    before = jnp.sum(same_owner & (slot_order[None, :] < slot_order[:, None]), axis=1)
    return (owners, before)


def local(
    queries,
    key_page_cache,
    value_page_cache,
    request_pages,
    context_length,
    output_weight,
    adapter_down_weight,
    adapter_up_weight,
    residual,
    host_slot_adapter,
    request_slot,
):
    attended = attend_rows(queries, key_page_cache, value_page_cache, request_pages, context_length)
    slot_total = host_slot_adapter.shape[0]
    row_count = attended.shape[0]
    slot_capacity = 2 * row_count // slot_total
    feature_here = attended.shape[1]
    local_output = adapter_up_weight.shape[2]
    owned_total = adapter_up_weight.shape[0]
    host_count = lax.axis_size("hst")
    per_owner = 2 * slot_total // host_count
    dispatch = slot_dispatch(request_slot, slot_total, slot_capacity)
    blocks = jnp.dot(dispatch.astype(jnp.bfloat16), attended, preferred_element_type=jnp.float32)
    blocks = blocks.astype(jnp.bfloat16).reshape(slot_total, slot_capacity, feature_here)
    owners, position = owner_slots(host_slot_adapter, owned_total)
    everyone = lax.all_gather(host_slot_adapter, "hst", axis=0, tiled=True)
    request_table = everyone.reshape(host_count, slot_total)
    owned_here = request_table // owned_total == lax.axis_index("hst")
    slot_order = jnp.arange(slot_total)
    earlier = slot_order[None, :] < slot_order[:, None]
    ahead_count = jnp.sum(owned_here[:, None, :] & earlier[None, :, :], axis=2)
    select_mask = owned_here[:, None, :] & (
        ahead_count[:, None, :] == jnp.arange(per_owner)[None, :, None]
    )
    local_index = request_table % owned_total
    picked_adapters = jnp.sum(jnp.where(select_mask, local_index[:, None, :], 0), axis=2)
    filled_slots = jnp.any(select_mask, axis=2)[:, :, None, None]
    down_outgoing = jnp.where(filled_slots, adapter_down_weight[picked_adapters], 0)
    up_outgoing = jnp.where(filled_slots, adapter_up_weight[picked_adapters], 0)
    got_down, got_up = (
        lax.all_to_all(down_outgoing, "hst", split_axis=0, concat_axis=0, tiled=True),
        lax.all_to_all(up_outgoing, "hst", split_axis=0, concat_axis=0, tiled=True),
    )
    slot_down = got_down[owners, position]
    slot_up_weight = got_up[owners, position]
    partial_sum = jnp.einsum("scd,skd->sck", blocks, slot_down, preferred_element_type=jnp.float32)
    reduced_activations = lax.psum(partial_sum, "tp").astype(jnp.bfloat16)
    adapter_blocks = jnp.einsum(
        "anp,api->ani", reduced_activations, slot_up_weight, preferred_element_type=jnp.float32
    )
    adapter_rows = jnp.dot(
        dispatch.astype(jnp.float32).T,
        adapter_blocks.reshape(slot_total * slot_capacity, local_output),
        precision=lax.Precision.HIGHEST,
    )
    base_terms = jnp.dot(attended, output_weight, preferred_element_type=jnp.float32)
    base_output = lax.psum_scatter(
        base_terms.astype(jnp.bfloat16), "tp", scatter_dimension=1, tiled=True
    ).astype(jnp.float32)
    return (residual.astype(jnp.float32) + base_output + ADAPTER_SCALE * adapter_rows).astype(
        jnp.bfloat16
    )


def solution(mesh):
    in_specs = (
        P("hst", "tp"),
        P("hst", None, "tp"),
        P("hst", None, "tp"),
        P("hst", None),
        P("hst"),
        P("tp", None),
        P("hst", None, "tp"),
        P("hst", None, "tp"),
        P("hst", "tp"),
        P("hst"),
        P("hst", None),
    )
    out_specs = P("hst", "tp")
    return jax.shard_map(local, mesh=mesh, in_specs=in_specs, out_specs=out_specs, check_vma=False)
```

profile of v0, /device:TPU:0, one launch (start us, length us, event | category | flops | bytes accessed | tf_op | source)
XLA Modules:
  0.0 450.3 jit_solution(12263486557950360750)
XLA Ops:
  6.5 1.2 dynamic-slice
  8.4 0.9 dynamic-update-slice
  9.3 13.1 %all-reduce = s32[256]{0:T(256)S(1)} all-reduce(s32[256]{0:T(256)S(1)} %dynamic-update-slice), channel_id=1, replica_groups=mesh['hst'=8,'tp'=4] {'hst'}, use_global_device_ids=true, to_apply=%add | all-reduce | flops 256 | bytes 2048
  22.4 0.1 reshape.146
  22.5 0.2 convert_reduce_fusion
  22.7 0.2 fusion.28
  22.9 0.2 select_reduce_fusion
  23.1 0.1 reshape.166
  23.2 7.6 %gather_fusion.2 = bf16[64,64,1024]{2,1,0:T(8,128)(2,1)} fusion(bf16[32,64,1024]{2,1,0:T(8,128)(2,1)} %param.17, s32[1024]{0:T(1024)S(1)} %pad_clamp_fusion), kind=kCustom, calls=%fused_computation.2 | custom fusion | bytes 16777472 | tf_op jit(solution)/shard_map/gather | solution.py:90
  30.8 7.6 %gather_fusion.4 = bf16[64,64,1024]{2,1,0:T(8,128)(2,1)} fusion(bf16[32,64,1024]{2,1,0:T(8,128)(2,1)} %param.18, s32[1024]{0:T(1024)S(1)} %pad_clamp_fusion), kind=kCustom, calls=%fused_computation.4 | custom fusion | bytes 16777472 | tf_op jit(solution)/shard_map/gather | solution.py:91
  38.4 9.2 %broadcast_select_fusion = (bf16[8,8,64,1024]{3,2,1,0:T(8,128)(2,1)}, bf16[8,8,64,1024]{3,2,1,0:T(8,128)(2,1)S(1)}) fusion(bf16[8,8,64,1024]{3,2,1,0:T(8,128)(2,1)} %bitcast.35, pred[8,8]{1,0:T(8,128)(4,1)S(1)} %fusion.28, bf16[8,8,64,1024]{3,2,1,0:T(8,128)(2,1)} %bitcast.34), kind=kLoop, calls=%fused_computation.7 | loop fusion | flops 8388608 | bytes 33554496 | tf_op jit(solution)/shard_map/jit(_where)/select_n | solution.py:91
  47.6 184.1 %all_to_all.10 = bf16[8,8,64,1024]{3,2,1,0:T(8,128)(2,1)} all-to-all(bf16[8,8,64,1024]{3,2,1,0:T(8,128)(2,1)S(1)} %get-tuple-element.6), channel_id=1, replica_groups=mesh['hst'=8,'tp'=4] {'hst'}, dimensions={0} | all-to-all | bytes 16777216 | tf_op jit(solution)/shard_map/all_to_all | solution.py:93
  231.7 5.2 %all-to-all-start.1 = ((bf16[8,8,64,1024]{3,2,1,0:T(8,128)(2,1)}), bf16[8,8,64,1024]{3,2,1,0:T(8,128)(2,1)}, u32[]{:S(2)}, u32[]{:S(2)}) async-start(bf16[8,8,64,1024]{3,2,1,0:T(8,128)(2,1)} %get-tuple-element.5), calls=%async_computation.2 | async-start | bytes 16777216 | tf_op jit(solution)/shard_map/all_to_all | solution.py:94
  236.9 0.0 reduce-scatter.2.cloned.1.call-start
  237.0 0.0 copy-done.2
  237.0 0.1 copy.17
  237.1 0.1 reshape.150
  237.2 5.1 %gather_fusion = bf16[512,16,256]{2,1,0:T(8,128)(2,1)} fusion(bf16[512,16,256]{2,1,0:T(8,128)(2,1)} %param.12, s32[1024]{0:T(1024)S(1)} %pad_clamp_fusion.1), kind=kCustom, calls=%fused_computation | custom fusion | bytes 8390656 | tf_op jit(solution)/shard_map/gather | solution.py:19
  242.3 7.0 %reshape.141 = bf16[64,128,2,128]{3,2,1,0:T(2,128)(2,1)} reshape(bf16[512,16,256]{2,1,0:T(8,128)(2,1)} %gather_fusion) | data formatting | bytes 8388608 | tf_op jit(solution)/shard_map/reshape | solution.py:19
  249.3 0.0 copy-done.1
  249.3 0.1 reshape.142
  249.3 5.2 %gather_fusion.1 = bf16[512,16,256]{2,1,0:T(8,128)(2,1)} fusion(bf16[512,16,256]{2,1,0:T(8,128)(2,1)} %param.13, s32[1024]{0:T(1024)S(1)} %pad_clamp_fusion.1), kind=kCustom, calls=%fused_computation.1 | custom fusion | bytes 8390656 | tf_op jit(solution)/shard_map/gather | solution.py:20
  254.5 6.9 %reshape.143 = bf16[64,128,2,128]{3,2,1,0:T(2,128)(2,1)} reshape(bf16[512,16,256]{2,1,0:T(8,128)(2,1)} %gather_fusion.1) | data formatting | bytes 8388608 | tf_op jit(solution)/shard_map/reshape | solution.py:20
  261.5 0.0 copy-done.3
  261.5 0.1 iota_compare_fusion.5
  261.5 4.7 %fusion.39 = (f32[64,2,4]{2,1,0:T(2,128)S(1)}, f32[64,2,4,128]{3,2,1,0:T(4,128)S(1)}) fusion(bf16[64,2,4,128]{3,2,1,0:T(4,128)(2,1)S(1)} %reshape.142, bf16[64,128,2,128]{3,2,1,0:T(2,128)(2,1)} %reshape.141, pred[64,128]{1,0:T(8,128)(4,1)S(1)} %iota_compare_fusion.5), kind=kOutput, calls=%fused_computation.69 | convolution fusion | flops 17039488 | bytes 4597760 | tf_op jit(solution)/shard_map/sub | solution.py:27
  266.2 3.4 fusion.12
  269.7 0.1 reshape.144
  269.8 0.0 copy-start.4
  269.8 0.0 copy-start.5
  269.8 5.8 %convolution_convert_fusion = bf16[64,4096]{1,0:T(8,128)(2,1)} fusion(bf16[64,1024]{1,0:T(8,128)(2,1)S(1)} %reshape.144, bf16[1024,4096]{1,0:T(8,128)(2,1)} %param.16), kind=kOutput, calls=%fused_computation.9 | convolution fusion | flops 537133056 | bytes 9043968 | tf_op jit(solution)/shard_map/dot_general | solution.py:108
  275.6 0.0 reduce-scatter.2.cloned.1.call-update
  275.6 0.0 copy-done.4
  275.6 0.2 convert_reduce_fusion.1
  275.8 0.2 convolution_convert_fusion.1
  276.0 0.1 reshape.145
  276.1 0.0 copy-done.5
  276.1 0.2 convert_reduce_fusion.2
  276.3 6.2 %gather_fusion.3 = bf16[32,64,1024]{2,1,0:T(8,128)(2,1)} fusion(bf16[8,8,64,1024]{3,2,1,0:T(8,128)(2,1)} %all_to_all.10, s32[32]{0:T(128)S(1)} %fusion.38), kind=kCustom, calls=%fused_computation.3 | custom fusion | bytes 8388864 | tf_op jit(solution)/shard_map/gather | solution.py:96
  282.5 135.7 %all-to-all-done.1 = bf16[8,8,64,1024]{3,2,1,0:T(8,128)(2,1)} async-done(((bf16[8,8,64,1024]{3,2,1,0:T(8,128)(2,1)}), bf16[8,8,64,1024]{3,2,1,0:T(8,128)(2,1)}, u32[]{:S(2)}, u32[]{:S(2)}) %all-to-all-start.1) | async-done | bytes 8388640 | tf_op jit(solution)/shard_map/all_to_all | solution.py:94
  418.2 6.1 %gather_fusion.5 = bf16[32,64,1024]{2,1,0:T(8,128)(2,1)} fusion(bf16[8,8,64,1024]{3,2,1,0:T(8,128)(2,1)} %all-to-all-done.1, s32[32]{0:T(128)S(1)} %fusion.38), kind=kCustom, calls=%fused_computation.5 | custom fusion | bytes 8388864 | tf_op jit(solution)/shard_map/gather | solution.py:97
  424.4 3.4 fusion.42
  427.8 10.7 %psum.7 = bf16[32,4,64]{2,1,0:T(4,128)(2,1)S(1)} all-reduce(f32[32,4,64]{2,1,0:T(4,128)S(1)} %fusion.42), channel_id=1, replica_groups=mesh['hst'=8,'tp'=4] {'tp'}, use_global_device_ids=true, to_apply=%region_8.9 | all-reduce | flops 8192 | bytes 49152 | tf_op jit(solution)/shard_map/psum | solution.py:99
  438.5 2.8 fusion.43
  441.3 0.2 reshape.147
  441.5 0.0 reduce-scatter.2.cloned.1.call-done
  441.5 0.0 copy-done
  441.5 1.9 fusion.11
  (15 shorter events, 0.1 us)
Async XLA Ops:
  231.7 5.2 %copy-start.2 = (s32[64,8]{0,1:T(8,128)S(1)}, s32[64,8]{0,1:T(8,128)}, u32[]{:S(2)}) copy-start(s32[64,8]{0,1:T(8,128)} %param.14) | copy-start | bytes 6148
  231.7 186.5 %all-to-all-start.1 = ((bf16[8,8,64,1024]{3,2,1,0:T(8,128)(2,1)}), bf16[8,8,64,1024]{3,2,1,0:T(8,128)(2,1)}, u32[]{:S(2)}, u32[]{:S(2)}) async-start(bf16[8,8,64,1024]{3,2,1,0:T(8,128)(2,1)} %get-tuple-element.5), calls=%async_computation.2 | async-start | bytes 16777216 | tf_op jit(solution)/shard_map/all_to_all | solution.py:94
  236.9 204.6 %reduce-scatter.2.cloned.1.call-start = ((), (), s32[]{:S(2)}) async-start(), calls=%async_computation.3 | async-start | bytes 655360 | tf_op jit(solution)/shard_map/reduce_scatter | solution.py:109
  242.3 7.0 %copy-start.1 = (bf16[64,1024]{1,0:T(8,128)(2,1)S(1)}, bf16[64,1024]{1,0:T(8,128)(2,1)}, u32[]{:S(2)}) copy-start(bf16[64,1024]{1,0:T(8,128)(2,1)} %param.11) | copy-start | bytes 393220
  254.5 6.9 %copy-start.3 = (s32[64]{0:T(128)S(1)}, s32[64]{0:T(128)}, u32[]{:S(2)}) copy-start(s32[64]{0:T(128)} %param.15) | copy-start | bytes 772
  269.8 5.8 %copy-start.4 = (s32[64,1]{0,1:T(1,128)S(1)}, s32[64,1]{0,1:T(1,128)}, u32[]{:S(2)}) copy-start(s32[64,1]{0,1:T(1,128)} %param.21) | copy-start | bytes 772
  269.8 6.4 %copy-start.5 = (s32[32]{0:T(128)S(1)}, s32[32]{0:T(128)}, u32[]{:S(2)}) copy-start(s32[32]{0:T(128)} %param.20) | copy-start | bytes 388
  424.4 17.2 %copy-start = (bf16[64,1024]{1,0:T(8,128)(2,1)S(1)}, bf16[64,1024]{1,0:T(8,128)(2,1)}, u32[]{:S(2)}) copy-start(bf16[64,1024]{1,0:T(8,128)(2,1)} %param.19) | copy-start | bytes 393220
Sparse Core Ops, SparseCore 0:
  275.7 22.9 reduce-scatter.1
where the time goes:
time: 451 us; the launch traced here: 450 us
  blocking collectives  208 us (46%)
  waiting for transfers between devices  136 us (30%)
  local copies, waits for them, and re-layouts  54.6 us (12%)
  matrix products  22.3 us (5%)
  between operations  14.2 us (3%)
  other arithmetic  10.4 us (2%)
  starting transfers between devices  5.21 us (1%)
    all_to_all x1, blocking collectives, local(): lax.all_to_all(down_outgoing, 'hst', split_axis=0, concat_axis=0, tiled=T...  184 us
    all_to_all x1, waiting for transfers between devices, local(): lax.all_to_all(up_outgoing, 'hst', split_axis=0, concat_axis=0, tiled=True)  136 us
    unnamed x1, blocking collectives  13.1 us
    psum x1, blocking collectives, local(): reduced_activations = lax.psum(partial_sum, 'tp').astype(jnp.bfloat16)  10.7 us
    select_n x1, other arithmetic, local(): up_outgoing = jnp.where(filled_slots, adapter_up_weight[picked_adapters], 0)  9.21 us
  transfers between devices with their start and end apart: 2, of which 1 were waited for; matrix products, arithmetic and copies ran while one was open for 13% of the time, Pallas kernels for 0%

commit v1 on v0

v1 whole, which is shorter than its diff:
```python
import functools
import math

import jax
import jax.numpy as jnp
from jax import lax
from jax.experimental import pallas as pl
from jax.experimental.pallas import tpu as pltpu
from jax.sharding import PartitionSpec as P

HD = 128
LANES = 128
HEAD_ROWS = 8
GROUP = 16
ADAPTER_SCALE = 2.0
CAP = 4
FIRST = 20
CHUNKS = 4

MIB = 1 << 20
NT = (((1,), (1,)), ((), ()))
TN = (((0,), (0,)), ((), ()))
NN = (((1,), (0,)), ((), ()))


def iota(shape, axis):
    return lax.broadcasted_iota(jnp.int32, shape, axis)


def pair_rows(slot_total, host_count):
    return CAP * (2 * slot_total // host_count)


def up_to(value, step):
    return -(-value // step) * step


def copies(source, target, sem, count):
    cut = source.shape[0] // count
    return [
        pltpu.make_async_copy(
            source.at[pl.ds(i * cut, cut)], target.at[pl.ds(i * cut, cut)], sem.at[i]
        )
        for i in range(count)
    ]


def in_hbm(*arrays):
    return [pltpu.with_memory_space_constraint(a, pltpu.HBM) for a in arrays]


def attention_kernel(owned_total, host_count, tp_count, room, *refs):
    pages_hbm, length_hbm, query_hbm, slot_hbm, stock_hbm, keys_hbm, values_hbm = refs[:7]
    down_hbm, output_hbm, attended_ref, place_ref, down_ref = refs[7:12]
    evens = tp_count // 2
    even_refs, odd_ref, refs = refs[12 : 12 + evens], refs[12 + evens], refs[13 + evens :]
    block_refs, refs = refs[:host_count], refs[host_count:]
    (
        pages_ref,
        length_ref,
        query_ref,
        slot_ref,
        stock_ref,
        keys,
        values,
        output,
        query_rows,
        outcome,
        packed,
        numbers,
        counts,
        small_sem,
        key_sem,
        value_sem,
        down_sem,
        output_sem,
    ) = refs
    row_count, feature_here = query_ref.shape
    page_total, page, kv_width = keys_hbm.shape
    heads = feature_here // HD
    kv_here = kv_width // HD
    share = heads // kv_here
    most_pages = pages_ref.shape[0]
    context = most_pages * page

    small_moves = [
        pltpu.make_async_copy(source, target, small_sem.at[i])
        for i, (source, target) in enumerate(
            (
                (query_hbm, query_ref),
                (slot_hbm, slot_ref),
                (stock_hbm, stock_ref),
                (pages_hbm, pages_ref),
                (length_hbm, length_ref),
            )
        )
    ]
    key_moves = copies(keys_hbm, keys, key_sem, CHUNKS)
    value_moves = copies(values_hbm, values, value_sem, CHUNKS)
    down_moves = copies(down_hbm, down_ref, down_sem, CHUNKS)
    width = output_hbm.shape[1] // tp_count
    output_moves = []
    for k in range(tp_count):
        columns = pl.ds(pl.multiple_of((lax.axis_index("tp") ^ k) * width, width), width)
        output_moves.append(copies(output_hbm.at[:, columns], output.at[k], output_sem.at[k], 2))
    for move in small_moves + key_moves:
        move.start()
    packed[...] = jnp.zeros_like(packed)
    numbers[...] = jnp.zeros_like(numbers)
    for o in range(host_count):
        counts[o] = 0
    for move in small_moves:
        move.wait()

    if heads < HEAD_ROWS:
        query_rows[...] = jnp.zeros_like(query_rows)
    for j in range(heads):
        query_rows[pl.ds(j, row_count, stride=HEAD_ROWS), :] = query_ref[
            :, j * HD : (j + 1) * HD
        ].astype(jnp.float32)

    me = lax.axis_index("hst")
    pad = up_to(room, 8)

    def count(r, most):
        adapter = stock_ref[0, slot_ref[0, r]]
        owner = lax.div(adapter, owned_total)
        before = counts[owner]
        counts[owner] = before + 1
        block = owner ^ me
        fits = before < room
        place_ref[r] = jnp.where(fits, block * room + before, host_count * room)
        where = jnp.where(fits, block * pad + before, host_count * pad)
        number = jnp.full((1, LANES), adapter - owner * owned_total + 1, jnp.int32)
        numbers[pl.ds(where, 1), :] = number.astype(jnp.float32)
        return jnp.maximum(most, before)

    most = lax.fori_loop(0, row_count, count, jnp.int32(0))
    over = jnp.where(jnp.full((8, LANES), most, jnp.int32) >= room, 1.0, 0.0)

    for move in key_moves[: CHUNKS // 2]:
        move.wait()
    for move in value_moves:
        move.start()
    for move in key_moves[CHUNKS // 2 :]:
        move.wait()

    head_of = iota((HEAD_ROWS, HD), 0) // share

    def tile_of(r):
        return pl.ds(pl.multiple_of(r * HEAD_ROWS, HEAD_ROWS), HEAD_ROWS)

    def some_scores(step, carry):
        first = step * GROUP
        scores = []
        for i in range(GROUP):
            r = first + i
            rows = query_rows[tile_of(r), :]
            wide = jnp.concatenate(
                [jnp.where(head_of == c, rows, 0.0) for c in range(kv_here)], axis=1
            ).astype(jnp.bfloat16)
            held = jnp.concatenate([keys[pages_ref[p, r]] for p in range(most_pages)], axis=0)
            part = lax.dot_general(wide, held, NT, preferred_element_type=jnp.float32)
            live = iota((HEAD_ROWS, context), 1) < length_ref[r]
            scores.append(jnp.where(live, part * (1.0 / math.sqrt(HD)), -jnp.inf))
        score = jnp.concatenate(scores, axis=0)
        weight = jnp.exp(score - jnp.max(score, axis=1, keepdims=True))
        weight = weight / jnp.sum(weight, axis=1, keepdims=True)
        size = GROUP * HEAD_ROWS
        outcome[pl.ds(pl.multiple_of(step * size, size), size), :] = weight
        return carry

    def some_values(step, carry):
        first = step * GROUP
        for i in range(GROUP):
            r = first + i
            held = jnp.concatenate([values[pages_ref[p, r]] for p in range(most_pages)], axis=0)
            part = lax.dot_general(
                outcome[tile_of(r), :].astype(jnp.bfloat16),
                held,
                NN,
                preferred_element_type=jnp.float32,
            )
            result = part[:, :HD]
            for c in range(1, kv_here):
                result = jnp.where(head_of == c, part[:, c * HD : (c + 1) * HD], result)
            outcome[tile_of(r), :] = result
            packed[tile_of(place_ref[r]), :] = result
        return carry

    lax.fori_loop(0, row_count // GROUP, some_scores, 0)
    for move in value_moves[: CHUNKS // 2]:
        move.wait()
    for moves in output_moves:
        for move in moves:
            move.start()
    for move in value_moves[CHUNKS // 2 :]:
        move.wait()
    lax.fori_loop(0, row_count // GROUP, some_values, 0)
    for move in down_moves:
        move.start()

    lane = iota((8, LANES), 1)
    size = room * HEAD_ROWS
    for k in range(host_count):
        tile = jnp.where(lane == LANES - 1, over, 0.0)
        for b in range(pad // 8):
            tile = jnp.where(lane == b, numbers[k * pad + 8 * b : k * pad + 8 * b + 8], tile)
        block_refs[k][...] = jnp.concatenate(
            [packed[k * size : (k + 1) * size], tile], axis=0
        ).astype(jnp.bfloat16)
    for j in range(heads):
        attended_ref[:, j * HD : (j + 1) * HD] = outcome[
            pl.ds(j, row_count, stride=HEAD_ROWS), :
        ].astype(jnp.bfloat16)
    rows = attended_ref[...]
    for k in range(tp_count):
        for move in output_moves[k]:
            move.wait()
        product = jnp.dot(rows, output[k], preferred_element_type=jnp.float32)
        if k % 2 == 0:
            even_refs[k // 2][...] = product.astype(jnp.bfloat16)
        else:
            first = k // 2 * row_count
            odd_ref[first : first + row_count] = product.astype(jnp.bfloat16)
    for move in down_moves:
        move.wait()


def attend(
    queries, keys, values, pages, lengths, slots, stock, down, output, owned_total, hosts, room
):
    row_count, feature_here = queries.shape
    tp_count = output.shape[1] // feature_here
    spec = pl.BlockSpec(memory_space=pltpu.VMEM)
    small = pl.BlockSpec(memory_space=pltpu.SMEM)
    far = pl.BlockSpec(memory_space=pl.ANY)
    evens = tp_count // 2
    base = jax.ShapeDtypeStruct((row_count, feature_here), jnp.bfloat16)
    odd = jax.ShapeDtypeStruct((evens * row_count, feature_here), jnp.bfloat16)
    block = jax.ShapeDtypeStruct((room * HEAD_ROWS + 8, LANES), jnp.bfloat16)
    outs = pl.pallas_call(
        functools.partial(attention_kernel, owned_total, hosts, tp_count, room),
        name="attend",
        out_shape=[
            jax.ShapeDtypeStruct((row_count, feature_here), jnp.bfloat16),
            jax.ShapeDtypeStruct((row_count,), jnp.int32),
            pltpu.VMEM(down.shape, jnp.bfloat16),
        ]
        + [base] * evens
        + [odd]
        + [block] * hosts,
        in_specs=[far] * 9,
        out_specs=[spec, small, spec] + [spec] * (evens + 1 + hosts),
        scratch_shapes=[
            pltpu.SMEM(pages.shape, jnp.int32),
            pltpu.SMEM(lengths.shape, jnp.int32),
            pltpu.VMEM(queries.shape, jnp.bfloat16),
            pltpu.SMEM(slots.shape, jnp.int32),
            pltpu.SMEM(stock.shape, jnp.int32),
            pltpu.VMEM(keys.shape, jnp.bfloat16),
            pltpu.VMEM(values.shape, jnp.bfloat16),
            pltpu.VMEM((tp_count, feature_here, feature_here), jnp.bfloat16),
            pltpu.VMEM((row_count * HEAD_ROWS, HD), jnp.float32),
            pltpu.VMEM((row_count * HEAD_ROWS, HD), jnp.float32),
            pltpu.VMEM(((hosts * room + 1) * HEAD_ROWS, HD), jnp.float32),
            pltpu.VMEM((hosts * up_to(room, 8) + 8, LANES), jnp.float32),
            pltpu.SMEM((hosts,), jnp.int32),
            pltpu.SemaphoreType.DMA((5,)),
            pltpu.SemaphoreType.DMA((CHUNKS,)),
            pltpu.SemaphoreType.DMA((CHUNKS,)),
            pltpu.SemaphoreType.DMA((CHUNKS,)),
            pltpu.SemaphoreType.DMA((tp_count, 2)),
        ],
        compiler_params=pltpu.CompilerParams(vmem_limit_bytes=32 * MIB),
        cost_estimate=pl.CostEstimate(
            flops=4 * row_count * HEAD_ROWS * 128 * feature_here,
            bytes_accessed=4 * keys.size + 2 * output.size + 2 * down.size,
            transcendentals=row_count * HEAD_ROWS * 128,
        ),
    )(*in_hbm(pages, lengths, queries, slots, stock, keys, values, down, output))
    return outs[:3], outs[3 : 3 + evens], outs[3 + evens], outs[4 + evens :]


def shrink_kernel(host_count, room, *refs):
    blocks = refs[:host_count]
    down_ref, up_hbm, partial_ref, number_ref, over_ref, up_ref = refs[host_count : host_count + 6]
    tiles, total, up_sem = refs[host_count + 6 :]
    up_moves = copies(up_hbm, up_ref, up_sem, CHUNKS)
    for move in up_moves:
        move.start()
    heads = down_ref.shape[1] // HD
    rows_all = host_count * room
    size = room * HEAD_ROWS
    width = 256
    rank = LANES // 2
    over = jnp.float32(0)
    lane = iota((8, LANES), 1)
    for k in range(host_count):
        tiles[k * size : (k + 1) * size] = blocks[k][:size].astype(jnp.float32)
        tile = blocks[k][size:].astype(jnp.float32)
        over = jnp.maximum(over, jnp.max(jnp.where(lane == LANES - 1, tile, 0.0)))
        for b in range(up_to(room, 8) // 8):
            rest = min(8, room - 8 * b)
            column = jnp.sum(jnp.where(lane == b, tile, 0.0), axis=1, keepdims=True)
            column = jnp.broadcast_to(column, (8, LANES))
            number_ref[k * room + 8 * b : k * room + 8 * b + rest] = column[:rest]
    over_ref[0] = (over > 0).astype(jnp.int32)
    rows = jnp.concatenate(
        [tiles[pl.ds(j, rows_all, stride=HEAD_ROWS), :].astype(jnp.bfloat16) for j in range(heads)],
        axis=1,
    )
    number = number_ref[...]
    own = (iota(number.shape, 1) // rank).astype(jnp.float32) + 1.0
    for step in range(down_ref.shape[0] // width):
        product = lax.dot_general(
            rows,
            down_ref[step * width : (step + 1) * width],
            NT,
            preferred_element_type=jnp.float32,
        )
        add = jnp.zeros_like(number) if step == 0 else total[...]
        for i in range(width // LANES):
            piece = product[:, i * LANES : (i + 1) * LANES]
            first = 2.0 * (step * (width // LANES) + i)
            add = jnp.where(number == own + first, piece + add, add)
        total[...] = add
    full = total[...]
    full = full + pltpu.roll(full, rank, 1)
    half = rows_all // 2
    left = iota((half, LANES), 1) < rank
    partial_ref[...] = jnp.where(left, full[:half], full[half:]).astype(jnp.bfloat16)
    for move in up_moves:
        move.wait()


def shrink(blocks, down, up, room):
    host_count = len(blocks)
    rows = host_count * room
    spec = pl.BlockSpec(memory_space=pltpu.VMEM)
    return pl.pallas_call(
        functools.partial(shrink_kernel, host_count, room),
        name="shrink",
        out_shape=(
            jax.ShapeDtypeStruct((rows // 2, LANES), jnp.bfloat16),
            jax.ShapeDtypeStruct((rows, LANES), jnp.float32),
            jax.ShapeDtypeStruct((1,), jnp.int32),
            pltpu.VMEM(up.shape, jnp.bfloat16),
        ),
        in_specs=[spec] * (host_count + 1) + [pl.BlockSpec(memory_space=pl.ANY)],
        out_specs=(spec, spec, pl.BlockSpec(memory_space=pltpu.SMEM), spec),
        scratch_shapes=[
            pltpu.VMEM((rows * HEAD_ROWS, HD), jnp.float32),
            pltpu.VMEM((rows, LANES), jnp.float32),
            pltpu.SemaphoreType.DMA((CHUNKS,)),
        ],
        compiler_params=pltpu.CompilerParams(vmem_limit_bytes=12 * MIB),
        cost_estimate=pl.CostEstimate(
            flops=2 * rows * down.size, bytes_accessed=2 * down.size, transcendentals=0
        ),
    )(*blocks, down, *in_hbm(up))


def expand_kernel(part_count, host_count, *refs):
    parts, (number_ref, up_ref) = refs[:part_count], refs[part_count : part_count + 2]
    outs, (spread, tiles) = refs[part_count + 2 : -2], refs[-2:]
    rows, columns = number_ref.shape[0], up_ref.shape[1]
    width = min(256, columns)
    rank = LANES // 2
    full = parts[0][...].astype(jnp.float32)
    for p in parts[1:]:
        full = full + p[...].astype(jnp.float32)
    other = pltpu.roll(full, rank, 1)
    left = iota(full.shape, 1) < rank
    both = jnp.concatenate(
        [jnp.where(left, full, other), jnp.where(left, other, full)], axis=0
    )
    number = number_ref[...]
    own = (iota(number.shape, 1) // rank).astype(jnp.float32) + 1.0
    for i in range(spread.shape[1] // LANES):
        spread[:, i * LANES : (i + 1) * LANES] = jnp.where(
            number == own + 2.0 * i, both, 0.0
        ).astype(jnp.bfloat16)
    if columns // HD < HEAD_ROWS:
        tiles[...] = jnp.zeros_like(tiles)
    for i in range(columns // width):
        result = jnp.dot(
            spread[...],
            up_ref[:, i * width : (i + 1) * width],
            preferred_element_type=jnp.float32,
        )
        for j in range(width // HD):
            tiles[pl.ds(i * (width // HD) + j, rows, stride=HEAD_ROWS), :] = result[
                :, j * HD : (j + 1) * HD
            ]
    size = rows // host_count * HEAD_ROWS
    for k in range(host_count):
        outs[k][...] = tiles[k * size : (k + 1) * size].astype(jnp.bfloat16)


def expand(parts, number, up, host_count):
    rows = number.shape[0]
    depth, columns = up.shape
    spec = pl.BlockSpec(memory_space=pltpu.VMEM)
    block = jax.ShapeDtypeStruct((rows // host_count * HEAD_ROWS, HD), jnp.bfloat16)
    return pl.pallas_call(
        functools.partial(expand_kernel, len(parts), host_count),
        name="expand",
        out_shape=[block] * host_count,
        in_specs=[spec] * (len(parts) + 2),
        out_specs=[spec] * host_count,
        scratch_shapes=[
            pltpu.VMEM((rows, depth), jnp.bfloat16),
            pltpu.VMEM((rows * HEAD_ROWS, HD), jnp.float32),
        ],
        compiler_params=pltpu.CompilerParams(vmem_limit_bytes=12 * MIB),
        cost_estimate=pl.CostEstimate(
            flops=2 * rows * up.size, bytes_accessed=2 * up.size, transcendentals=0
        ),
    )(*parts, number, up)


def finish_kernel(base_count, back_count, place_ref, residual_ref, *refs):
    bases, backs = refs[:base_count], refs[base_count : base_count + back_count]
    more, (out_ref, tiles, sorted_tiles) = refs[base_count + back_count : -3], refs[-3:]
    row_count, columns = residual_ref.shape
    size = backs[0].shape[0]
    for k in range(back_count):
        tiles[k * size : (k + 1) * size] = backs[k][...].astype(jnp.float32)
    tiles[back_count * size :] = jnp.zeros((HEAD_ROWS, HD), jnp.float32)
    for r in range(row_count):
        where = pl.multiple_of(place_ref[r] * HEAD_ROWS, HEAD_ROWS)
        sorted_tiles[r * HEAD_ROWS : (r + 1) * HEAD_ROWS] = tiles[pl.ds(where, HEAD_ROWS), :]
    for j in range(columns // HD):
        cut = slice(j * HD, (j + 1) * HD)
        total = sorted_tiles[pl.ds(j, row_count, stride=HEAD_ROWS), :]
        for m in more:
            total = total + m[:, cut]
        total = residual_ref[:, cut].astype(jnp.float32) + ADAPTER_SCALE * total
        for b in bases:
            total = total + b[:row_count, cut].astype(jnp.float32)
        out_ref[:, cut] = total.astype(jnp.bfloat16)


def finish(place, residual, bases, backs, *more):
    spec = pl.BlockSpec(memory_space=pltpu.VMEM)
    size = backs[0].shape[0]
    return pl.pallas_call(
        functools.partial(finish_kernel, len(bases), len(backs)),
        name="finish",
        out_shape=pltpu.HBM(residual.shape, jnp.bfloat16),
        in_specs=[pl.BlockSpec(memory_space=pltpu.SMEM)]
        + [spec] * (1 + len(bases) + len(backs) + len(more)),
        out_specs=spec,
        scratch_shapes=[
            pltpu.VMEM((len(backs) * size + HEAD_ROWS, HD), jnp.float32),
            pltpu.VMEM((residual.shape[0] * HEAD_ROWS, HD), jnp.float32),
        ],
        compiler_params=pltpu.CompilerParams(vmem_limit_bytes=8 * MIB),
    )(place, residual, *bases, *backs, *more)


def swap(value, axis, k):
    size = lax.axis_size(axis)
    return lax.ppermute(value, axis, [(i, i ^ k) for i in range(size)])


def swap_all(values, axis):
    return [values[0]] + [swap(values[k], axis, k) for k in range(1, len(values))]


def second_pass(attended, down, up, stock, slots, room, rest):
    owned_total, rank, feature_here = down.shape
    host_count = lax.axis_size("hst")
    tp_count = lax.axis_size("tp")
    row_count = attended.shape[0]
    adapter = stock[slots]
    owner = adapter // owned_total
    order = jnp.arange(row_count)
    same = (owner[:, None] == owner[None, :]) & (order[None, :] < order[:, None])
    before = jnp.sum(same, axis=1)
    target = jnp.where(before >= room, owner * rest + before - room, -1)
    place = (target[:, None] == jnp.arange(host_count * rest)[None, :]).astype(jnp.float32)
    number = (adapter % owned_total + 1).astype(jnp.float32)
    numbers = jnp.broadcast_to((place.T @ number)[:, None], (host_count * rest, LANES))
    rows = jnp.dot(
        place.T.astype(jnp.bfloat16), attended, preferred_element_type=jnp.float32
    ).astype(jnp.bfloat16)
    rows = jnp.concatenate([rows, numbers.astype(jnp.bfloat16)], axis=1)
    rows = lax.all_to_all(rows, "hst", split_axis=0, concat_axis=0, tiled=True)
    number = rows[:, feature_here].astype(jnp.int32)
    rows = rows[:, :feature_here]
    uses = number[:, None] == jnp.arange(1, owned_total + 1)[None, :]
    product = jnp.einsum("rd,akd->rak", rows, down, preferred_element_type=jnp.float32)
    partial_sum = jnp.sum(jnp.where(uses[:, :, None], product, 0), axis=1)
    shrunk = sum([partial_sum] + [swap(partial_sum, "tp", k) for k in range(1, tp_count)])
    spread = jnp.where(uses[:, :, None], shrunk.astype(jnp.bfloat16)[:, None, :], 0)
    raised = jnp.einsum("rak,aki->ri", spread, up, preferred_element_type=jnp.float32)
    back = lax.all_to_all(
        raised.astype(jnp.bfloat16), "hst", split_axis=0, concat_axis=0, tiled=True
    )
    return jnp.dot(place.astype(jnp.bfloat16), back, preferred_element_type=jnp.float32)


def local(
    queries,
    key_page_cache,
    value_page_cache,
    request_pages,
    context_length,
    output_weight,
    adapter_down_weight,
    adapter_up_weight,
    residual,
    host_slot_adapter,
    request_slot,
):
    owned_total, rank, feature_here = adapter_down_weight.shape
    host_count = lax.axis_size("hst")
    tp_count = lax.axis_size("tp")
    slot_total = host_slot_adapter.shape[0]
    most = pair_rows(slot_total, host_count)
    room = min(FIRST, most)
    (attended, place, down), evens, odd, blocks = attend(
        queries,
        key_page_cache,
        value_page_cache,
        request_pages.T,
        context_length,
        request_slot.reshape(1, -1),
        host_slot_adapter.reshape(1, slot_total),
        adapter_down_weight.reshape(owned_total * rank, feature_here),
        output_weight,
        owned_total,
        host_count,
        room,
    )
    near = swap(odd, "tp", 1)
    row_count = attended.shape[0]
    bases = [evens[0], near]
    for k in range(2, tp_count, 2):
        pair = evens[k // 2] + near[k // 2 * row_count : (k // 2 + 1) * row_count]
        bases.append(swap(pair, "tp", k))
    blocks = swap_all(blocks, "hst")
    partial_sum, number, over, up = shrink(
        blocks, down, adapter_up_weight.reshape(owned_total * rank, -1), room
    )
    parts = swap_all([partial_sum] * tp_count, "tp")
    parts, bases = lax.optimization_barrier((parts, bases))
    raised = expand(parts, number, up, host_count)
    backs = swap_all(raised, "hst")
    if room == most:
        return finish(place, residual, bases, backs)

    def with_second(bases, backs):
        more = second_pass(
            attended,
            adapter_down_weight,
            adapter_up_weight,
            host_slot_adapter,
            request_slot[:, 0],
            room,
            up_to(most - room, 16),
        )
        return finish(place, residual, bases, backs, more)

    def first_only(bases, backs):
        return finish(place, residual, bases, backs)

    return lax.cond(over[0] > 0, with_second, first_only, bases, backs)


def solution(mesh):
    in_specs = (
        P("hst", "tp"),
        P("hst", None, "tp"),
        P("hst", None, "tp"),
        P("hst", None),
        P("hst"),
        P("tp", None),
        P("hst", None, "tp"),
        P("hst", None, "tp"),
        P("hst", "tp"),
        P("hst"),
        P("hst", None),
    )
    out_specs = P("hst", "tp")
    return jax.shard_map(local, mesh=mesh, in_specs=in_specs, out_specs=out_specs, check_vma=False)
```

time: 451 us -> 55.3 us (0.12)
  blocking collectives: 208 us -> 0 us
  waiting for transfers between devices: 136 us -> 10.3 us
  local copies, waits for them, and re-layouts: 54.6 us -> 0.02 us
  matrix products: 22.3 us -> 0 us
  starting transfers between devices: 5.21 us -> 27.4 us
  Pallas kernels: 0 us -> 16.6 us
  between operations: 14.2 us -> 0.76 us
  other arithmetic: 10.4 us -> 0.02 us
    all_to_all x1 -> x0, blocking collectives: 184 us -> none  [local(): lax.all_to_all(down_outgoing, 'hst', split_axis=0, concat_axis=0, tiled=T...]
    all_to_all x1 -> x0, waiting for transfers between devices: 136 us -> none  [local(): lax.all_to_all(up_outgoing, 'hst', split_axis=0, concat_axis=0, tiled=True)]
    gather x6 -> x0, local copies, waits for them, and re-layouts: 37.8 us -> none  [the longest x1 7.6 us: local(): adapter_down_weight[picked_adapters]]
    ppermute x0 -> x19, starting transfers between devices: none -> 27.4 us  [swap(): return lax.ppermute(value, axis, [(i, i ^ k) for i in range(size)])]
    dot_general x6 -> x0, matrix products: 17.6 us -> none  [the longest x1 5.78 us: local(): jnp.dot(attended, output_weight, preferred_element_type=jnp.float32)]
    pallas_call x0 -> x4, Pallas kernels: none -> 16.6 us  [the longest x1 10.2 us: attend(): pl.pallas_call(functools.partial(attention_kernel, owned_total, hosts, tp...]
    reshape x7 -> x0, local copies, waits for them, and re-layouts: 14.4 us -> none  [the longest x1 6.97 us: attend_rows(): key_rows = key_page_cache[request_pages].reshape(row_count, -1, kv_here, HD)]
    unnamed x1 -> x0, blocking collectives: 13.1 us -> none
  transfers between devices with their start and end apart: 2 -> 19, of which waited for: 1 -> 7; matrix products, arithmetic and copies ran while one was open for 13% -> 0% of each run, Pallas kernels for 0% -> 7%
where the time goes in v1:
time: 55.3 us; the launch traced here: 55.1 us
  starting transfers between devices  27.4 us (50%)
  Pallas kernels  16.6 us (30%)
  waiting for transfers between devices  10.3 us (19%)
  between operations  0.76 us (1%)
    ppermute x19, starting transfers between devices, swap(): return lax.ppermute(value, axis, [(i, i ^ k) for i in range(size)])  27.4 us
    ppermute x19, waiting for transfers between devices, swap(): return lax.ppermute(value, axis, [(i, i ^ k) for i in range(size)])  10.3 us
    pallas_call x1, Pallas kernels, attend(): pl.pallas_call(functools.partial(attention_kernel, owned_total, hosts, tp...  10.2 us
    pallas_call x1, Pallas kernels, shrink(): pl.pallas_call(functools.partial(shrink_kernel, host_count, room), name='...  3.95 us
    pallas_call x1, Pallas kernels, finish(): pl.pallas_call(functools.partial(finish_kernel, len(bases), len(backs)),...  1.4 us
  transfers between devices with their start and end apart: 19, of which 7 were waited for; matrix products, arithmetic and copies ran while one was open for 0% of the time, Pallas kernels for 7%

profile of v1, /device:TPU:0, one launch (start us, length us, event | category | flops | bytes accessed | tf_op | source)
XLA Modules:
  0.0 55.1 jit_solution(1546208876597292268)
XLA Ops:
  0.0 10.2 %attend.1 = (bf16[64,1024]{1,0:T(8,128)(2,1)S(1)}, s32[64]{0:T(128)S(1)}, bf16[2048,1024]{1,0:T(8,128)(2,1)S(1)}, bf16[64,1024]{1,0:T(8,128)(2,1)S(1)}, bf16[64,...) custom-call(s32[8,64]{1,0:T(8,128)} %bitcast.37, ...), custom_call_target="tpu_custom_call" | custom-call | flops 268435456 | bytes 20971520 | tf_op jit(solution)/shard_map/attend/pallas_call | solution.py:242
  10.2 0.5 collective-permute-start.13
  10.8 2.6 %collective-permute-start.3 = (bf16[168,128]{1,0:T(8,128)(2,1)S(1)}, bf16[168,128]{1,0:T(8,128)(2,1)S(1)}, u32[]{:S(2)}, u32[]{:S(2)}) collective-permute-start(bf16[168,128]{1,0:T(8,128)(2,1)S(1)} %get-tuple-element.135), channel_id=1, source_target_pairs={{0,4},{4,0},{8,12},{12,8},{16,20},{20,16},{24,28},{28,24},{1,5},{5... | collective-permute-start | bytes 129032 | tf_op jit(solution)/shard_map/ppermute | solution.py:465
  13.3 1.6 %collective-permute-start.4 = (bf16[168,128]{1,0:T(8,128)(2,1)S(1)}, bf16[168,128]{1,0:T(8,128)(2,1)S(1)}, u32[]{:S(2)}, u32[]{:S(2)}) collective-permute-start(bf16[168,128]{1,0:T(8,128)(2,1)S(1)} %get-tuple-element.136), channel_id=1, source_target_pairs={{0,8},{4,12},{8,0},{12,4},{16,24},{20,28},{24,16},{28,20},{1,9},{5... | collective-permute-start | bytes 129032 | tf_op jit(solution)/shard_map/ppermute | solution.py:465
  14.9 0.0 collective-permute-start.5
  14.9 0.0 collective-permute-done.13
  14.9 2.0 %collective-permute-start.14 = (bf16[64,1024]{1,0:T(8,128)(2,1)S(1)}, bf16[64,1024]{1,0:T(8,128)(2,1)S(1)}, u32[]{:S(2)}, u32[]{:S(2)}) collective-permute-start(bf16[64,1024]{1,0:T(8,128)(2,1)S(1)} %slice_add_fusion), channel_id=1, source_target_pairs={{0,2},{1,3},{2,0},{3,1},{4,6},{5,7},{6,4},{7,5},{8,10},{9,11},{10,... | collective-permute-start | bytes 393224 | tf_op jit(solution)/shard_map/ppermute | solution.py:465
  16.9 2.6 %collective-permute-start.6 = (bf16[168,128]{1,0:T(8,128)(2,1)S(1)}, bf16[168,128]{1,0:T(8,128)(2,1)S(1)}, u32[]{:S(2)}, u32[]{:S(2)}) collective-permute-start(bf16[168,128]{1,0:T(8,128)(2,1)S(1)} %get-tuple-element.138), channel_id=1, source_target_pairs={{0,16},{4,20},{8,24},{12,28},{16,0},{20,4},{24,8},{28,12},{1,17},{... | collective-permute-start | bytes 129032 | tf_op jit(solution)/shard_map/ppermute | solution.py:465
  19.5 0.0 collective-permute-done.3.refs_1_
  19.5 1.3 %collective-permute-start.7 = (bf16[168,128]{1,0:T(8,128)(2,1)S(1)}, bf16[168,128]{1,0:T(8,128)(2,1)S(1)}, u32[]{:S(2)}, u32[]{:S(2)}) collective-permute-start(bf16[168,128]{1,0:T(8,128)(2,1)S(1)} %get-tuple-element.139), channel_id=1, source_target_pairs={{0,20},{4,16},{8,28},{12,24},{16,4},{20,0},{24,12},{28,8},{1,21},{... | collective-permute-start | bytes 129032 | tf_op jit(solution)/shard_map/ppermute | solution.py:465
  20.8 0.0 collective-permute-done.4.refs_2_
  20.8 3.6 %collective-permute-start.8 = (bf16[168,128]{1,0:T(8,128)(2,1)S(1)}, bf16[168,128]{1,0:T(8,128)(2,1)S(1)}, u32[]{:S(2)}, u32[]{:S(2)}) collective-permute-start(bf16[168,128]{1,0:T(8,128)(2,1)S(1)} %get-tuple-element.140), channel_id=1, source_target_pairs={{0,24},{4,28},{8,16},{12,20},{16,8},{20,12},{24,0},{28,4},{1,25},{... | collective-permute-start | bytes 129032 | tf_op jit(solution)/shard_map/ppermute | solution.py:465
  24.4 0.0 collective-permute-done.5.refs_3_
  24.4 0.2 collective-permute-start.9
  24.6 0.0 collective-permute-done.6.refs_4_
  24.6 1.3 %collective-permute-done.7.refs_5_ = bf16[168,128]{1,0:T(8,128)(2,1)S(1)} collective-permute-done((bf16[168,128]{1,0:T(8,128)(2,1)S(1)}, bf16[168,128]{1,0:T(8,128)(2,1)S(1)}, u32[]{:S(2)}, u32[]{:S(2)}) %collective-permute-start.7) | collective-permute-done | bytes 43040 | tf_op jit(solution)/shard_map/ppermute | solution.py:465
  25.9 1.0 %collective-permute-done.8.refs_6_ = bf16[168,128]{1,0:T(8,128)(2,1)S(1)} collective-permute-done((bf16[168,128]{1,0:T(8,128)(2,1)S(1)}, bf16[168,128]{1,0:T(8,128)(2,1)S(1)}, u32[]{:S(2)}, u32[]{:S(2)}) %collective-permute-start.8) | collective-permute-done | bytes 43040 | tf_op jit(solution)/shard_map/ppermute | solution.py:465
  27.0 4.2 %collective-permute-done.9.refs_7_ = bf16[168,128]{1,0:T(8,128)(2,1)S(1)} collective-permute-done((bf16[168,128]{1,0:T(8,128)(2,1)S(1)}, bf16[168,128]{1,0:T(8,128)(2,1)S(1)}, u32[]{:S(2)}, u32[]{:S(2)}) %collective-permute-start.9) | collective-permute-done | bytes 43040 | tf_op jit(solution)/shard_map/ppermute | solution.py:465
  31.1 4.0 %shrink.1 = (bf16[80,128]{1,0:T(8,128)(2,1)S(1)}, f32[160,128]{1,0:T(8,128)S(1)}, s32[1]{0:T(128)}, bf16[2048,1024]{1,0:T(8,128)(2,1)S(1)}) custom-call(bf16[168,128]{1,0:T(8,128)(2,1)S(1)} %get-tuple-element.134.refs_0_, bf16[168,128]{1,0:T(8,128)(2,1)S(1)} %collective-permute-done.3.refs_1_, bf16[168,128]{1,0:T(8,128)(2,1)S(1)} %collective-permute-done.4.refs_2_, ...), custom_call_target="tpu_custom_call" | custom-call | flops 671088640 | bytes 4194304 | tf_op jit(solution)/shard_map/shrink/pallas_call | solution.py:341
  35.1 0.0 copy-start
  35.1 0.0 copy-start.2
  35.1 0.0 copy-start.3
  35.1 0.1 collective-permute-start.12
  35.2 0.6 %collective-permute-start.11 = (bf16[80,128]{1,0:T(8,128)(2,1)S(1)}, bf16[80,128]{1,0:T(8,128)(2,1)S(1)}, u32[]{:S(2)}, u32[]{:S(2)}) collective-permute-start(bf16[80,128]{1,0:T(8,128)(2,1)S(1)} %get-tuple-element.152.refs_0_), channel_id=1, source_target_pairs={{0,2},{1,3},{2,0},{3,1},{4,6},{5,7},{6,4},{7,5},{8,10},{9,11},{10,... | collective-permute-start | bytes 61448 | tf_op jit(solution)/shard_map/ppermute | solution.py:465
  35.8 1.3 %collective-permute-start.10 = (bf16[80,128]{1,0:T(8,128)(2,1)S(1)}, bf16[80,128]{1,0:T(8,128)(2,1)S(1)}, u32[]{:S(2)}, u32[]{:S(2)}) collective-permute-start(bf16[80,128]{1,0:T(8,128)(2,1)S(1)} %get-tuple-element.152.refs_0_), channel_id=1, source_target_pairs={{0,1},{1,0},{2,3},{3,2},{4,5},{5,4},{6,7},{7,6},{8,9},{9,8},{10,11... | collective-permute-start | bytes 61448 | tf_op jit(solution)/shard_map/ppermute | solution.py:465
  37.0 1.3 %collective-permute-done.12.refs_3_ = bf16[80,128]{1,0:T(8,128)(2,1)S(1)} collective-permute-done((bf16[80,128]{1,0:T(8,128)(2,1)S(1)}, bf16[80,128]{1,0:T(8,128)(2,1)S(1)}, u32[]{:S(2)}, u32[]{:S(2)}) %collective-permute-start.12) | collective-permute-done | bytes 20512 | tf_op jit(solution)/shard_map/ppermute | solution.py:465
  38.4 0.7 %collective-permute-done.11.refs_2_ = bf16[80,128]{1,0:T(8,128)(2,1)S(1)} collective-permute-done((bf16[80,128]{1,0:T(8,128)(2,1)S(1)}, bf16[80,128]{1,0:T(8,128)(2,1)S(1)}, u32[]{:S(2)}, u32[]{:S(2)}) %collective-permute-start.11) | collective-permute-done | bytes 20512 | tf_op jit(solution)/shard_map/ppermute | solution.py:465
  39.0 0.0 collective-permute-done.10.refs_1_
  39.0 0.0 collective-permute-done.14
  39.0 1.0 %expand.1 = (bf16[160,128]{1,0:T(8,128)(2,1)S(1)}, bf16[160,128]{1,0:T(8,128)(2,1)S(1)}, bf16[160,128]{1,0:T(8,128)(2,1)S(1)}, bf16[160,128]{1,0:T(8,128)(2,1)S(...) custom-call(bf16[80,128]{1,0:T(8,128)(2,1)S(1)} %get-tuple-element.1, ...), custom_call_target="tpu_custom_call" | custom-call | flops 671088640 | bytes 4194304 | tf_op jit(solution)/shard_map/expand/pallas_call | solution.py:406
  40.1 0.6 %collective-permute-start.15 = (bf16[160,128]{1,0:T(8,128)(2,1)S(1)}, bf16[160,128]{1,0:T(8,128)(2,1)S(1)}, u32[]{:S(2)}, u32[]{:S(2)}) collective-permute-start(bf16[160,128]{1,0:T(8,128)(2,1)S(1)} %get-tuple-element.159), channel_id=1, source_target_pairs={{0,4},{4,0},{8,12},{12,8},{16,20},{20,16},{24,28},{28,24},{1,5},{5... | collective-permute-start | bytes 122888 | tf_op jit(solution)/shard_map/ppermute | solution.py:465
  40.7 0.0 collective-permute-start.16
  40.7 2.9 %collective-permute-start.17 = (bf16[160,128]{1,0:T(8,128)(2,1)S(1)}, bf16[160,128]{1,0:T(8,128)(2,1)S(1)}, u32[]{:S(2)}, u32[]{:S(2)}) collective-permute-start(bf16[160,128]{1,0:T(8,128)(2,1)S(1)} %get-tuple-element.161), channel_id=1, source_target_pairs={{0,12},{4,8},{8,4},{12,0},{16,28},{20,24},{24,20},{28,16},{1,13},{... | collective-permute-start | bytes 122888 | tf_op jit(solution)/shard_map/ppermute | solution.py:465
  43.6 0.0 collective-permute-start.18
  43.6 2.9 %collective-permute-start.19 = (bf16[160,128]{1,0:T(8,128)(2,1)S(1)}, bf16[160,128]{1,0:T(8,128)(2,1)S(1)}, u32[]{:S(2)}, u32[]{:S(2)}) collective-permute-start(bf16[160,128]{1,0:T(8,128)(2,1)S(1)} %get-tuple-element.163), channel_id=1, source_target_pairs={{0,20},{4,16},{8,28},{12,24},{16,4},{20,0},{24,12},{28,8},{1,21},{... | collective-permute-start | bytes 122888 | tf_op jit(solution)/shard_map/ppermute | solution.py:465
  46.5 0.0 collective-permute-done.15
  46.5 0.5 collective-permute-start.20
  47.0 0.0 collective-permute-done.16
  47.0 4.3 %collective-permute-start.21 = (bf16[160,128]{1,0:T(8,128)(2,1)S(1)}, bf16[160,128]{1,0:T(8,128)(2,1)S(1)}, u32[]{:S(2)}, u32[]{:S(2)}) collective-permute-start(bf16[160,128]{1,0:T(8,128)(2,1)S(1)} %get-tuple-element.165), channel_id=1, source_target_pairs={{0,28},{4,24},{8,20},{12,16},{16,12},{20,8},{24,4},{28,0},{1,29},{... | collective-permute-start | bytes 122888 | tf_op jit(solution)/shard_map/ppermute | solution.py:465
  51.9 0.0 collective-permute-done.17
  52.0 0.0 collective-permute-done.18
  52.0 0.0 collective-permute-done.19
  52.0 0.4 collective-permute-done.20
  52.3 1.4 %collective-permute-done.21 = bf16[160,128]{1,0:T(8,128)(2,1)S(1)} collective-permute-done((bf16[160,128]{1,0:T(8,128)(2,1)S(1)}, bf16[160,128]{1,0:T(8,128)(2,1)S(1)}, u32[]{:S(2)}, u32[]{:S(2)}) %collective-permute-start.21) | collective-permute-done | bytes 40992 | tf_op jit(solution)/shard_map/ppermute | solution.py:465
  53.7 0.0 copy-done
  53.7 0.0 copy-done.3
  53.7 1.4 %conditional.1 = (bf16[64,1024]{1,0:T(8,128)(2,1)}) conditional(s32[]{:T(128)} %bitcast.14, (s32[64]{0:T(128)S(1)}, bf16[64,1024]{1,0:T(8,128)(2,1)S(1)}, bf16[64,1024]{1,0:T(8,128)(2,1)S(1)}, bf16[128,1024]{1,0:T(8,128)(2,1)S(1)}, bf16[64,1024]{1,0:T(8,128)(2,1)S(1)}, /*index=5*/bf16[160,128]{1,0:T(8,128)(2,1)S(1)}, bf16[160,128]{1,0:T(8,128)(2,1)S(1)}, ...), branch_computations={%region_0.0_spmd, %region_1.4_spmd} | conditional | flops 1109062016 | bytes 29252028 | solution.py:570
  53.7 1.4 %finish.2 = bf16[64,1024]{1,0:T(8,128)(2,1)} custom-call(s32[64]{0:T(128)S(1)} %get-tuple-element.70.place_ref, bf16[64,1024]{1,0:T(8,128)(2,1)S(1)} %get-tuple-element.71.residual_ref, bf16[64,1024]{1,0:T(8,128)(2,1)S(1)} %get-tuple-element.72.refs_0_, bf16[128,1024]{1,0:T(8,128)(2,1)S(1)} %get-tuple-element.73.refs_1_, ...), custom_call_target="tpu_custom_call" | custom-call | tf_op jit(solution)/shard_map/cond/branch_0_fun/finish/pallas_call | solution.py:448
  (2 shorter events, 0.0 us)
Async XLA Ops:
  10.2 4.7 %collective-permute-start.13 = (bf16[128,1024]{1,0:T(8,128)(2,1)S(1)}, bf16[128,1024]{1,0:T(8,128)(2,1)S(1)}, u32[]{:S(2)}, u32[]{:S(2)}) collective-permute-start(bf16[128,1024]{1,0:T(8,128)(2,1)S(1)} %get-tuple-element.147), channel_id=1, source_target_pairs={{0,1},{1,0},{2,3},{3,2},{4,5},{5,4},{6,7},{7,6},{8,9},{9,8},{10,11... | collective-permute-start | bytes 786440 | tf_op jit(solution)/shard_map/ppermute | solution.py:465
  10.8 8.8 %collective-permute-start.3 = (bf16[168,128]{1,0:T(8,128)(2,1)S(1)}, bf16[168,128]{1,0:T(8,128)(2,1)S(1)}, u32[]{:S(2)}, u32[]{:S(2)}) collective-permute-start(bf16[168,128]{1,0:T(8,128)(2,1)S(1)} %get-tuple-element.135), channel_id=1, source_target_pairs={{0,4},{4,0},{8,12},{12,8},{16,20},{20,16},{24,28},{28,24},{1,5},{5... | collective-permute-start | bytes 129032 | tf_op jit(solution)/shard_map/ppermute | solution.py:465
  13.3 7.5 %collective-permute-start.4 = (bf16[168,128]{1,0:T(8,128)(2,1)S(1)}, bf16[168,128]{1,0:T(8,128)(2,1)S(1)}, u32[]{:S(2)}, u32[]{:S(2)}) collective-permute-start(bf16[168,128]{1,0:T(8,128)(2,1)S(1)} %get-tuple-element.136), channel_id=1, source_target_pairs={{0,8},{4,12},{8,0},{12,4},{16,24},{20,28},{24,16},{28,20},{1,9},{5... | collective-permute-start | bytes 129032 | tf_op jit(solution)/shard_map/ppermute | solution.py:465
  14.9 9.5 %collective-permute-start.5 = (bf16[168,128]{1,0:T(8,128)(2,1)S(1)}, bf16[168,128]{1,0:T(8,128)(2,1)S(1)}, u32[]{:S(2)}, u32[]{:S(2)}) collective-permute-start(bf16[168,128]{1,0:T(8,128)(2,1)S(1)} %get-tuple-element.137), channel_id=1, source_target_pairs={{0,12},{4,8},{8,4},{12,0},{16,28},{20,24},{24,20},{28,16},{1,13},{... | collective-permute-start | bytes 129032 | tf_op jit(solution)/shard_map/ppermute | solution.py:465
  14.9 24.1 %collective-permute-start.14 = (bf16[64,1024]{1,0:T(8,128)(2,1)S(1)}, bf16[64,1024]{1,0:T(8,128)(2,1)S(1)}, u32[]{:S(2)}, u32[]{:S(2)}) collective-permute-start(bf16[64,1024]{1,0:T(8,128)(2,1)S(1)} %slice_add_fusion), channel_id=1, source_target_pairs={{0,2},{1,3},{2,0},{3,1},{4,6},{5,7},{6,4},{7,5},{8,10},{9,11},{10,... | collective-permute-start | bytes 393224 | tf_op jit(solution)/shard_map/ppermute | solution.py:465
  16.9 7.7 %collective-permute-start.6 = (bf16[168,128]{1,0:T(8,128)(2,1)S(1)}, bf16[168,128]{1,0:T(8,128)(2,1)S(1)}, u32[]{:S(2)}, u32[]{:S(2)}) collective-permute-start(bf16[168,128]{1,0:T(8,128)(2,1)S(1)} %get-tuple-element.138), channel_id=1, source_target_pairs={{0,16},{4,20},{8,24},{12,28},{16,0},{20,4},{24,8},{28,12},{1,17},{... | collective-permute-start | bytes 129032 | tf_op jit(solution)/shard_map/ppermute | solution.py:465
  19.5 6.4 %collective-permute-start.7 = (bf16[168,128]{1,0:T(8,128)(2,1)S(1)}, bf16[168,128]{1,0:T(8,128)(2,1)S(1)}, u32[]{:S(2)}, u32[]{:S(2)}) collective-permute-start(bf16[168,128]{1,0:T(8,128)(2,1)S(1)} %get-tuple-element.139), channel_id=1, source_target_pairs={{0,20},{4,16},{8,28},{12,24},{16,4},{20,0},{24,12},{28,8},{1,21},{... | collective-permute-start | bytes 129032 | tf_op jit(solution)/shard_map/ppermute | solution.py:465
  20.8 6.2 %collective-permute-start.8 = (bf16[168,128]{1,0:T(8,128)(2,1)S(1)}, bf16[168,128]{1,0:T(8,128)(2,1)S(1)}, u32[]{:S(2)}, u32[]{:S(2)}) collective-permute-start(bf16[168,128]{1,0:T(8,128)(2,1)S(1)} %get-tuple-element.140), channel_id=1, source_target_pairs={{0,24},{4,28},{8,16},{12,20},{16,8},{20,12},{24,0},{28,4},{1,25},{... | collective-permute-start | bytes 129032 | tf_op jit(solution)/shard_map/ppermute | solution.py:465
  24.4 6.7 %collective-permute-start.9 = (bf16[168,128]{1,0:T(8,128)(2,1)S(1)}, bf16[168,128]{1,0:T(8,128)(2,1)S(1)}, u32[]{:S(2)}, u32[]{:S(2)}) collective-permute-start(bf16[168,128]{1,0:T(8,128)(2,1)S(1)} %get-tuple-element.141), channel_id=1, source_target_pairs={{0,28},{4,24},{8,20},{12,16},{16,12},{20,8},{24,4},{28,0},{1,29},{... | collective-permute-start | bytes 129032 | tf_op jit(solution)/shard_map/ppermute | solution.py:465
  35.1 18.6 %copy-start = (s32[32]{0:T(128)S(1)}, s32[32]{0:T(128)}, u32[]{:S(2)}) copy-start(s32[32]{0:T(128)} %param.22) | copy-start | bytes 388
  35.1 18.6 %copy-start.2 = (bf16[64,1024]{1,0:T(8,128)(2,1)S(1)}, bf16[64,1024]{1,0:T(8,128)(2,1)}, u32[]{:S(2)}) copy-start(bf16[64,1024]{1,0:T(8,128)(2,1)} %param.21) | copy-start | bytes 393220
  35.1 18.6 %copy-start.3 = (s32[64,1]{0,1:T(1,128)S(1)}, s32[64,1]{0,1:T(1,128)}, u32[]{:S(2)}) copy-start(s32[64,1]{0,1:T(1,128)} %param.23) | copy-start | bytes 772
  35.1 3.3 %collective-permute-start.12 = (bf16[80,128]{1,0:T(8,128)(2,1)S(1)}, bf16[80,128]{1,0:T(8,128)(2,1)S(1)}, u32[]{:S(2)}, u32[]{:S(2)}) collective-permute-start(bf16[80,128]{1,0:T(8,128)(2,1)S(1)} %get-tuple-element.152.refs_0_), channel_id=1, source_target_pairs={{0,3},{1,2},{2,1},{3,0},{4,7},{5,6},{6,5},{7,4},{8,11},{9,10},{10,... | collective-permute-start | bytes 61448 | tf_op jit(solution)/shard_map/ppermute | solution.py:465
  35.2 3.8 %collective-permute-start.11 = (bf16[80,128]{1,0:T(8,128)(2,1)S(1)}, bf16[80,128]{1,0:T(8,128)(2,1)S(1)}, u32[]{:S(2)}, u32[]{:S(2)}) collective-permute-start(bf16[80,128]{1,0:T(8,128)(2,1)S(1)} %get-tuple-element.152.refs_0_), channel_id=1, source_target_pairs={{0,2},{1,3},{2,0},{3,1},{4,6},{5,7},{6,4},{7,5},{8,10},{9,11},{10,... | collective-permute-start | bytes 61448 | tf_op jit(solution)/shard_map/ppermute | solution.py:465
  35.8 3.3 %collective-permute-start.10 = (bf16[80,128]{1,0:T(8,128)(2,1)S(1)}, bf16[80,128]{1,0:T(8,128)(2,1)S(1)}, u32[]{:S(2)}, u32[]{:S(2)}) collective-permute-start(bf16[80,128]{1,0:T(8,128)(2,1)S(1)} %get-tuple-element.152.refs_0_), channel_id=1, source_target_pairs={{0,1},{1,0},{2,3},{3,2},{4,5},{5,4},{6,7},{7,6},{8,9},{9,8},{10,11... | collective-permute-start | bytes 61448 | tf_op jit(solution)/shard_map/ppermute | solution.py:465
  40.1 6.5 %collective-permute-start.15 = (bf16[160,128]{1,0:T(8,128)(2,1)S(1)}, bf16[160,128]{1,0:T(8,128)(2,1)S(1)}, u32[]{:S(2)}, u32[]{:S(2)}) collective-permute-start(bf16[160,128]{1,0:T(8,128)(2,1)S(1)} %get-tuple-element.159), channel_id=1, source_target_pairs={{0,4},{4,0},{8,12},{12,8},{16,20},{20,16},{24,28},{28,24},{1,5},{5... | collective-permute-start | bytes 122888 | tf_op jit(solution)/shard_map/ppermute | solution.py:465
  40.7 6.3 %collective-permute-start.16 = (bf16[160,128]{1,0:T(8,128)(2,1)S(1)}, bf16[160,128]{1,0:T(8,128)(2,1)S(1)}, u32[]{:S(2)}, u32[]{:S(2)}) collective-permute-start(bf16[160,128]{1,0:T(8,128)(2,1)S(1)} %get-tuple-element.160), channel_id=1, source_target_pairs={{0,8},{4,12},{8,0},{12,4},{16,24},{20,28},{24,16},{28,20},{1,9},{5... | collective-permute-start | bytes 122888 | tf_op jit(solution)/shard_map/ppermute | solution.py:465
  40.7 11.3 %collective-permute-start.17 = (bf16[160,128]{1,0:T(8,128)(2,1)S(1)}, bf16[160,128]{1,0:T(8,128)(2,1)S(1)}, u32[]{:S(2)}, u32[]{:S(2)}) collective-permute-start(bf16[160,128]{1,0:T(8,128)(2,1)S(1)} %get-tuple-element.161), channel_id=1, source_target_pairs={{0,12},{4,8},{8,4},{12,0},{16,28},{20,24},{24,20},{28,16},{1,13},{... | collective-permute-start | bytes 122888 | tf_op jit(solution)/shard_map/ppermute | solution.py:465
  43.6 8.3 %collective-permute-start.18 = (bf16[160,128]{1,0:T(8,128)(2,1)S(1)}, bf16[160,128]{1,0:T(8,128)(2,1)S(1)}, u32[]{:S(2)}, u32[]{:S(2)}) collective-permute-start(bf16[160,128]{1,0:T(8,128)(2,1)S(1)} %get-tuple-element.162), channel_id=1, source_target_pairs={{0,16},{4,20},{8,24},{12,28},{16,0},{20,4},{24,8},{28,12},{1,17},{... | collective-permute-start | bytes 122888 | tf_op jit(solution)/shard_map/ppermute | solution.py:465
  43.6 8.3 %collective-permute-start.19 = (bf16[160,128]{1,0:T(8,128)(2,1)S(1)}, bf16[160,128]{1,0:T(8,128)(2,1)S(1)}, u32[]{:S(2)}, u32[]{:S(2)}) collective-permute-start(bf16[160,128]{1,0:T(8,128)(2,1)S(1)} %get-tuple-element.163), channel_id=1, source_target_pairs={{0,20},{4,16},{8,28},{12,24},{16,4},{20,0},{24,12},{28,8},{1,21},{... | collective-permute-start | bytes 122888 | tf_op jit(solution)/shard_map/ppermute | solution.py:465
  46.5 5.8 %collective-permute-start.20 = (bf16[160,128]{1,0:T(8,128)(2,1)S(1)}, bf16[160,128]{1,0:T(8,128)(2,1)S(1)}, u32[]{:S(2)}, u32[]{:S(2)}) collective-permute-start(bf16[160,128]{1,0:T(8,128)(2,1)S(1)} %get-tuple-element.164), channel_id=1, source_target_pairs={{0,24},{4,28},{8,16},{12,20},{16,8},{20,12},{24,0},{28,4},{1,25},{... | collective-permute-start | bytes 122888 | tf_op jit(solution)/shard_map/ppermute | solution.py:465
  47.0 6.7 %collective-permute-start.21 = (bf16[160,128]{1,0:T(8,128)(2,1)S(1)}, bf16[160,128]{1,0:T(8,128)(2,1)S(1)}, u32[]{:S(2)}, u32[]{:S(2)}) collective-permute-start(bf16[160,128]{1,0:T(8,128)(2,1)S(1)} %get-tuple-element.165), channel_id=1, source_target_pairs={{0,28},{4,24},{8,20},{12,16},{16,12},{20,8},{24,4},{28,0},{1,29},{... | collective-permute-start | bytes 122888 | tf_op jit(solution)/shard_map/ppermute | solution.py:465

commit v2 on v1

--- a/solution.py
+++ b/solution.py
@@ -35,6 +35,14 @@
     return -(-value // step) * step
 
 
+def block_of(k, count):
+    return jnp.where(k == 0, 0, count - k)
+
+
+def partners(count):
+    return [0, *range(count - 1, 0, -1)]
+
+
 def copies(source, target, sem, count):
     cut = source.shape[0] // count
     return [
@@ -49,12 +57,10 @@
     return [pltpu.with_memory_space_constraint(a, pltpu.HBM) for a in arrays]
 
 
-def attention_kernel(owned_total, host_count, tp_count, room, *refs):
+def attention_kernel(owned_total, host_count, room, *refs):
     pages_hbm, length_hbm, query_hbm, slot_hbm, stock_hbm, keys_hbm, values_hbm = refs[:7]
-    down_hbm, output_hbm, attended_ref, place_ref, down_ref = refs[7:12]
-    evens = tp_count // 2
-    even_refs, odd_ref, refs = refs[12 : 12 + evens], refs[12 + evens], refs[13 + evens :]
-    block_refs, refs = refs[:host_count], refs[host_count:]
+    down_hbm, up_hbm, attended_ref, place_ref, down_ref, up_ref = refs[7:13]
+    block_refs, refs = refs[13 : 13 + host_count], refs[13 + host_count :]
     (
         pages_ref,
         length_ref,
@@ -63,7 +69,6 @@
         stock_ref,
         keys,
         values,
-        output,
         query_rows,
         outcome,
         packed,
@@ -72,8 +77,7 @@
         small_sem,
         key_sem,
         value_sem,
-        down_sem,
-        output_sem,
+        weight_sem,
     ) = refs
     row_count, feature_here = query_ref.shape
     page_total, page, kv_width = keys_hbm.shape
@@ -97,13 +101,9 @@
     ]
     key_moves = copies(keys_hbm, keys, key_sem, CHUNKS)
     value_moves = copies(values_hbm, values, value_sem, CHUNKS)
-    down_moves = copies(down_hbm, down_ref, down_sem, CHUNKS)
-    width = output_hbm.shape[1] // tp_count
-    output_moves = []
-    for k in range(tp_count):
-        columns = pl.ds(pl.multiple_of((lax.axis_index("tp") ^ k) * width, width), width)
-        output_moves.append(copies(output_hbm.at[:, columns], output.at[k], output_sem.at[k], 2))
-    for move in small_moves + key_moves:
+    weight_moves = copies(down_hbm, down_ref, weight_sem.at[0], CHUNKS)
+    weight_moves += copies(up_hbm, up_ref, weight_sem.at[1], CHUNKS)
+    for move in small_moves + key_moves + value_moves:
         move.start()
     packed[...] = jnp.zeros_like(packed)
     numbers[...] = jnp.zeros_like(numbers)
@@ -127,7 +127,7 @@
         owner = lax.div(adapter, owned_total)
         before = counts[owner]
         counts[owner] = before + 1
-        block = owner ^ me
+        block = block_of(owner ^ me, host_count)
         fits = before < room
         place_ref[r] = jnp.where(fits, block * room + before, host_count * room)
         where = jnp.where(fits, block * pad + before, host_count * pad)
@@ -138,12 +138,10 @@
     most = lax.fori_loop(0, row_count, count, jnp.int32(0))
     over = jnp.where(jnp.full((8, LANES), most, jnp.int32) >= room, 1.0, 0.0)
 
-    for move in key_moves[: CHUNKS // 2]:
+    for move in key_moves:
         move.wait()
-    for move in value_moves:
+    for move in weight_moves:
         move.start()
-    for move in key_moves[CHUNKS // 2 :]:
-        move.wait()
 
     head_of = iota((HEAD_ROWS, HD), 0) // share
 
@@ -189,16 +187,9 @@
         return carry
 
     lax.fori_loop(0, row_count // GROUP, some_scores, 0)
-    for move in value_moves[: CHUNKS // 2]:
-        move.wait()
-    for moves in output_moves:
-        for move in moves:
-            move.start()
-    for move in value_moves[CHUNKS // 2 :]:
+    for move in value_moves:
         move.wait()
     lax.fori_loop(0, row_count // GROUP, some_values, 0)
-    for move in down_moves:
-        move.start()
 
     lane = iota((8, LANES), 1)
     size = room * HEAD_ROWS
@@ -213,45 +204,30 @@
         attended_ref[:, j * HD : (j + 1) * HD] = outcome[
             pl.ds(j, row_count, stride=HEAD_ROWS), :
         ].astype(jnp.bfloat16)
-    rows = attended_ref[...]
-    for k in range(tp_count):
-        for move in output_moves[k]:
-            move.wait()
-        product = jnp.dot(rows, output[k], preferred_element_type=jnp.float32)
-        if k % 2 == 0:
-            even_refs[k // 2][...] = product.astype(jnp.bfloat16)
-        else:
-            first = k // 2 * row_count
-            odd_ref[first : first + row_count] = product.astype(jnp.bfloat16)
-    for move in down_moves:
+    for move in weight_moves:
         move.wait()
 
 
 def attend(
-    queries, keys, values, pages, lengths, slots, stock, down, output, owned_total, hosts, room
+    queries, keys, values, pages, lengths, slots, stock, down, up, owned_total, hosts, room
 ):
     row_count, feature_here = queries.shape
-    tp_count = output.shape[1] // feature_here
     spec = pl.BlockSpec(memory_space=pltpu.VMEM)
     small = pl.BlockSpec(memory_space=pltpu.SMEM)
     far = pl.BlockSpec(memory_space=pl.ANY)
-    evens = tp_count // 2
-    base = jax.ShapeDtypeStruct((row_count, feature_here), jnp.bfloat16)
-    odd = jax.ShapeDtypeStruct((evens * row_count, feature_here), jnp.bfloat16)
     block = jax.ShapeDtypeStruct((room * HEAD_ROWS + 8, LANES), jnp.bfloat16)
     outs = pl.pallas_call(
-        functools.partial(attention_kernel, owned_total, hosts, tp_count, room),
+        functools.partial(attention_kernel, owned_total, hosts, room),
         name="attend",
         out_shape=[
             jax.ShapeDtypeStruct((row_count, feature_here), jnp.bfloat16),
             jax.ShapeDtypeStruct((row_count,), jnp.int32),
             pltpu.VMEM(down.shape, jnp.bfloat16),
+            pltpu.VMEM(up.shape, jnp.bfloat16),
         ]
-        + [base] * evens
-        + [odd]
         + [block] * hosts,
         in_specs=[far] * 9,
-        out_specs=[spec, small, spec] + [spec] * (evens + 1 + hosts),
+        out_specs=[spec, small, spec, spec] + [spec] * hosts,
         scratch_shapes=[
             pltpu.SMEM(pages.shape, jnp.int32),
             pltpu.SMEM(lengths.shape, jnp.int32),
@@ -260,7 +236,6 @@
             pltpu.SMEM(stock.shape, jnp.int32),
             pltpu.VMEM(keys.shape, jnp.bfloat16),
             pltpu.VMEM(values.shape, jnp.bfloat16),
-            pltpu.VMEM((tp_count, feature_here, feature_here), jnp.bfloat16),
             pltpu.VMEM((row_count * HEAD_ROWS, HD), jnp.float32),
             pltpu.VMEM((row_count * HEAD_ROWS, HD), jnp.float32),
             pltpu.VMEM(((hosts * room + 1) * HEAD_ROWS, HD), jnp.float32),
@@ -269,26 +244,90 @@
             pltpu.SemaphoreType.DMA((5,)),
             pltpu.SemaphoreType.DMA((CHUNKS,)),
             pltpu.SemaphoreType.DMA((CHUNKS,)),
-            pltpu.SemaphoreType.DMA((CHUNKS,)),
-            pltpu.SemaphoreType.DMA((tp_count, 2)),
+            pltpu.SemaphoreType.DMA((2, CHUNKS)),
         ],
-        compiler_params=pltpu.CompilerParams(vmem_limit_bytes=32 * MIB),
+        compiler_params=pltpu.CompilerParams(vmem_limit_bytes=24 * MIB),
         cost_estimate=pl.CostEstimate(
             flops=4 * row_count * HEAD_ROWS * 128 * feature_here,
-            bytes_accessed=4 * keys.size + 2 * output.size + 2 * down.size,
+            bytes_accessed=4 * keys.size + 4 * down.size,
             transcendentals=row_count * HEAD_ROWS * 128,
         ),
-    )(*in_hbm(pages, lengths, queries, slots, stock, keys, values, down, output))
-    return outs[:3], outs[3 : 3 + evens], outs[3 + evens], outs[4 + evens :]
+    )(*in_hbm(pages, lengths, queries, slots, stock, keys, values, down, up))
+    return outs[:4], outs[4:]
+
+
+def base_moves(weight_hbm, weight, sem, parity):
+    count, parts = sem.shape
+    me = lax.axis_index("tp")
+    depth, width = weight.shape[1:]
+    cut = depth // parts
+    moves = []
+    for i in range(count):
+        columns = pl.ds(pl.multiple_of((me ^ (2 * i + parity)) * width, width), width)
+        for part in range(parts):
+            rows = pl.ds(part * cut, cut)
+            moves.append(
+                pltpu.make_async_copy(
+                    weight_hbm.at[rows, columns], weight.at[i, rows], sem.at[i, part]
+                )
+            )
+    return moves
+
+
+def odd_kernel(attended_ref, weight_hbm, out_ref, weight, sem):
+    moves = base_moves(weight_hbm, weight, sem, 1)
+    for move in moves:
+        move.start()
+    count, parts = sem.shape
+    rows = attended_ref[...]
+    for i in range(count):
+        for move in moves[i * parts : (i + 1) * parts]:
+            move.wait()
+        out_ref[i * rows.shape[0] : (i + 1) * rows.shape[0]] = jnp.dot(
+            rows, weight[i], preferred_element_type=jnp.float32
+        ).astype(jnp.bfloat16)
+
+
+def even_kernel(attended_ref, weight_hbm, *refs):
+    outs, (weight, sem) = refs[:-2], refs[-2:]
+    moves = base_moves(weight_hbm, weight, sem, 0)
+    for move in moves:
+        move.start()
+    count, parts = sem.shape
+    rows = attended_ref[...]
+    for i in range(count):
+        for move in moves[i * parts : (i + 1) * parts]:
+            move.wait()
+        outs[i][...] = jnp.dot(rows, weight[i], preferred_element_type=jnp.float32).astype(
+            jnp.bfloat16
+        )
+
+
+def base_half(kernel, name, attended, weight, out_shape):
+    row_count, depth = attended.shape
+    count = weight.shape[1] // depth // 2
+    spec = pl.BlockSpec(memory_space=pltpu.VMEM)
+    return pl.pallas_call(
+        kernel,
+        name=name,
+        out_shape=out_shape,
+        in_specs=[spec, pl.BlockSpec(memory_space=pl.ANY)],
+        out_specs=jax.tree.map(lambda _: spec, out_shape),
+        scratch_shapes=[
+            pltpu.VMEM((count, depth, depth), jnp.bfloat16),
+            pltpu.SemaphoreType.DMA((count, 8)),
+        ],
+        compiler_params=pltpu.CompilerParams(vmem_limit_bytes=12 * MIB),
+        cost_estimate=pl.CostEstimate(
+            flops=row_count * weight.size, bytes_accessed=weight.size, transcendentals=0
+        ),
+    )(attended, *in_hbm(weight))
 
 
 def shrink_kernel(host_count, room, *refs):
     blocks = refs[:host_count]
-    down_ref, up_hbm, partial_ref, number_ref, over_ref, up_ref = refs[host_count : host_count + 6]
-    tiles, total, up_sem = refs[host_count + 6 :]
-    up_moves = copies(up_hbm, up_ref, up_sem, CHUNKS)
-    for move in up_moves:
-        move.start()
+    down_ref, odd_ref, partial_ref, joint_ref, number_ref, over_ref = refs[host_count:-2]
+    tiles, total = refs[-2:]
     heads = down_ref.shape[1] // HD
     rows_all = host_count * room
     size = room * HEAD_ROWS
@@ -330,11 +369,14 @@
     half = rows_all // 2
     left = iota((half, LANES), 1) < rank
     partial_ref[...] = jnp.where(left, full[:half], full[half:]).astype(jnp.bfloat16)
-    for move in up_moves:
-        move.wait()
-
-
-def shrink(blocks, down, up, room):
+    joint_ref[:half] = partial_ref[...]
+    odd_rows = odd_ref.shape[0]
+    for j in range(odd_ref.shape[1] // LANES):
+        first = half + j * odd_rows
+        joint_ref[first : first + odd_rows] = odd_ref[:, j * LANES : (j + 1) * LANES]
+
+
+def shrink(blocks, down, odd, room):
     host_count = len(blocks)
     rows = host_count * room
     spec = pl.BlockSpec(memory_space=pltpu.VMEM)
@@ -343,33 +385,34 @@
         name="shrink",
         out_shape=(
             jax.ShapeDtypeStruct((rows // 2, LANES), jnp.bfloat16),
+            jax.ShapeDtypeStruct((rows // 2 + odd.size // LANES, LANES), jnp.bfloat16),
             jax.ShapeDtypeStruct((rows, LANES), jnp.float32),
             jax.ShapeDtypeStruct((1,), jnp.int32),
-            pltpu.VMEM(up.shape, jnp.bfloat16),
         ),
-        in_specs=[spec] * (host_count + 1) + [pl.BlockSpec(memory_space=pl.ANY)],
-        out_specs=(spec, spec, pl.BlockSpec(memory_space=pltpu.SMEM), spec),
+        in_specs=[spec] * (host_count + 2),
+        out_specs=(spec, spec, spec, pl.BlockSpec(memory_space=pltpu.SMEM)),
         scratch_shapes=[
             pltpu.VMEM((rows * HEAD_ROWS, HD), jnp.float32),
             pltpu.VMEM((rows, LANES), jnp.float32),
-            pltpu.SemaphoreType.DMA((CHUNKS,)),
         ],
         compiler_params=pltpu.CompilerParams(vmem_limit_bytes=12 * MIB),
         cost_estimate=pl.CostEstimate(
             flops=2 * rows * down.size, bytes_accessed=2 * down.size, transcendentals=0
         ),
-    )(*blocks, down, *in_hbm(up))
-
-
-def expand_kernel(part_count, host_count, *refs):
-    parts, (number_ref, up_ref) = refs[:part_count], refs[part_count : part_count + 2]
-    outs, (spread, tiles) = refs[part_count + 2 : -2], refs[-2:]
+    )(*blocks, down, odd)
+
+
+def expand_kernel(part_count, even_count, host_count, *refs):
+    parts, refs = refs[:part_count], refs[part_count:]
+    evens, (number_ref, up_ref), refs = refs[:even_count], refs[even_count:][:2], refs[even_count + 2 :]
+    outs, sums, (spread, tiles) = refs[:host_count], refs[host_count:-2], refs[-2:]
     rows, columns = number_ref.shape[0], up_ref.shape[1]
     width = min(256, columns)
     rank = LANES // 2
+    half = rows // 2
     full = parts[0][...].astype(jnp.float32)
     for p in parts[1:]:
-        full = full + p[...].astype(jnp.float32)
+        full = full + p[:half].astype(jnp.float32)
     other = pltpu.roll(full, rank, 1)
     left = iota(full.shape, 1) < rank
     both = jnp.concatenate(
@@ -396,19 +439,29 @@
     size = rows // host_count * HEAD_ROWS
     for k in range(host_count):
         outs[k][...] = tiles[k * size : (k + 1) * size].astype(jnp.bfloat16)
-
-
-def expand(parts, number, up, host_count):
+    row_count = evens[0].shape[0]
+    for i in range(even_count):
+        for j in range(columns // LANES):
+            first = half + (j * even_count + i) * row_count
+            cut = slice(j * LANES, (j + 1) * LANES)
+            sums[i][:, cut] = (
+                evens[i][:, cut].astype(jnp.float32)
+                + parts[1][first : first + row_count].astype(jnp.float32)
+            ).astype(jnp.bfloat16)
+
+
+def expand(parts, evens, number, up, host_count):
     rows = number.shape[0]
     depth, columns = up.shape
     spec = pl.BlockSpec(memory_space=pltpu.VMEM)
     block = jax.ShapeDtypeStruct((rows // host_count * HEAD_ROWS, HD), jnp.bfloat16)
-    return pl.pallas_call(
-        functools.partial(expand_kernel, len(parts), host_count),
+    outs = pl.pallas_call(
+        functools.partial(expand_kernel, len(parts), len(evens), host_count),
         name="expand",
-        out_shape=[block] * host_count,
-        in_specs=[spec] * (len(parts) + 2),
-        out_specs=[spec] * host_count,
+        out_shape=[block] * host_count
+        + [jax.ShapeDtypeStruct(e.shape, jnp.bfloat16) for e in evens],
+        in_specs=[spec] * (len(parts) + len(evens) + 2),
+        out_specs=[spec] * (host_count + len(evens)),
         scratch_shapes=[
             pltpu.VMEM((rows, depth), jnp.bfloat16),
             pltpu.VMEM((rows * HEAD_ROWS, HD), jnp.float32),
@@ -417,7 +470,8 @@
         cost_estimate=pl.CostEstimate(
             flops=2 * rows * up.size, bytes_accessed=2 * up.size, transcendentals=0
         ),
-    )(*parts, number, up)
+    )(*parts, *evens, number, up)
+    return outs[:host_count], outs[host_count:]
 
 
 def finish_kernel(base_count, back_count, place_ref, residual_ref, *refs):
@@ -438,7 +492,7 @@
             total = total + m[:, cut]
         total = residual_ref[:, cut].astype(jnp.float32) + ADAPTER_SCALE * total
         for b in bases:
-            total = total + b[:row_count, cut].astype(jnp.float32)
+            total = total + b[:, cut].astype(jnp.float32)
         out_ref[:, cut] = total.astype(jnp.bfloat16)
 
 
@@ -465,8 +519,8 @@
     return lax.ppermute(value, axis, [(i, i ^ k) for i in range(size)])
 
 
-def swap_all(values, axis):
-    return [values[0]] + [swap(values[k], axis, k) for k in range(1, len(values))]
+def swap_all(values, axis, ks):
+    return [v if k == 0 else swap(v, axis, k) for v, k in zip(values, ks)]
 
 
 def second_pass(attended, down, up, stock, slots, room, rest):
@@ -521,7 +575,7 @@
     slot_total = host_slot_adapter.shape[0]
     most = pair_rows(slot_total, host_count)
     room = min(FIRST, most)
-    (attended, place, down), evens, odd, blocks = attend(
+    (attended, place, down, up), blocks = attend(
         queries,
         key_page_cache,
         value_page_cache,
@@ -530,25 +584,29 @@
         request_slot.reshape(1, -1),
         host_slot_adapter.reshape(1, slot_total),
         adapter_down_weight.reshape(owned_total * rank, feature_here),
-        output_weight,
+        adapter_up_weight.reshape(owned_total * rank, -1),
         owned_total,
         host_count,
         room,
     )
-    near = swap(odd, "tp", 1)
     row_count = attended.shape[0]
-    bases = [evens[0], near]
-    for k in range(2, tp_count, 2):
-        pair = evens[k // 2] + near[k // 2 * row_count : (k // 2 + 1) * row_count]
-        bases.append(swap(pair, "tp", k))
-    blocks = swap_all(blocks, "hst")
-    partial_sum, number, over, up = shrink(
-        blocks, down, adapter_up_weight.reshape(owned_total * rank, -1), room
-    )
-    parts = swap_all([partial_sum] * tp_count, "tp")
-    parts, bases = lax.optimization_barrier((parts, bases))
-    raised = expand(parts, number, up, host_count)
-    backs = swap_all(raised, "hst")
+    ks = partners(host_count)
+    blocks = swap_all(blocks, "hst", ks)
+    evens = tp_count // 2
+    one = jax.ShapeDtypeStruct((row_count, feature_here), jnp.bfloat16)
+    odd = jax.ShapeDtypeStruct((evens * row_count, feature_here), jnp.bfloat16)
+    odd = base_half(odd_kernel, "base_odd", attended, output_weight, odd)
+    blocks, odd = lax.optimization_barrier((blocks, odd))
+    partial_sum, joint, number, over = shrink(blocks, down, odd, room)
+    parts = [partial_sum, joint] + [partial_sum] * (tp_count - 2)
+    parts = swap_all(parts, "tp", range(tp_count))
+    even = base_half(even_kernel, "base_even", attended, output_weight, [one] * evens)
+    parts, even = lax.optimization_barrier((parts, even))
+    raised, bases = expand(parts, even, number, up, host_count)
+    bases = swap_all(bases, "tp", range(0, tp_count, 2))
+    late = host_count // 2 + 1
+    last, bases = lax.optimization_barrier((raised[late:], bases))
+    backs = swap_all([*raised[:late], *last], "hst", ks)
     if room == most:
         return finish(place, residual, bases, backs)
 

time: 55.3 us -> 49 us (0.89)
  waiting for transfers between devices: 10.3 us -> 3.41 us
  Pallas kernels: 16.6 us -> 17.6 us
    ppermute x19 -> x18, waiting for transfers between devices: 10.3 us -> 3.41 us  [swap(): return lax.ppermute(value, axis, [(i, i ^ k) for i in range(size)])]
    pallas_call x2 -> x4, Pallas kernels: 11.3 us -> 14.1 us  [the longest x1 7.53 us: attend(): pl.pallas_call(functools.partial(attention_kernel, owned_total, hosts, ro...]
    pallas_call x1, Pallas kernels: 3.95 us -> 2.11 us  [shrink(): pl.pallas_call(functools.partial(shrink_kernel, host_count, room), name='...]
    ppermute x19 -> x18, starting transfers between devices: 27.4 us -> 27 us  [swap(): return lax.ppermute(value, axis, [(i, i ^ k) for i in range(size)])]
  transfers between devices with their start and end apart: 19 -> 18, of which waited for: 7 -> 5; matrix products, arithmetic and copies ran while one was open for 0% -> 0% of each run, Pallas kernels for 7% -> 11%
where the time goes in v2:
time: 49 us; the launch traced here: 48.9 us
  starting transfers between devices  27 us (55%)
  Pallas kernels  17.6 us (36%)
  waiting for transfers between devices  3.41 us (7%)
  between operations  0.8 us (2%)
    ppermute x18, starting transfers between devices, swap(): return lax.ppermute(value, axis, [(i, i ^ k) for i in range(size)])  27 us
    pallas_call x1, Pallas kernels, attend(): pl.pallas_call(functools.partial(attention_kernel, owned_total, hosts, ro...  7.53 us
    pallas_call x2, Pallas kernels, base_half(): pl.pallas_call(kernel, name=name, out_shape=out_shape, in_specs=[spec, pl...  5.54 us
    ppermute x18, waiting for transfers between devices, swap(): return lax.ppermute(value, axis, [(i, i ^ k) for i in range(size)])  3.41 us
    pallas_call x1, Pallas kernels, shrink(): pl.pallas_call(functools.partial(shrink_kernel, host_count, room), name='...  2.11 us
    pallas_call x1, Pallas kernels, finish(): pl.pallas_call(functools.partial(finish_kernel, len(bases), len(backs)),...  1.38 us
    pallas_call x1, Pallas kernels, expand(): pl.pallas_call(functools.partial(expand_kernel, len(parts), len(evens), h...  1.04 us
  transfers between devices with their start and end apart: 18, of which 5 were waited for; matrix products, arithmetic and copies ran while one was open for 0% of the time, Pallas kernels for 11%

profile of v2, /device:TPU:0, one launch (start us, length us, event | category | flops | bytes accessed | tf_op | source)
XLA Modules:
  0.0 48.9 jit_solution(12178668752831807715)
XLA Ops:
  0.0 7.5 %attend.1 = (bf16[64,1024]{1,0:T(8,128)(2,1)S(1)}, s32[64]{0:T(128)S(1)}, bf16[2048,1024]{1,0:T(8,128)(2,1)S(1)}, bf16[2048,1024]{1,0:T(8,128)(2,1)S(1)}, bf16[1...) custom-call(s32[8,64]{1,0:T(8,128)} %bitcast.37, ...), custom_call_target="tpu_custom_call" | custom-call | flops 268435456 | bytes 16777216 | tf_op jit(solution)/shard_map/attend/pallas_call | solution.py:219
  7.5 6.0 %collective-permute-start.3 = (bf16[168,128]{1,0:T(8,128)(2,1)S(1)}, bf16[168,128]{1,0:T(8,128)(2,1)S(1)}, u32[]{:S(2)}, u32[]{:S(2)}) collective-permute-start(bf16[168,128]{1,0:T(8,128)(2,1)S(1)} %get-tuple-element.144), channel_id=1, source_target_pairs={{0,28},{4,24},{8,20},{12,16},{16,12},{20,8},{24,4},{28,0},{1,29},{... | collective-permute-start | bytes 129032 | tf_op jit(solution)/shard_map/ppermute | solution.py:519
  13.6 0.2 collective-permute-start.4
  13.8 0.8 %collective-permute-start.5 = (bf16[168,128]{1,0:T(8,128)(2,1)S(1)}, bf16[168,128]{1,0:T(8,128)(2,1)S(1)}, u32[]{:S(2)}, u32[]{:S(2)}) collective-permute-start(bf16[168,128]{1,0:T(8,128)(2,1)S(1)} %get-tuple-element.146), channel_id=1, source_target_pairs={{0,20},{4,16},{8,28},{12,24},{16,4},{20,0},{24,12},{28,8},{1,21},{... | collective-permute-start | bytes 129032 | tf_op jit(solution)/shard_map/ppermute | solution.py:519
  14.6 2.0 %collective-permute-start.6 = (bf16[168,128]{1,0:T(8,128)(2,1)S(1)}, bf16[168,128]{1,0:T(8,128)(2,1)S(1)}, u32[]{:S(2)}, u32[]{:S(2)}) collective-permute-start(bf16[168,128]{1,0:T(8,128)(2,1)S(1)} %get-tuple-element.147), channel_id=1, source_target_pairs={{0,16},{4,20},{8,24},{12,28},{16,0},{20,4},{24,8},{28,12},{1,17},{... | collective-permute-start | bytes 129032 | tf_op jit(solution)/shard_map/ppermute | solution.py:519
  16.6 2.3 %collective-permute-start.7 = (bf16[168,128]{1,0:T(8,128)(2,1)S(1)}, bf16[168,128]{1,0:T(8,128)(2,1)S(1)}, u32[]{:S(2)}, u32[]{:S(2)}) collective-permute-start(bf16[168,128]{1,0:T(8,128)(2,1)S(1)} %get-tuple-element.148), channel_id=1, source_target_pairs={{0,12},{4,8},{8,4},{12,0},{16,28},{20,24},{24,20},{28,16},{1,13},{... | collective-permute-start | bytes 129032 | tf_op jit(solution)/shard_map/ppermute | solution.py:519
  18.9 0.0 collective-permute-done.3.refs_1_
  18.9 0.8 %collective-permute-start.8 = (bf16[168,128]{1,0:T(8,128)(2,1)S(1)}, bf16[168,128]{1,0:T(8,128)(2,1)S(1)}, u32[]{:S(2)}, u32[]{:S(2)}) collective-permute-start(bf16[168,128]{1,0:T(8,128)(2,1)S(1)} %get-tuple-element.149), channel_id=1, source_target_pairs={{0,8},{4,12},{8,0},{12,4},{16,24},{20,28},{24,16},{28,20},{1,9},{5... | collective-permute-start | bytes 129032 | tf_op jit(solution)/shard_map/ppermute | solution.py:519
  19.7 0.0 collective-permute-done.4.refs_2_
  19.7 0.4 collective-permute-start.9
  20.1 2.8 %base_odd.1.refs_9_ = bf16[128,1024]{1,0:T(8,128)(2,1)S(1)} custom-call(bf16[64,1024]{1,0:T(8,128)(2,1)S(1)} %get-tuple-element.151.attended_ref, bf16[1024,4096]{1,0:T(8,128)(2,1)} %weight_hbm.3), custom_call_target="tpu_custom_call" | custom-call | flops 268435456 | bytes 4194304 | tf_op jit(solution)/shard_map/base_odd/pallas_call | solution.py:310
  22.9 0.0 collective-permute-done.5.refs_3_
  22.9 0.0 collective-permute-done.6.refs_4_
  22.9 0.0 collective-permute-done.7.refs_5_
  22.9 0.0 collective-permute-done.8.refs_6_
  22.9 0.8 %collective-permute-done.9.refs_7_ = bf16[168,128]{1,0:T(8,128)(2,1)S(1)} collective-permute-done((bf16[168,128]{1,0:T(8,128)(2,1)S(1)}, bf16[168,128]{1,0:T(8,128)(2,1)S(1)}, u32[]{:S(2)}, u32[]{:S(2)}) %collective-permute-start.9) | collective-permute-done | bytes 43040 | tf_op jit(solution)/shard_map/ppermute | solution.py:519
  23.7 2.1 %shrink.1 = (bf16[80,128]{1,0:T(8,128)(2,1)S(1)}, bf16[1104,128]{1,0:T(8,128)(2,1)S(1)}, f32[160,128]{1,0:T(8,128)S(1)}, s32[1]{0:T(128)}) custom-call(bf16[168,128]{1,0:T(8,128)(2,1)S(1)} %get-tuple-element.152.refs_0_, bf16[168,128]{1,0:T(8,128)(2,1)S(1)} %collective-permute-done.3.refs_1_, bf16[168,128]{1,0:T(8,128)(2,1)S(1)} %collective-permute-done.4.refs_2_, ...), custom_call_target="tpu_custom_call" | custom-call | flops 671088640 | bytes 4194304 | tf_op jit(solution)/shard_map/shrink/pallas_call | solution.py:383
  25.8 0.1 collective-permute-start.10
  25.9 1.6 %collective-permute-start.12 = (bf16[80,128]{1,0:T(8,128)(2,1)S(1)}, bf16[80,128]{1,0:T(8,128)(2,1)S(1)}, u32[]{:S(2)}, u32[]{:S(2)}) collective-permute-start(bf16[80,128]{1,0:T(8,128)(2,1)S(1)} %get-tuple-element.168.refs_0_), channel_id=1, source_target_pairs={{0,3},{1,2},{2,1},{3,0},{4,7},{5,6},{6,5},{7,4},{8,11},{9,10},{10,... | collective-permute-start | bytes 61448 | tf_op jit(solution)/shard_map/ppermute | solution.py:519
  27.5 0.5 %collective-permute-start.11 = (bf16[80,128]{1,0:T(8,128)(2,1)S(1)}, bf16[80,128]{1,0:T(8,128)(2,1)S(1)}, u32[]{:S(2)}, u32[]{:S(2)}) collective-permute-start(bf16[80,128]{1,0:T(8,128)(2,1)S(1)} %get-tuple-element.168.refs_0_), channel_id=1, source_target_pairs={{0,2},{1,3},{2,0},{3,1},{4,6},{5,7},{6,4},{7,5},{8,10},{9,11},{10,... | collective-permute-start | bytes 61448 | tf_op jit(solution)/shard_map/ppermute | solution.py:519
  28.0 2.8 %base_even.1 = (bf16[64,1024]{1,0:T(8,128)(2,1)S(1)}, bf16[64,1024]{1,0:T(8,128)(2,1)S(1)}) custom-call(bf16[64,1024]{1,0:T(8,128)(2,1)S(1)} %get-tuple-element.151.attended_ref, bf16[1024,4096]{1,0:T(8,128)(2,1)} %weight_hbm.3), custom_call_target="tpu_custom_call" | custom-call | flops 268435456 | bytes 4194304 | tf_op jit(solution)/shard_map/base_even/pallas_call | solution.py:310
  30.8 0.0 copy-start
  30.8 0.0 copy-start.2
  30.8 0.0 copy-start.3
  30.8 0.0 collective-permute-done.12.refs_3_
  30.9 0.4 collective-permute-done.11.refs_2_
  31.3 0.0 collective-permute-done.10.refs_1_
  31.3 1.0 %expand.1 = (bf16[160,128]{1,0:T(8,128)(2,1)S(1)}, bf16[160,128]{1,0:T(8,128)(2,1)S(1)}, bf16[160,128]{1,0:T(8,128)(2,1)S(1)}, bf16[160,128]{1,0:T(8,128)(2,1)S(...) custom-call(bf16[80,128]{1,0:T(8,128)(2,1)S(1)} %get-tuple-element.1, ...), custom_call_target="tpu_custom_call" | custom-call | flops 671088640 | bytes 4194304 | tf_op jit(solution)/shard_map/expand/pallas_call | solution.py:458
  32.4 1.2 %collective-permute-start.13 = (bf16[64,1024]{1,0:T(8,128)(2,1)S(1)}, bf16[64,1024]{1,0:T(8,128)(2,1)S(1)}, u32[]{:S(2)}, u32[]{:S(2)}) collective-permute-start(bf16[64,1024]{1,0:T(8,128)(2,1)S(1)} %get-tuple-element.180), channel_id=1, source_target_pairs={{0,2},{1,3},{2,0},{3,1},{4,6},{5,7},{6,4},{7,5},{8,10},{9,11},{10,... | collective-permute-start | bytes 393224 | tf_op jit(solution)/shard_map/ppermute | solution.py:519
  33.5 3.9 %collective-permute-start.14 = (bf16[160,128]{1,0:T(8,128)(2,1)S(1)}, bf16[160,128]{1,0:T(8,128)(2,1)S(1)}, u32[]{:S(2)}, u32[]{:S(2)}) collective-permute-start(bf16[160,128]{1,0:T(8,128)(2,1)S(1)} %get-tuple-element.184), channel_id=1, source_target_pairs={{0,28},{4,24},{8,20},{12,16},{16,12},{20,8},{24,4},{28,0},{1,29},{... | collective-permute-start | bytes 122888 | tf_op jit(solution)/shard_map/ppermute | solution.py:519
  37.4 0.2 collective-permute-start.15
  37.6 1.0 %collective-permute-start.16 = (bf16[160,128]{1,0:T(8,128)(2,1)S(1)}, bf16[160,128]{1,0:T(8,128)(2,1)S(1)}, u32[]{:S(2)}, u32[]{:S(2)}) collective-permute-start(bf16[160,128]{1,0:T(8,128)(2,1)S(1)} %get-tuple-element.186), channel_id=1, source_target_pairs={{0,20},{4,16},{8,28},{12,24},{16,4},{20,0},{24,12},{28,8},{1,21},{... | collective-permute-start | bytes 122888 | tf_op jit(solution)/shard_map/ppermute | solution.py:519
  38.6 2.5 %collective-permute-start.17 = (bf16[160,128]{1,0:T(8,128)(2,1)S(1)}, bf16[160,128]{1,0:T(8,128)(2,1)S(1)}, u32[]{:S(2)}, u32[]{:S(2)}) collective-permute-start(bf16[160,128]{1,0:T(8,128)(2,1)S(1)} %get-tuple-element.187), channel_id=1, source_target_pairs={{0,16},{4,20},{8,24},{12,28},{16,0},{20,4},{24,8},{28,12},{1,17},{... | collective-permute-start | bytes 122888 | tf_op jit(solution)/shard_map/ppermute | solution.py:519
  41.2 0.0 collective-permute-done.13
  41.2 1.5 %collective-permute-start.18 = (bf16[160,128]{1,0:T(8,128)(2,1)S(1)}, bf16[160,128]{1,0:T(8,128)(2,1)S(1)}, u32[]{:S(2)}, u32[]{:S(2)}) collective-permute-start(bf16[160,128]{1,0:T(8,128)(2,1)S(1)} %get-tuple-element.188), channel_id=1, source_target_pairs={{0,12},{4,8},{8,4},{12,0},{16,28},{20,24},{24,20},{28,16},{1,13},{... | collective-permute-start | bytes 122888 | tf_op jit(solution)/shard_map/ppermute | solution.py:519
  42.7 0.0 collective-permute-done.14
  42.7 0.8 %collective-permute-start.19 = (bf16[160,128]{1,0:T(8,128)(2,1)S(1)}, bf16[160,128]{1,0:T(8,128)(2,1)S(1)}, u32[]{:S(2)}, u32[]{:S(2)}) collective-permute-start(bf16[160,128]{1,0:T(8,128)(2,1)S(1)} %get-tuple-element.189), channel_id=1, source_target_pairs={{0,8},{4,12},{8,0},{12,4},{16,24},{20,28},{24,16},{28,20},{1,9},{5... | collective-permute-start | bytes 122888 | tf_op jit(solution)/shard_map/ppermute | solution.py:519
  43.5 0.0 collective-permute-done.15
  43.5 1.2 %collective-permute-start.20 = (bf16[160,128]{1,0:T(8,128)(2,1)S(1)}, bf16[160,128]{1,0:T(8,128)(2,1)S(1)}, u32[]{:S(2)}, u32[]{:S(2)}) collective-permute-start(bf16[160,128]{1,0:T(8,128)(2,1)S(1)} %get-tuple-element.190), channel_id=1, source_target_pairs={{0,4},{4,0},{8,12},{12,8},{16,20},{20,16},{24,28},{28,24},{1,5},{5... | collective-permute-start | bytes 122888 | tf_op jit(solution)/shard_map/ppermute | solution.py:519
  45.3 0.0 collective-permute-done.16
  45.3 0.0 collective-permute-done.17
  45.3 0.7 %collective-permute-done.18 = bf16[160,128]{1,0:T(8,128)(2,1)S(1)} collective-permute-done((bf16[160,128]{1,0:T(8,128)(2,1)S(1)}, bf16[160,128]{1,0:T(8,128)(2,1)S(1)}, u32[]{:S(2)}, u32[]{:S(2)}) %collective-permute-start.18) | collective-permute-done | bytes 40992 | tf_op jit(solution)/shard_map/ppermute | solution.py:519
  46.1 0.6 %collective-permute-done.19 = bf16[160,128]{1,0:T(8,128)(2,1)S(1)} collective-permute-done((bf16[160,128]{1,0:T(8,128)(2,1)S(1)}, bf16[160,128]{1,0:T(8,128)(2,1)S(1)}, u32[]{:S(2)}, u32[]{:S(2)}) %collective-permute-start.19) | collective-permute-done | bytes 40992 | tf_op jit(solution)/shard_map/ppermute | solution.py:519
  46.7 0.8 %collective-permute-done.20 = bf16[160,128]{1,0:T(8,128)(2,1)S(1)} collective-permute-done((bf16[160,128]{1,0:T(8,128)(2,1)S(1)}, bf16[160,128]{1,0:T(8,128)(2,1)S(1)}, u32[]{:S(2)}, u32[]{:S(2)}) %collective-permute-start.20) | collective-permute-done | bytes 40992 | tf_op jit(solution)/shard_map/ppermute | solution.py:519
  47.5 0.0 copy-done
  47.5 0.0 copy-done.2
  47.5 1.4 %conditional.1 = (bf16[64,1024]{1,0:T(8,128)(2,1)}) conditional(s32[]{:T(128)} %bitcast.14, (s32[64]{0:T(128)S(1)}, bf16[64,1024]{1,0:T(8,128)(2,1)S(1)}, bf16[64,1024]{1,0:T(8,128)(2,1)S(1)}, bf16[64,1024]{1,0:T(8,128)(2,1)S(1)}, bf16[160,128]{1,0:T(8,128)(2,1)S(1)}, /*index=5*/bf16[160,128]{1,0:T(8,128)(2,1)S(1)}, bf16[160,128]{1,0:T(8,128)(2,1)S(1)}, ...), branch_computations={%region_0.0_spmd, %region_1.4_spmd} | conditional | flops 1109062016 | bytes 29252028 | solution.py:628
  47.5 1.4 %finish.2 = bf16[64,1024]{1,0:T(8,128)(2,1)} custom-call(s32[64]{0:T(128)S(1)} %get-tuple-element.66.place_ref, bf16[64,1024]{1,0:T(8,128)(2,1)S(1)} %get-tuple-element.67.residual_ref, bf16[64,1024]{1,0:T(8,128)(2,1)S(1)} %get-tuple-element.68.refs_0_, bf16[64,1024]{1,0:T(8,128)(2,1)S(1)} %get-tuple-element.69.refs_1_, ...), custom_call_target="tpu_custom_call" | custom-call | tf_op jit(solution)/shard_map/cond/branch_0_fun/finish/pallas_call | solution.py:502
  (1 shorter events, 0.0 us)
Async XLA Ops:
  7.5 11.3 %collective-permute-start.3 = (bf16[168,128]{1,0:T(8,128)(2,1)S(1)}, bf16[168,128]{1,0:T(8,128)(2,1)S(1)}, u32[]{:S(2)}, u32[]{:S(2)}) collective-permute-start(bf16[168,128]{1,0:T(8,128)(2,1)S(1)} %get-tuple-element.144), channel_id=1, source_target_pairs={{0,28},{4,24},{8,20},{12,16},{16,12},{20,8},{24,4},{28,0},{1,29},{... | collective-permute-start | bytes 129032 | tf_op jit(solution)/shard_map/ppermute | solution.py:519
  13.6 6.1 %collective-permute-start.4 = (bf16[168,128]{1,0:T(8,128)(2,1)S(1)}, bf16[168,128]{1,0:T(8,128)(2,1)S(1)}, u32[]{:S(2)}, u32[]{:S(2)}) collective-permute-start(bf16[168,128]{1,0:T(8,128)(2,1)S(1)} %get-tuple-element.145), channel_id=1, source_target_pairs={{0,24},{4,28},{8,16},{12,20},{16,8},{20,12},{24,0},{28,4},{1,25},{... | collective-permute-start | bytes 129032 | tf_op jit(solution)/shard_map/ppermute | solution.py:519
  13.8 9.1 %collective-permute-start.5 = (bf16[168,128]{1,0:T(8,128)(2,1)S(1)}, bf16[168,128]{1,0:T(8,128)(2,1)S(1)}, u32[]{:S(2)}, u32[]{:S(2)}) collective-permute-start(bf16[168,128]{1,0:T(8,128)(2,1)S(1)} %get-tuple-element.146), channel_id=1, source_target_pairs={{0,20},{4,16},{8,28},{12,24},{16,4},{20,0},{24,12},{28,8},{1,21},{... | collective-permute-start | bytes 129032 | tf_op jit(solution)/shard_map/ppermute | solution.py:519
  14.6 8.3 %collective-permute-start.6 = (bf16[168,128]{1,0:T(8,128)(2,1)S(1)}, bf16[168,128]{1,0:T(8,128)(2,1)S(1)}, u32[]{:S(2)}, u32[]{:S(2)}) collective-permute-start(bf16[168,128]{1,0:T(8,128)(2,1)S(1)} %get-tuple-element.147), channel_id=1, source_target_pairs={{0,16},{4,20},{8,24},{12,28},{16,0},{20,4},{24,8},{28,12},{1,17},{... | collective-permute-start | bytes 129032 | tf_op jit(solution)/shard_map/ppermute | solution.py:519
  16.6 6.3 %collective-permute-start.7 = (bf16[168,128]{1,0:T(8,128)(2,1)S(1)}, bf16[168,128]{1,0:T(8,128)(2,1)S(1)}, u32[]{:S(2)}, u32[]{:S(2)}) collective-permute-start(bf16[168,128]{1,0:T(8,128)(2,1)S(1)} %get-tuple-element.148), channel_id=1, source_target_pairs={{0,12},{4,8},{8,4},{12,0},{16,28},{20,24},{24,20},{28,16},{1,13},{... | collective-permute-start | bytes 129032 | tf_op jit(solution)/shard_map/ppermute | solution.py:519
  18.9 4.0 %collective-permute-start.8 = (bf16[168,128]{1,0:T(8,128)(2,1)S(1)}, bf16[168,128]{1,0:T(8,128)(2,1)S(1)}, u32[]{:S(2)}, u32[]{:S(2)}) collective-permute-start(bf16[168,128]{1,0:T(8,128)(2,1)S(1)} %get-tuple-element.149), channel_id=1, source_target_pairs={{0,8},{4,12},{8,0},{12,4},{16,24},{20,28},{24,16},{28,20},{1,9},{5... | collective-permute-start | bytes 129032 | tf_op jit(solution)/shard_map/ppermute | solution.py:519
  19.7 4.0 %collective-permute-start.9 = (bf16[168,128]{1,0:T(8,128)(2,1)S(1)}, bf16[168,128]{1,0:T(8,128)(2,1)S(1)}, u32[]{:S(2)}, u32[]{:S(2)}) collective-permute-start(bf16[168,128]{1,0:T(8,128)(2,1)S(1)} %get-tuple-element.150), channel_id=1, source_target_pairs={{0,4},{4,0},{8,12},{12,8},{16,20},{20,16},{24,28},{28,24},{1,5},{5... | collective-permute-start | bytes 129032 | tf_op jit(solution)/shard_map/ppermute | solution.py:519
  25.8 5.5 %collective-permute-start.10 = (bf16[1104,128]{1,0:T(8,128)(2,1)S(1)}, bf16[1104,128]{1,0:T(8,128)(2,1)S(1)}, u32[]{:S(2)}, u32[]{:S(2)}) collective-permute-start(bf16[1104,128]{1,0:T(8,128)(2,1)S(1)} %get-tuple-element.165), channel_id=1, source_target_pairs={{0,1},{1,0},{2,3},{3,2},{4,5},{5,4},{6,7},{7,6},{8,9},{9,8},{10,11... | collective-permute-start | bytes 847880 | tf_op jit(solution)/shard_map/ppermute | solution.py:519
  25.9 5.0 %collective-permute-start.12 = (bf16[80,128]{1,0:T(8,128)(2,1)S(1)}, bf16[80,128]{1,0:T(8,128)(2,1)S(1)}, u32[]{:S(2)}, u32[]{:S(2)}) collective-permute-start(bf16[80,128]{1,0:T(8,128)(2,1)S(1)} %get-tuple-element.168.refs_0_), channel_id=1, source_target_pairs={{0,3},{1,2},{2,1},{3,0},{4,7},{5,6},{6,5},{7,4},{8,11},{9,10},{10,... | collective-permute-start | bytes 61448 | tf_op jit(solution)/shard_map/ppermute | solution.py:519
  27.5 3.8 %collective-permute-start.11 = (bf16[80,128]{1,0:T(8,128)(2,1)S(1)}, bf16[80,128]{1,0:T(8,128)(2,1)S(1)}, u32[]{:S(2)}, u32[]{:S(2)}) collective-permute-start(bf16[80,128]{1,0:T(8,128)(2,1)S(1)} %get-tuple-element.168.refs_0_), channel_id=1, source_target_pairs={{0,2},{1,3},{2,0},{3,1},{4,6},{5,7},{6,4},{7,5},{8,10},{9,11},{10,... | collective-permute-start | bytes 61448 | tf_op jit(solution)/shard_map/ppermute | solution.py:519
  30.8 16.7 %copy-start = (s32[32]{0:T(128)S(1)}, s32[32]{0:T(128)}, u32[]{:S(2)}) copy-start(s32[32]{0:T(128)} %param.22) | copy-start | bytes 388
  30.8 16.7 %copy-start.2 = (bf16[64,1024]{1,0:T(8,128)(2,1)S(1)}, bf16[64,1024]{1,0:T(8,128)(2,1)}, u32[]{:S(2)}) copy-start(bf16[64,1024]{1,0:T(8,128)(2,1)} %param.21) | copy-start | bytes 393220
  30.8 16.7 %copy-start.3 = (s32[64,1]{0,1:T(1,128)S(1)}, s32[64,1]{0,1:T(1,128)}, u32[]{:S(2)}) copy-start(s32[64,1]{0,1:T(1,128)} %param.23) | copy-start | bytes 772
  32.4 8.8 %collective-permute-start.13 = (bf16[64,1024]{1,0:T(8,128)(2,1)S(1)}, bf16[64,1024]{1,0:T(8,128)(2,1)S(1)}, u32[]{:S(2)}, u32[]{:S(2)}) collective-permute-start(bf16[64,1024]{1,0:T(8,128)(2,1)S(1)} %get-tuple-element.180), channel_id=1, source_target_pairs={{0,2},{1,3},{2,0},{3,1},{4,6},{5,7},{6,4},{7,5},{8,10},{9,11},{10,... | collective-permute-start | bytes 393224 | tf_op jit(solution)/shard_map/ppermute | solution.py:519
  33.5 9.2 %collective-permute-start.14 = (bf16[160,128]{1,0:T(8,128)(2,1)S(1)}, bf16[160,128]{1,0:T(8,128)(2,1)S(1)}, u32[]{:S(2)}, u32[]{:S(2)}) collective-permute-start(bf16[160,128]{1,0:T(8,128)(2,1)S(1)} %get-tuple-element.184), channel_id=1, source_target_pairs={{0,28},{4,24},{8,20},{12,16},{16,12},{20,8},{24,4},{28,0},{1,29},{... | collective-permute-start | bytes 122888 | tf_op jit(solution)/shard_map/ppermute | solution.py:519
  37.4 6.1 %collective-permute-start.15 = (bf16[160,128]{1,0:T(8,128)(2,1)S(1)}, bf16[160,128]{1,0:T(8,128)(2,1)S(1)}, u32[]{:S(2)}, u32[]{:S(2)}) collective-permute-start(bf16[160,128]{1,0:T(8,128)(2,1)S(1)} %get-tuple-element.185), channel_id=1, source_target_pairs={{0,24},{4,28},{8,16},{12,20},{16,8},{20,12},{24,0},{28,4},{1,25},{... | collective-permute-start | bytes 122888 | tf_op jit(solution)/shard_map/ppermute | solution.py:519
  37.6 7.7 %collective-permute-start.16 = (bf16[160,128]{1,0:T(8,128)(2,1)S(1)}, bf16[160,128]{1,0:T(8,128)(2,1)S(1)}, u32[]{:S(2)}, u32[]{:S(2)}) collective-permute-start(bf16[160,128]{1,0:T(8,128)(2,1)S(1)} %get-tuple-element.186), channel_id=1, source_target_pairs={{0,20},{4,16},{8,28},{12,24},{16,4},{20,0},{24,12},{28,8},{1,21},{... | collective-permute-start | bytes 122888 | tf_op jit(solution)/shard_map/ppermute | solution.py:519
  38.6 6.7 %collective-permute-start.17 = (bf16[160,128]{1,0:T(8,128)(2,1)S(1)}, bf16[160,128]{1,0:T(8,128)(2,1)S(1)}, u32[]{:S(2)}, u32[]{:S(2)}) collective-permute-start(bf16[160,128]{1,0:T(8,128)(2,1)S(1)} %get-tuple-element.187), channel_id=1, source_target_pairs={{0,16},{4,20},{8,24},{12,28},{16,0},{20,4},{24,8},{28,12},{1,17},{... | collective-permute-start | bytes 122888 | tf_op jit(solution)/shard_map/ppermute | solution.py:519
  41.2 4.9 %collective-permute-start.18 = (bf16[160,128]{1,0:T(8,128)(2,1)S(1)}, bf16[160,128]{1,0:T(8,128)(2,1)S(1)}, u32[]{:S(2)}, u32[]{:S(2)}) collective-permute-start(bf16[160,128]{1,0:T(8,128)(2,1)S(1)} %get-tuple-element.188), channel_id=1, source_target_pairs={{0,12},{4,8},{8,4},{12,0},{16,28},{20,24},{24,20},{28,16},{1,13},{... | collective-permute-start | bytes 122888 | tf_op jit(solution)/shard_map/ppermute | solution.py:519
  42.7 4.0 %collective-permute-start.19 = (bf16[160,128]{1,0:T(8,128)(2,1)S(1)}, bf16[160,128]{1,0:T(8,128)(2,1)S(1)}, u32[]{:S(2)}, u32[]{:S(2)}) collective-permute-start(bf16[160,128]{1,0:T(8,128)(2,1)S(1)} %get-tuple-element.189), channel_id=1, source_target_pairs={{0,8},{4,12},{8,0},{12,4},{16,24},{20,28},{24,16},{28,20},{1,9},{5... | collective-permute-start | bytes 122888 | tf_op jit(solution)/shard_map/ppermute | solution.py:519
  43.5 4.0 %collective-permute-start.20 = (bf16[160,128]{1,0:T(8,128)(2,1)S(1)}, bf16[160,128]{1,0:T(8,128)(2,1)S(1)}, u32[]{:S(2)}, u32[]{:S(2)}) collective-permute-start(bf16[160,128]{1,0:T(8,128)(2,1)S(1)} %get-tuple-element.190), channel_id=1, source_target_pairs={{0,4},{4,0},{8,12},{12,8},{16,20},{20,16},{24,28},{28,24},{1,5},{5... | collective-permute-start | bytes 122888 | tf_op jit(solution)/shard_map/ppermute | solution.py:519

commit v3 on v2

--- a/solution.py
+++ b/solution.py
@@ -15,7 +15,7 @@
 ADAPTER_SCALE = 2.0
 CAP = 4
 FIRST = 20
-CHUNKS = 4
+CHUNKS = 8
 
 MIB = 1 << 20
 NT = (((1,), (1,)), ((), ()))
@@ -59,8 +59,8 @@
 
 def attention_kernel(owned_total, host_count, room, *refs):
     pages_hbm, length_hbm, query_hbm, slot_hbm, stock_hbm, keys_hbm, values_hbm = refs[:7]
-    down_hbm, up_hbm, attended_ref, place_ref, down_ref, up_ref = refs[7:13]
-    block_refs, refs = refs[13 : 13 + host_count], refs[13 + host_count :]
+    down_hbm, attended_ref, place_ref, down_ref = refs[7:11]
+    block_refs, refs = refs[11 : 11 + host_count], refs[11 + host_count :]
     (
         pages_ref,
         length_ref,
@@ -101,9 +101,8 @@
     ]
     key_moves = copies(keys_hbm, keys, key_sem, CHUNKS)
     value_moves = copies(values_hbm, values, value_sem, CHUNKS)
-    weight_moves = copies(down_hbm, down_ref, weight_sem.at[0], CHUNKS)
-    weight_moves += copies(up_hbm, up_ref, weight_sem.at[1], CHUNKS)
-    for move in small_moves + key_moves + value_moves:
+    weight_moves = copies(down_hbm, down_ref, weight_sem, CHUNKS)
+    for move in small_moves + key_moves:
         move.start()
     packed[...] = jnp.zeros_like(packed)
     numbers[...] = jnp.zeros_like(numbers)
@@ -111,6 +110,8 @@
         counts[o] = 0
     for move in small_moves:
         move.wait()
+    for move in value_moves:
+        move.start()
 
     if heads < HEAD_ROWS:
         query_rows[...] = jnp.zeros_like(query_rows)
@@ -209,7 +210,7 @@
 
 
 def attend(
-    queries, keys, values, pages, lengths, slots, stock, down, up, owned_total, hosts, room
+    queries, keys, values, pages, lengths, slots, stock, down, owned_total, hosts, room
 ):
     row_count, feature_here = queries.shape
     spec = pl.BlockSpec(memory_space=pltpu.VMEM)
@@ -223,11 +224,10 @@
             jax.ShapeDtypeStruct((row_count, feature_here), jnp.bfloat16),
             jax.ShapeDtypeStruct((row_count,), jnp.int32),
             pltpu.VMEM(down.shape, jnp.bfloat16),
-            pltpu.VMEM(up.shape, jnp.bfloat16),
         ]
         + [block] * hosts,
-        in_specs=[far] * 9,
-        out_specs=[spec, small, spec, spec] + [spec] * hosts,
+        in_specs=[far] * 8,
+        out_specs=[spec, small, spec] + [spec] * hosts,
         scratch_shapes=[
             pltpu.SMEM(pages.shape, jnp.int32),
             pltpu.SMEM(lengths.shape, jnp.int32),
@@ -244,16 +244,16 @@
             pltpu.SemaphoreType.DMA((5,)),
             pltpu.SemaphoreType.DMA((CHUNKS,)),
             pltpu.SemaphoreType.DMA((CHUNKS,)),
-            pltpu.SemaphoreType.DMA((2, CHUNKS)),
+            pltpu.SemaphoreType.DMA((CHUNKS,)),
         ],
         compiler_params=pltpu.CompilerParams(vmem_limit_bytes=24 * MIB),
         cost_estimate=pl.CostEstimate(
             flops=4 * row_count * HEAD_ROWS * 128 * feature_here,
-            bytes_accessed=4 * keys.size + 4 * down.size,
+            bytes_accessed=4 * keys.size + 2 * down.size,
             transcendentals=row_count * HEAD_ROWS * 128,
         ),
-    )(*in_hbm(pages, lengths, queries, slots, stock, keys, values, down, up))
-    return outs[:4], outs[4:]
+    )(*in_hbm(pages, lengths, queries, slots, stock, keys, values, down))
+    return outs[:3], outs[3:]
 
 
 def base_moves(weight_hbm, weight, sem, parity):
@@ -326,8 +326,11 @@
 
 def shrink_kernel(host_count, room, *refs):
     blocks = refs[:host_count]
-    down_ref, odd_ref, partial_ref, joint_ref, number_ref, over_ref = refs[host_count:-2]
-    tiles, total = refs[-2:]
+    down_ref, odd_ref, up_hbm, partial_ref, joint_ref, number_ref, over_ref = refs[host_count:-4]
+    up_ref, tiles, total, up_sem = refs[-4:]
+    up_moves = copies(up_hbm, up_ref, up_sem, up_sem.shape[0])
+    for move in up_moves:
+        move.start()
     heads = down_ref.shape[1] // HD
     rows_all = host_count * room
     size = room * HEAD_ROWS
@@ -374,9 +377,11 @@
     for j in range(odd_ref.shape[1] // LANES):
         first = half + j * odd_rows
         joint_ref[first : first + odd_rows] = odd_ref[:, j * LANES : (j + 1) * LANES]
-
-
-def shrink(blocks, down, odd, room):
+    for move in up_moves:
+        move.wait()
+
+
+def shrink(blocks, down, odd, up, room):
     host_count = len(blocks)
     rows = host_count * room
     spec = pl.BlockSpec(memory_space=pltpu.VMEM)
@@ -388,18 +393,20 @@
             jax.ShapeDtypeStruct((rows // 2 + odd.size // LANES, LANES), jnp.bfloat16),
             jax.ShapeDtypeStruct((rows, LANES), jnp.float32),
             jax.ShapeDtypeStruct((1,), jnp.int32),
+            pltpu.VMEM(up.shape, jnp.bfloat16),
         ),
-        in_specs=[spec] * (host_count + 2),
-        out_specs=(spec, spec, spec, pl.BlockSpec(memory_space=pltpu.SMEM)),
+        in_specs=[spec] * (host_count + 2) + [pl.BlockSpec(memory_space=pl.ANY)],
+        out_specs=(spec, spec, spec, pl.BlockSpec(memory_space=pltpu.SMEM), spec),
         scratch_shapes=[
             pltpu.VMEM((rows * HEAD_ROWS, HD), jnp.float32),
             pltpu.VMEM((rows, LANES), jnp.float32),
+            pltpu.SemaphoreType.DMA((16,)),
         ],
         compiler_params=pltpu.CompilerParams(vmem_limit_bytes=12 * MIB),
         cost_estimate=pl.CostEstimate(
             flops=2 * rows * down.size, bytes_accessed=2 * down.size, transcendentals=0
         ),
-    )(*blocks, down, odd)
+    )(*blocks, down, odd, *in_hbm(up))
 
 
 def expand_kernel(part_count, even_count, host_count, *refs):
@@ -476,7 +483,8 @@
 
 def finish_kernel(base_count, back_count, place_ref, residual_ref, *refs):
     bases, backs = refs[:base_count], refs[base_count : base_count + back_count]
-    more, (out_ref, tiles, sorted_tiles) = refs[base_count + back_count : -3], refs[-3:]
+    more, refs = refs[base_count + back_count : -5], refs[-5:]
+    out_hbm, tiles, sorted_tiles, out_ref, sem = refs
     row_count, columns = residual_ref.shape
     size = backs[0].shape[0]
     for k in range(back_count):
@@ -485,6 +493,7 @@
     for r in range(row_count):
         where = pl.multiple_of(place_ref[r] * HEAD_ROWS, HEAD_ROWS)
         sorted_tiles[r * HEAD_ROWS : (r + 1) * HEAD_ROWS] = tiles[pl.ds(where, HEAD_ROWS), :]
+    moves = []
     for j in range(columns // HD):
         cut = slice(j * HD, (j + 1) * HD)
         total = sorted_tiles[pl.ds(j, row_count, stride=HEAD_ROWS), :]
@@ -494,6 +503,14 @@
         for b in bases:
             total = total + b[:, cut].astype(jnp.float32)
         out_ref[:, cut] = total.astype(jnp.bfloat16)
+        if j % 2 == 1:
+            part = pl.ds((j - 1) * HD, 2 * HD)
+            moves.append(
+                pltpu.make_async_copy(out_ref.at[:, part], out_hbm.at[:, part], sem.at[j // 2])
+            )
+            moves[-1].start()
+    for move in moves:
+        move.wait()
 
 
 def finish(place, residual, bases, backs, *more):
@@ -505,10 +522,12 @@
         out_shape=pltpu.HBM(residual.shape, jnp.bfloat16),
         in_specs=[pl.BlockSpec(memory_space=pltpu.SMEM)]
         + [spec] * (1 + len(bases) + len(backs) + len(more)),
-        out_specs=spec,
+        out_specs=pl.BlockSpec(memory_space=pl.ANY),
         scratch_shapes=[
             pltpu.VMEM((len(backs) * size + HEAD_ROWS, HD), jnp.float32),
             pltpu.VMEM((residual.shape[0] * HEAD_ROWS, HD), jnp.float32),
+            pltpu.VMEM(residual.shape, jnp.bfloat16),
+            pltpu.SemaphoreType.DMA((residual.shape[1] // HD // 2,)),
         ],
         compiler_params=pltpu.CompilerParams(vmem_limit_bytes=8 * MIB),
     )(place, residual, *bases, *backs, *more)
@@ -575,7 +594,7 @@
     slot_total = host_slot_adapter.shape[0]
     most = pair_rows(slot_total, host_count)
     room = min(FIRST, most)
-    (attended, place, down, up), blocks = attend(
+    (attended, place, down), blocks = attend(
         queries,
         key_page_cache,
         value_page_cache,
@@ -584,7 +603,6 @@
         request_slot.reshape(1, -1),
         host_slot_adapter.reshape(1, slot_total),
         adapter_down_weight.reshape(owned_total * rank, feature_here),
-        adapter_up_weight.reshape(owned_total * rank, -1),
         owned_total,
         host_count,
         room,
@@ -597,7 +615,9 @@
     odd = jax.ShapeDtypeStruct((evens * row_count, feature_here), jnp.bfloat16)
     odd = base_half(odd_kernel, "base_odd", attended, output_weight, odd)
     blocks, odd = lax.optimization_barrier((blocks, odd))
-    partial_sum, joint, number, over = shrink(blocks, down, odd, room)
+    partial_sum, joint, number, over, up = shrink(
+        blocks, down, odd, adapter_up_weight.reshape(owned_total * rank, -1), room
+    )
     parts = [partial_sum, joint] + [partial_sum] * (tp_count - 2)
     parts = swap_all(parts, "tp", range(tp_count))
     even = base_half(even_kernel, "base_even", attended, output_weight, [one] * evens)

time: 49 us -> 50.9 us (1.039)
  Pallas kernels: 17.6 us -> 19.5 us
    pallas_call x1, Pallas kernels: 2.11 us -> 4.27 us  [shrink(): pl.pallas_call(functools.partial(shrink_kernel, host_count, room), name='...]
where the time goes in v3:
time: 50.9 us; the launch traced here: 50.8 us
  starting transfers between devices  27 us (53%)
  Pallas kernels  19.5 us (38%)
  waiting for transfers between devices  3.41 us (7%)
  between operations  0.8 us (2%)
    ppermute x18, starting transfers between devices, swap(): return lax.ppermute(value, axis, [(i, i ^ k) for i in range(size)])  27 us
    pallas_call x1, Pallas kernels, attend(): pl.pallas_call(functools.partial(attention_kernel, owned_total, hosts, ro...  7.25 us
    pallas_call x2, Pallas kernels, base_half(): pl.pallas_call(kernel, name=name, out_shape=out_shape, in_specs=[spec, pl...  5.54 us
    pallas_call x1, Pallas kernels, shrink(): pl.pallas_call(functools.partial(shrink_kernel, host_count, room), name='...  4.27 us
    ppermute x18, waiting for transfers between devices, swap(): return lax.ppermute(value, axis, [(i, i ^ k) for i in range(size)])  3.41 us
    pallas_call x1, Pallas kernels, finish(): pl.pallas_call(functools.partial(finish_kernel, len(bases), len(backs)),...  1.38 us
    pallas_call x1, Pallas kernels, expand(): pl.pallas_call(functools.partial(expand_kernel, len(parts), len(evens), h...  1.07 us
  transfers between devices with their start and end apart: 18, of which 5 were waited for; matrix products, arithmetic and copies ran while one was open for 0% of the time, Pallas kernels for 11%

profile of v3, /device:TPU:0, one launch (start us, length us, event | category | flops | bytes accessed | tf_op | source)
XLA Modules:
  0.0 50.8 jit_solution(16027934083211404203)
XLA Ops:
  0.0 7.2 %attend.1 = (bf16[64,1024]{1,0:T(8,128)(2,1)S(1)}, s32[64]{0:T(128)S(1)}, bf16[2048,1024]{1,0:T(8,128)(2,1)S(1)}, bf16[168,128]{1,0:T(8,128)(2,1)S(1)}, bf16[168...) custom-call(s32[8,64]{1,0:T(8,128)} %bitcast.37, ...), custom_call_target="tpu_custom_call" | custom-call | flops 268435456 | bytes 12582912 | tf_op jit(solution)/shard_map/attend/pallas_call | solution.py:220
  7.3 6.0 %collective-permute-start.3 = (bf16[168,128]{1,0:T(8,128)(2,1)S(1)}, bf16[168,128]{1,0:T(8,128)(2,1)S(1)}, u32[]{:S(2)}, u32[]{:S(2)}) collective-permute-start(bf16[168,128]{1,0:T(8,128)(2,1)S(1)} %get-tuple-element.144), channel_id=1, source_target_pairs={{0,28},{4,24},{8,20},{12,16},{16,12},{20,8},{24,4},{28,0},{1,29},{... | collective-permute-start | bytes 129032 | tf_op jit(solution)/shard_map/ppermute | solution.py:538
  13.3 0.2 collective-permute-start.4
  13.5 0.8 %collective-permute-start.5 = (bf16[168,128]{1,0:T(8,128)(2,1)S(1)}, bf16[168,128]{1,0:T(8,128)(2,1)S(1)}, u32[]{:S(2)}, u32[]{:S(2)}) collective-permute-start(bf16[168,128]{1,0:T(8,128)(2,1)S(1)} %get-tuple-element.146), channel_id=1, source_target_pairs={{0,20},{4,16},{8,28},{12,24},{16,4},{20,0},{24,12},{28,8},{1,21},{... | collective-permute-start | bytes 129032 | tf_op jit(solution)/shard_map/ppermute | solution.py:538
  14.3 2.0 %collective-permute-start.6 = (bf16[168,128]{1,0:T(8,128)(2,1)S(1)}, bf16[168,128]{1,0:T(8,128)(2,1)S(1)}, u32[]{:S(2)}, u32[]{:S(2)}) collective-permute-start(bf16[168,128]{1,0:T(8,128)(2,1)S(1)} %get-tuple-element.147), channel_id=1, source_target_pairs={{0,16},{4,20},{8,24},{12,28},{16,0},{20,4},{24,8},{28,12},{1,17},{... | collective-permute-start | bytes 129032 | tf_op jit(solution)/shard_map/ppermute | solution.py:538
  16.3 2.3 %collective-permute-start.7 = (bf16[168,128]{1,0:T(8,128)(2,1)S(1)}, bf16[168,128]{1,0:T(8,128)(2,1)S(1)}, u32[]{:S(2)}, u32[]{:S(2)}) collective-permute-start(bf16[168,128]{1,0:T(8,128)(2,1)S(1)} %get-tuple-element.148), channel_id=1, source_target_pairs={{0,12},{4,8},{8,4},{12,0},{16,28},{20,24},{24,20},{28,16},{1,13},{... | collective-permute-start | bytes 129032 | tf_op jit(solution)/shard_map/ppermute | solution.py:538
  18.6 0.0 collective-permute-done.3.refs_1_
  18.6 0.8 %collective-permute-start.8 = (bf16[168,128]{1,0:T(8,128)(2,1)S(1)}, bf16[168,128]{1,0:T(8,128)(2,1)S(1)}, u32[]{:S(2)}, u32[]{:S(2)}) collective-permute-start(bf16[168,128]{1,0:T(8,128)(2,1)S(1)} %get-tuple-element.149), channel_id=1, source_target_pairs={{0,8},{4,12},{8,0},{12,4},{16,24},{20,28},{24,16},{28,20},{1,9},{5... | collective-permute-start | bytes 129032 | tf_op jit(solution)/shard_map/ppermute | solution.py:538
  19.4 0.0 collective-permute-done.4.refs_2_
  19.4 0.4 collective-permute-start.9
  19.8 2.8 %base_odd.1.refs_9_ = bf16[128,1024]{1,0:T(8,128)(2,1)S(1)} custom-call(bf16[64,1024]{1,0:T(8,128)(2,1)S(1)} %get-tuple-element.151.attended_ref, bf16[1024,4096]{1,0:T(8,128)(2,1)} %weight_hbm.3), custom_call_target="tpu_custom_call" | custom-call | flops 268435456 | bytes 4194304 | tf_op jit(solution)/shard_map/base_odd/pallas_call | solution.py:310
  22.6 0.0 collective-permute-done.5.refs_3_
  22.6 0.0 collective-permute-done.6.refs_4_
  22.6 0.0 collective-permute-done.7.refs_5_
  22.6 0.0 collective-permute-done.8.refs_6_
  22.6 0.8 %collective-permute-done.9.refs_7_ = bf16[168,128]{1,0:T(8,128)(2,1)S(1)} collective-permute-done((bf16[168,128]{1,0:T(8,128)(2,1)S(1)}, bf16[168,128]{1,0:T(8,128)(2,1)S(1)}, u32[]{:S(2)}, u32[]{:S(2)}) %collective-permute-start.9) | collective-permute-done | bytes 43040 | tf_op jit(solution)/shard_map/ppermute | solution.py:538
  23.4 4.3 %shrink.1 = (bf16[80,128]{1,0:T(8,128)(2,1)S(1)}, bf16[1104,128]{1,0:T(8,128)(2,1)S(1)}, f32[160,128]{1,0:T(8,128)S(1)}, s32[1]{0:T(128)}, bf16[2048,1024]{1,0:T(8,128)(2,1)S(1)}) custom-call(bf16[168,128]{1,0:T(8,128)(2,1)S(1)} %get-tuple-element.152.refs_0_, bf16[168,128]{1,0:T(8,128)(2,1)S(1)} %collective-permute-done.3.refs_1_, ...), custom_call_target="tpu_custom_call" | custom-call | flops 671088640 | bytes 4194304 | tf_op jit(solution)/shard_map/shrink/pallas_call | solution.py:388
  27.7 0.1 collective-permute-start.10
  27.8 1.6 %collective-permute-start.12 = (bf16[80,128]{1,0:T(8,128)(2,1)S(1)}, bf16[80,128]{1,0:T(8,128)(2,1)S(1)}, u32[]{:S(2)}, u32[]{:S(2)}) collective-permute-start(bf16[80,128]{1,0:T(8,128)(2,1)S(1)} %get-tuple-element.168.refs_0_), channel_id=1, source_target_pairs={{0,3},{1,2},{2,1},{3,0},{4,7},{5,6},{6,5},{7,4},{8,11},{9,10},{10,... | collective-permute-start | bytes 61448 | tf_op jit(solution)/shard_map/ppermute | solution.py:538
  29.4 0.5 collective-permute-start.11
  29.9 2.8 %base_even.1 = (bf16[64,1024]{1,0:T(8,128)(2,1)S(1)}, bf16[64,1024]{1,0:T(8,128)(2,1)S(1)}) custom-call(bf16[64,1024]{1,0:T(8,128)(2,1)S(1)} %get-tuple-element.151.attended_ref, bf16[1024,4096]{1,0:T(8,128)(2,1)} %weight_hbm.3), custom_call_target="tpu_custom_call" | custom-call | flops 268435456 | bytes 4194304 | tf_op jit(solution)/shard_map/base_even/pallas_call | solution.py:310
  32.7 0.0 copy-start
  32.7 0.0 copy-start.2
  32.7 0.0 copy-start.3
  32.7 0.0 collective-permute-done.12.refs_3_
  32.7 0.4 collective-permute-done.11.refs_2_
  33.2 0.0 collective-permute-done.10.refs_1_
  33.2 1.1 %expand.1 = (bf16[160,128]{1,0:T(8,128)(2,1)S(1)}, bf16[160,128]{1,0:T(8,128)(2,1)S(1)}, bf16[160,128]{1,0:T(8,128)(2,1)S(1)}, bf16[160,128]{1,0:T(8,128)(2,1)S(...) custom-call(bf16[80,128]{1,0:T(8,128)(2,1)S(1)} %get-tuple-element.1, ...), custom_call_target="tpu_custom_call" | custom-call | flops 671088640 | bytes 4194304 | tf_op jit(solution)/shard_map/expand/pallas_call | solution.py:465
  34.3 1.2 %collective-permute-start.13 = (bf16[64,1024]{1,0:T(8,128)(2,1)S(1)}, bf16[64,1024]{1,0:T(8,128)(2,1)S(1)}, u32[]{:S(2)}, u32[]{:S(2)}) collective-permute-start(bf16[64,1024]{1,0:T(8,128)(2,1)S(1)} %get-tuple-element.180), channel_id=1, source_target_pairs={{0,2},{1,3},{2,0},{3,1},{4,6},{5,7},{6,4},{7,5},{8,10},{9,11},{10,... | collective-permute-start | bytes 393224 | tf_op jit(solution)/shard_map/ppermute | solution.py:538
  35.4 3.9 %collective-permute-start.14 = (bf16[160,128]{1,0:T(8,128)(2,1)S(1)}, bf16[160,128]{1,0:T(8,128)(2,1)S(1)}, u32[]{:S(2)}, u32[]{:S(2)}) collective-permute-start(bf16[160,128]{1,0:T(8,128)(2,1)S(1)} %get-tuple-element.184), channel_id=1, source_target_pairs={{0,28},{4,24},{8,20},{12,16},{16,12},{20,8},{24,4},{28,0},{1,29},{... | collective-permute-start | bytes 122888 | tf_op jit(solution)/shard_map/ppermute | solution.py:538
  39.3 0.2 collective-permute-start.15
  39.5 1.0 %collective-permute-start.16 = (bf16[160,128]{1,0:T(8,128)(2,1)S(1)}, bf16[160,128]{1,0:T(8,128)(2,1)S(1)}, u32[]{:S(2)}, u32[]{:S(2)}) collective-permute-start(bf16[160,128]{1,0:T(8,128)(2,1)S(1)} %get-tuple-element.186), channel_id=1, source_target_pairs={{0,20},{4,16},{8,28},{12,24},{16,4},{20,0},{24,12},{28,8},{1,21},{... | collective-permute-start | bytes 122888 | tf_op jit(solution)/shard_map/ppermute | solution.py:538
  40.5 2.5 %collective-permute-start.17 = (bf16[160,128]{1,0:T(8,128)(2,1)S(1)}, bf16[160,128]{1,0:T(8,128)(2,1)S(1)}, u32[]{:S(2)}, u32[]{:S(2)}) collective-permute-start(bf16[160,128]{1,0:T(8,128)(2,1)S(1)} %get-tuple-element.187), channel_id=1, source_target_pairs={{0,16},{4,20},{8,24},{12,28},{16,0},{20,4},{24,8},{28,12},{1,17},{... | collective-permute-start | bytes 122888 | tf_op jit(solution)/shard_map/ppermute | solution.py:538
  43.1 0.0 collective-permute-done.13
  43.1 1.5 %collective-permute-start.18 = (bf16[160,128]{1,0:T(8,128)(2,1)S(1)}, bf16[160,128]{1,0:T(8,128)(2,1)S(1)}, u32[]{:S(2)}, u32[]{:S(2)}) collective-permute-start(bf16[160,128]{1,0:T(8,128)(2,1)S(1)} %get-tuple-element.188), channel_id=1, source_target_pairs={{0,12},{4,8},{8,4},{12,0},{16,28},{20,24},{24,20},{28,16},{1,13},{... | collective-permute-start | bytes 122888 | tf_op jit(solution)/shard_map/ppermute | solution.py:538
  44.6 0.0 collective-permute-done.14
  44.6 0.8 %collective-permute-start.19 = (bf16[160,128]{1,0:T(8,128)(2,1)S(1)}, bf16[160,128]{1,0:T(8,128)(2,1)S(1)}, u32[]{:S(2)}, u32[]{:S(2)}) collective-permute-start(bf16[160,128]{1,0:T(8,128)(2,1)S(1)} %get-tuple-element.189), channel_id=1, source_target_pairs={{0,8},{4,12},{8,0},{12,4},{16,24},{20,28},{24,16},{28,20},{1,9},{5... | collective-permute-start | bytes 122888 | tf_op jit(solution)/shard_map/ppermute | solution.py:538
  45.4 0.0 collective-permute-done.15
  45.4 1.2 %collective-permute-start.20 = (bf16[160,128]{1,0:T(8,128)(2,1)S(1)}, bf16[160,128]{1,0:T(8,128)(2,1)S(1)}, u32[]{:S(2)}, u32[]{:S(2)}) collective-permute-start(bf16[160,128]{1,0:T(8,128)(2,1)S(1)} %get-tuple-element.190), channel_id=1, source_target_pairs={{0,4},{4,0},{8,12},{12,8},{16,20},{20,16},{24,28},{28,24},{1,5},{5... | collective-permute-start | bytes 122888 | tf_op jit(solution)/shard_map/ppermute | solution.py:538
  47.2 0.0 collective-permute-done.16
  47.2 0.0 collective-permute-done.17
  47.2 0.7 %collective-permute-done.18 = bf16[160,128]{1,0:T(8,128)(2,1)S(1)} collective-permute-done((bf16[160,128]{1,0:T(8,128)(2,1)S(1)}, bf16[160,128]{1,0:T(8,128)(2,1)S(1)}, u32[]{:S(2)}, u32[]{:S(2)}) %collective-permute-start.18) | collective-permute-done | bytes 40992 | tf_op jit(solution)/shard_map/ppermute | solution.py:538
  48.0 0.6 %collective-permute-done.19 = bf16[160,128]{1,0:T(8,128)(2,1)S(1)} collective-permute-done((bf16[160,128]{1,0:T(8,128)(2,1)S(1)}, bf16[160,128]{1,0:T(8,128)(2,1)S(1)}, u32[]{:S(2)}, u32[]{:S(2)}) %collective-permute-start.19) | collective-permute-done | bytes 40992 | tf_op jit(solution)/shard_map/ppermute | solution.py:538
  48.6 0.8 %collective-permute-done.20 = bf16[160,128]{1,0:T(8,128)(2,1)S(1)} collective-permute-done((bf16[160,128]{1,0:T(8,128)(2,1)S(1)}, bf16[160,128]{1,0:T(8,128)(2,1)S(1)}, u32[]{:S(2)}, u32[]{:S(2)}) %collective-permute-start.20) | collective-permute-done | bytes 40992 | tf_op jit(solution)/shard_map/ppermute | solution.py:538
  49.4 0.0 copy-done
  49.4 0.0 copy-done.2
  49.4 1.4 %conditional.1 = (bf16[64,1024]{1,0:T(8,128)(2,1)}) conditional(s32[]{:T(128)} %bitcast.14, (s32[64]{0:T(128)S(1)}, bf16[64,1024]{1,0:T(8,128)(2,1)S(1)}, bf16[64,1024]{1,0:T(8,128)(2,1)S(1)}, bf16[64,1024]{1,0:T(8,128)(2,1)S(1)}, bf16[160,128]{1,0:T(8,128)(2,1)S(1)}, /*index=5*/bf16[160,128]{1,0:T(8,128)(2,1)S(1)}, bf16[160,128]{1,0:T(8,128)(2,1)S(1)}, ...), branch_computations={%region_0.0_spmd, %region_1.4_spmd} | conditional | flops 1109062016 | bytes 29252028 | solution.py:648
  49.4 1.4 %finish.2 = bf16[64,1024]{1,0:T(8,128)(2,1)} custom-call(s32[64]{0:T(128)S(1)} %get-tuple-element.66.place_ref, bf16[64,1024]{1,0:T(8,128)(2,1)S(1)} %get-tuple-element.67.residual_ref, bf16[64,1024]{1,0:T(8,128)(2,1)S(1)} %get-tuple-element.68.refs_0_, bf16[64,1024]{1,0:T(8,128)(2,1)S(1)} %get-tuple-element.69.refs_1_, ...), custom_call_target="tpu_custom_call" | custom-call | tf_op jit(solution)/shard_map/cond/branch_0_fun/finish/pallas_call | solution.py:519
  (1 shorter events, 0.0 us)
Async XLA Ops:
  7.3 11.3 %collective-permute-start.3 = (bf16[168,128]{1,0:T(8,128)(2,1)S(1)}, bf16[168,128]{1,0:T(8,128)(2,1)S(1)}, u32[]{:S(2)}, u32[]{:S(2)}) collective-permute-start(bf16[168,128]{1,0:T(8,128)(2,1)S(1)} %get-tuple-element.144), channel_id=1, source_target_pairs={{0,28},{4,24},{8,20},{12,16},{16,12},{20,8},{24,4},{28,0},{1,29},{... | collective-permute-start | bytes 129032 | tf_op jit(solution)/shard_map/ppermute | solution.py:538
  13.3 6.1 %collective-permute-start.4 = (bf16[168,128]{1,0:T(8,128)(2,1)S(1)}, bf16[168,128]{1,0:T(8,128)(2,1)S(1)}, u32[]{:S(2)}, u32[]{:S(2)}) collective-permute-start(bf16[168,128]{1,0:T(8,128)(2,1)S(1)} %get-tuple-element.145), channel_id=1, source_target_pairs={{0,24},{4,28},{8,16},{12,20},{16,8},{20,12},{24,0},{28,4},{1,25},{... | collective-permute-start | bytes 129032 | tf_op jit(solution)/shard_map/ppermute | solution.py:538
  13.5 9.1 %collective-permute-start.5 = (bf16[168,128]{1,0:T(8,128)(2,1)S(1)}, bf16[168,128]{1,0:T(8,128)(2,1)S(1)}, u32[]{:S(2)}, u32[]{:S(2)}) collective-permute-start(bf16[168,128]{1,0:T(8,128)(2,1)S(1)} %get-tuple-element.146), channel_id=1, source_target_pairs={{0,20},{4,16},{8,28},{12,24},{16,4},{20,0},{24,12},{28,8},{1,21},{... | collective-permute-start | bytes 129032 | tf_op jit(solution)/shard_map/ppermute | solution.py:538
  14.3 8.3 %collective-permute-start.6 = (bf16[168,128]{1,0:T(8,128)(2,1)S(1)}, bf16[168,128]{1,0:T(8,128)(2,1)S(1)}, u32[]{:S(2)}, u32[]{:S(2)}) collective-permute-start(bf16[168,128]{1,0:T(8,128)(2,1)S(1)} %get-tuple-element.147), channel_id=1, source_target_pairs={{0,16},{4,20},{8,24},{12,28},{16,0},{20,4},{24,8},{28,12},{1,17},{... | collective-permute-start | bytes 129032 | tf_op jit(solution)/shard_map/ppermute | solution.py:538
  16.3 6.3 %collective-permute-start.7 = (bf16[168,128]{1,0:T(8,128)(2,1)S(1)}, bf16[168,128]{1,0:T(8,128)(2,1)S(1)}, u32[]{:S(2)}, u32[]{:S(2)}) collective-permute-start(bf16[168,128]{1,0:T(8,128)(2,1)S(1)} %get-tuple-element.148), channel_id=1, source_target_pairs={{0,12},{4,8},{8,4},{12,0},{16,28},{20,24},{24,20},{28,16},{1,13},{... | collective-permute-start | bytes 129032 | tf_op jit(solution)/shard_map/ppermute | solution.py:538
  18.6 4.0 %collective-permute-start.8 = (bf16[168,128]{1,0:T(8,128)(2,1)S(1)}, bf16[168,128]{1,0:T(8,128)(2,1)S(1)}, u32[]{:S(2)}, u32[]{:S(2)}) collective-permute-start(bf16[168,128]{1,0:T(8,128)(2,1)S(1)} %get-tuple-element.149), channel_id=1, source_target_pairs={{0,8},{4,12},{8,0},{12,4},{16,24},{20,28},{24,16},{28,20},{1,9},{5... | collective-permute-start | bytes 129032 | tf_op jit(solution)/shard_map/ppermute | solution.py:538
  19.4 4.0 %collective-permute-start.9 = (bf16[168,128]{1,0:T(8,128)(2,1)S(1)}, bf16[168,128]{1,0:T(8,128)(2,1)S(1)}, u32[]{:S(2)}, u32[]{:S(2)}) collective-permute-start(bf16[168,128]{1,0:T(8,128)(2,1)S(1)} %get-tuple-element.150), channel_id=1, source_target_pairs={{0,4},{4,0},{8,12},{12,8},{16,20},{20,16},{24,28},{28,24},{1,5},{5... | collective-permute-start | bytes 129032 | tf_op jit(solution)/shard_map/ppermute | solution.py:538
  27.7 5.5 %collective-permute-start.10 = (bf16[1104,128]{1,0:T(8,128)(2,1)S(1)}, bf16[1104,128]{1,0:T(8,128)(2,1)S(1)}, u32[]{:S(2)}, u32[]{:S(2)}) collective-permute-start(bf16[1104,128]{1,0:T(8,128)(2,1)S(1)} %get-tuple-element.165), channel_id=1, source_target_pairs={{0,1},{1,0},{2,3},{3,2},{4,5},{5,4},{6,7},{7,6},{8,9},{9,8},{10,11... | collective-permute-start | bytes 847880 | tf_op jit(solution)/shard_map/ppermute | solution.py:538
  27.8 5.0 %collective-permute-start.12 = (bf16[80,128]{1,0:T(8,128)(2,1)S(1)}, bf16[80,128]{1,0:T(8,128)(2,1)S(1)}, u32[]{:S(2)}, u32[]{:S(2)}) collective-permute-start(bf16[80,128]{1,0:T(8,128)(2,1)S(1)} %get-tuple-element.168.refs_0_), channel_id=1, source_target_pairs={{0,3},{1,2},{2,1},{3,0},{4,7},{5,6},{6,5},{7,4},{8,11},{9,10},{10,... | collective-permute-start | bytes 61448 | tf_op jit(solution)/shard_map/ppermute | solution.py:538
  29.4 3.8 %collective-permute-start.11 = (bf16[80,128]{1,0:T(8,128)(2,1)S(1)}, bf16[80,128]{1,0:T(8,128)(2,1)S(1)}, u32[]{:S(2)}, u32[]{:S(2)}) collective-permute-start(bf16[80,128]{1,0:T(8,128)(2,1)S(1)} %get-tuple-element.168.refs_0_), channel_id=1, source_target_pairs={{0,2},{1,3},{2,0},{3,1},{4,6},{5,7},{6,4},{7,5},{8,10},{9,11},{10,... | collective-permute-start | bytes 61448 | tf_op jit(solution)/shard_map/ppermute | solution.py:538
  32.7 16.7 %copy-start = (s32[32]{0:T(128)S(1)}, s32[32]{0:T(128)}, u32[]{:S(2)}) copy-start(s32[32]{0:T(128)} %param.22) | copy-start | bytes 388
  32.7 16.7 %copy-start.2 = (bf16[64,1024]{1,0:T(8,128)(2,1)S(1)}, bf16[64,1024]{1,0:T(8,128)(2,1)}, u32[]{:S(2)}) copy-start(bf16[64,1024]{1,0:T(8,128)(2,1)} %param.21) | copy-start | bytes 393220
  32.7 16.7 %copy-start.3 = (s32[64,1]{0,1:T(1,128)S(1)}, s32[64,1]{0,1:T(1,128)}, u32[]{:S(2)}) copy-start(s32[64,1]{0,1:T(1,128)} %param.23) | copy-start | bytes 772
  34.3 8.8 %collective-permute-start.13 = (bf16[64,1024]{1,0:T(8,128)(2,1)S(1)}, bf16[64,1024]{1,0:T(8,128)(2,1)S(1)}, u32[]{:S(2)}, u32[]{:S(2)}) collective-permute-start(bf16[64,1024]{1,0:T(8,128)(2,1)S(1)} %get-tuple-element.180), channel_id=1, source_target_pairs={{0,2},{1,3},{2,0},{3,1},{4,6},{5,7},{6,4},{7,5},{8,10},{9,11},{10,... | collective-permute-start | bytes 393224 | tf_op jit(solution)/shard_map/ppermute | solution.py:538
  35.4 9.2 %collective-permute-start.14 = (bf16[160,128]{1,0:T(8,128)(2,1)S(1)}, bf16[160,128]{1,0:T(8,128)(2,1)S(1)}, u32[]{:S(2)}, u32[]{:S(2)}) collective-permute-start(bf16[160,128]{1,0:T(8,128)(2,1)S(1)} %get-tuple-element.184), channel_id=1, source_target_pairs={{0,28},{4,24},{8,20},{12,16},{16,12},{20,8},{24,4},{28,0},{1,29},{... | collective-permute-start | bytes 122888 | tf_op jit(solution)/shard_map/ppermute | solution.py:538
  39.3 6.1 %collective-permute-start.15 = (bf16[160,128]{1,0:T(8,128)(2,1)S(1)}, bf16[160,128]{1,0:T(8,128)(2,1)S(1)}, u32[]{:S(2)}, u32[]{:S(2)}) collective-permute-start(bf16[160,128]{1,0:T(8,128)(2,1)S(1)} %get-tuple-element.185), channel_id=1, source_target_pairs={{0,24},{4,28},{8,16},{12,20},{16,8},{20,12},{24,0},{28,4},{1,25},{... | collective-permute-start | bytes 122888 | tf_op jit(solution)/shard_map/ppermute | solution.py:538
  39.5 7.7 %collective-permute-start.16 = (bf16[160,128]{1,0:T(8,128)(2,1)S(1)}, bf16[160,128]{1,0:T(8,128)(2,1)S(1)}, u32[]{:S(2)}, u32[]{:S(2)}) collective-permute-start(bf16[160,128]{1,0:T(8,128)(2,1)S(1)} %get-tuple-element.186), channel_id=1, source_target_pairs={{0,20},{4,16},{8,28},{12,24},{16,4},{20,0},{24,12},{28,8},{1,21},{... | collective-permute-start | bytes 122888 | tf_op jit(solution)/shard_map/ppermute | solution.py:538
  40.5 6.7 %collective-permute-start.17 = (bf16[160,128]{1,0:T(8,128)(2,1)S(1)}, bf16[160,128]{1,0:T(8,128)(2,1)S(1)}, u32[]{:S(2)}, u32[]{:S(2)}) collective-permute-start(bf16[160,128]{1,0:T(8,128)(2,1)S(1)} %get-tuple-element.187), channel_id=1, source_target_pairs={{0,16},{4,20},{8,24},{12,28},{16,0},{20,4},{24,8},{28,12},{1,17},{... | collective-permute-start | bytes 122888 | tf_op jit(solution)/shard_map/ppermute | solution.py:538
  43.1 4.9 %collective-permute-start.18 = (bf16[160,128]{1,0:T(8,128)(2,1)S(1)}, bf16[160,128]{1,0:T(8,128)(2,1)S(1)}, u32[]{:S(2)}, u32[]{:S(2)}) collective-permute-start(bf16[160,128]{1,0:T(8,128)(2,1)S(1)} %get-tuple-element.188), channel_id=1, source_target_pairs={{0,12},{4,8},{8,4},{12,0},{16,28},{20,24},{24,20},{28,16},{1,13},{... | collective-permute-start | bytes 122888 | tf_op jit(solution)/shard_map/ppermute | solution.py:538
  44.6 4.0 %collective-permute-start.19 = (bf16[160,128]{1,0:T(8,128)(2,1)S(1)}, bf16[160,128]{1,0:T(8,128)(2,1)S(1)}, u32[]{:S(2)}, u32[]{:S(2)}) collective-permute-start(bf16[160,128]{1,0:T(8,128)(2,1)S(1)} %get-tuple-element.189), channel_id=1, source_target_pairs={{0,8},{4,12},{8,0},{12,4},{16,24},{20,28},{24,16},{28,20},{1,9},{5... | collective-permute-start | bytes 122888 | tf_op jit(solution)/shard_map/ppermute | solution.py:538
  45.4 4.0 %collective-permute-start.20 = (bf16[160,128]{1,0:T(8,128)(2,1)S(1)}, bf16[160,128]{1,0:T(8,128)(2,1)S(1)}, u32[]{:S(2)}, u32[]{:S(2)}) collective-permute-start(bf16[160,128]{1,0:T(8,128)(2,1)S(1)} %get-tuple-element.190), channel_id=1, source_target_pairs={{0,4},{4,0},{8,12},{12,8},{16,20},{20,16},{24,28},{28,24},{1,5},{5... | collective-permute-start | bytes 122888 | tf_op jit(solution)/shard_map/ppermute | solution.py:538

commit v4 on v2

--- a/solution.py
+++ b/solution.py
@@ -74,6 +74,8 @@
         packed,
         numbers,
         counts,
+        spot_ref,
+        places,
         small_sem,
         key_sem,
         value_sem,
@@ -129,13 +131,16 @@
         counts[owner] = before + 1
         block = block_of(owner ^ me, host_count)
         fits = before < room
-        place_ref[r] = jnp.where(fits, block * room + before, host_count * room)
+        spot = jnp.where(fits, block * room + before, host_count * room)
+        spot_ref[r] = spot
+        places[pl.ds(r, 1), :] = jnp.where(iota((1, places.shape[1]), 1) == spot, 1.0, 0.0)
         where = jnp.where(fits, block * pad + before, host_count * pad)
         number = jnp.full((1, LANES), adapter - owner * owned_total + 1, jnp.int32)
         numbers[pl.ds(where, 1), :] = number.astype(jnp.float32)
         return jnp.maximum(most, before)
 
     most = lax.fori_loop(0, row_count, count, jnp.int32(0))
+    place_ref[...] = places[...].astype(jnp.bfloat16)
     over = jnp.where(jnp.full((8, LANES), most, jnp.int32) >= room, 1.0, 0.0)
 
     for move in key_moves:
@@ -183,7 +188,7 @@
             for c in range(1, kv_here):
                 result = jnp.where(head_of == c, part[:, c * HD : (c + 1) * HD], result)
             outcome[tile_of(r), :] = result
-            packed[tile_of(place_ref[r]), :] = result
+            packed[tile_of(spot_ref[r]), :] = result
         return carry
 
     lax.fori_loop(0, row_count // GROUP, some_scores, 0)
@@ -213,7 +218,6 @@
 ):
     row_count, feature_here = queries.shape
     spec = pl.BlockSpec(memory_space=pltpu.VMEM)
-    small = pl.BlockSpec(memory_space=pltpu.SMEM)
     far = pl.BlockSpec(memory_space=pl.ANY)
     block = jax.ShapeDtypeStruct((room * HEAD_ROWS + 8, LANES), jnp.bfloat16)
     outs = pl.pallas_call(
@@ -221,13 +225,13 @@
         name="attend",
         out_shape=[
             jax.ShapeDtypeStruct((row_count, feature_here), jnp.bfloat16),
-            jax.ShapeDtypeStruct((row_count,), jnp.int32),
+            jax.ShapeDtypeStruct((row_count, up_to(hosts * room, LANES)), jnp.bfloat16),
             pltpu.VMEM(down.shape, jnp.bfloat16),
             pltpu.VMEM(up.shape, jnp.bfloat16),
         ]
         + [block] * hosts,
         in_specs=[far] * 9,
-        out_specs=[spec, small, spec, spec] + [spec] * hosts,
+        out_specs=[spec] * (4 + hosts),
         scratch_shapes=[
             pltpu.SMEM(pages.shape, jnp.int32),
             pltpu.SMEM(lengths.shape, jnp.int32),
@@ -241,6 +245,8 @@
             pltpu.VMEM(((hosts * room + 1) * HEAD_ROWS, HD), jnp.float32),
             pltpu.VMEM((hosts * up_to(room, 8) + 8, LANES), jnp.float32),
             pltpu.SMEM((hosts,), jnp.int32),
+            pltpu.SMEM((row_count,), jnp.int32),
+            pltpu.VMEM((row_count, up_to(hosts * room, LANES)), jnp.float32),
             pltpu.SemaphoreType.DMA((5,)),
             pltpu.SemaphoreType.DMA((CHUNKS,)),
             pltpu.SemaphoreType.DMA((CHUNKS,)),
@@ -333,18 +339,18 @@
     size = room * HEAD_ROWS
     width = 256
     rank = LANES // 2
-    over = jnp.float32(0)
     lane = iota((8, LANES), 1)
+    over = jnp.zeros((8, LANES), jnp.float32)
     for k in range(host_count):
         tiles[k * size : (k + 1) * size] = blocks[k][:size].astype(jnp.float32)
         tile = blocks[k][size:].astype(jnp.float32)
-        over = jnp.maximum(over, jnp.max(jnp.where(lane == LANES - 1, tile, 0.0)))
+        over = jnp.maximum(over, jnp.where(lane == LANES - 1, tile, 0.0))
         for b in range(up_to(room, 8) // 8):
             rest = min(8, room - 8 * b)
             column = jnp.sum(jnp.where(lane == b, tile, 0.0), axis=1, keepdims=True)
             column = jnp.broadcast_to(column, (8, LANES))
             number_ref[k * room + 8 * b : k * room + 8 * b + rest] = column[:rest]
-    over_ref[0] = (over > 0).astype(jnp.int32)
+    over_ref[...] = over
     rows = jnp.concatenate(
         [tiles[pl.ds(j, rows_all, stride=HEAD_ROWS), :].astype(jnp.bfloat16) for j in range(heads)],
         axis=1,
@@ -387,10 +393,10 @@
             jax.ShapeDtypeStruct((rows // 2, LANES), jnp.bfloat16),
             jax.ShapeDtypeStruct((rows // 2 + odd.size // LANES, LANES), jnp.bfloat16),
             jax.ShapeDtypeStruct((rows, LANES), jnp.float32),
-            jax.ShapeDtypeStruct((1,), jnp.int32),
+            jax.ShapeDtypeStruct((8, LANES), jnp.float32),
         ),
         in_specs=[spec] * (host_count + 2),
-        out_specs=(spec, spec, spec, pl.BlockSpec(memory_space=pltpu.SMEM)),
+        out_specs=(spec,) * 4,
         scratch_shapes=[
             pltpu.VMEM((rows * HEAD_ROWS, HD), jnp.float32),
             pltpu.VMEM((rows, LANES), jnp.float32),
@@ -476,18 +482,19 @@
 
 def finish_kernel(base_count, back_count, place_ref, residual_ref, *refs):
     bases, backs = refs[:base_count], refs[base_count : base_count + back_count]
-    more, (out_ref, tiles, sorted_tiles) = refs[base_count + back_count : -3], refs[-3:]
-    row_count, columns = residual_ref.shape
+    more, (out_ref, tiles) = refs[base_count + back_count : -2], refs[-2:]
+    columns = residual_ref.shape[1]
     size = backs[0].shape[0]
     for k in range(back_count):
         tiles[k * size : (k + 1) * size] = backs[k][...].astype(jnp.float32)
-    tiles[back_count * size :] = jnp.zeros((HEAD_ROWS, HD), jnp.float32)
-    for r in range(row_count):
-        where = pl.multiple_of(place_ref[r] * HEAD_ROWS, HEAD_ROWS)
-        sorted_tiles[r * HEAD_ROWS : (r + 1) * HEAD_ROWS] = tiles[pl.ds(where, HEAD_ROWS), :]
+    used = back_count * size
+    if used < tiles.shape[0]:
+        tiles[used:] = jnp.zeros((tiles.shape[0] - used, HD), jnp.float32)
+    place = place_ref[...]
     for j in range(columns // HD):
         cut = slice(j * HD, (j + 1) * HD)
-        total = sorted_tiles[pl.ds(j, row_count, stride=HEAD_ROWS), :]
+        column = tiles[pl.ds(j, place.shape[1], stride=HEAD_ROWS), :].astype(jnp.bfloat16)
+        total = jnp.dot(place, column, preferred_element_type=jnp.float32)
         for m in more:
             total = total + m[:, cut]
         total = residual_ref[:, cut].astype(jnp.float32) + ADAPTER_SCALE * total
@@ -498,17 +505,14 @@
 
 def finish(place, residual, bases, backs, *more):
     spec = pl.BlockSpec(memory_space=pltpu.VMEM)
-    size = backs[0].shape[0]
     return pl.pallas_call(
         functools.partial(finish_kernel, len(bases), len(backs)),
         name="finish",
         out_shape=pltpu.HBM(residual.shape, jnp.bfloat16),
-        in_specs=[pl.BlockSpec(memory_space=pltpu.SMEM)]
-        + [spec] * (1 + len(bases) + len(backs) + len(more)),
+        in_specs=[spec] * (2 + len(bases) + len(backs) + len(more)),
         out_specs=spec,
         scratch_shapes=[
-            pltpu.VMEM((len(backs) * size + HEAD_ROWS, HD), jnp.float32),
-            pltpu.VMEM((residual.shape[0] * HEAD_ROWS, HD), jnp.float32),
+            pltpu.VMEM((place.shape[1] * HEAD_ROWS, HD), jnp.float32),
         ],
         compiler_params=pltpu.CompilerParams(vmem_limit_bytes=8 * MIB),
     )(place, residual, *bases, *backs, *more)
@@ -625,7 +629,7 @@
     def first_only(bases, backs):
         return finish(place, residual, bases, backs)
 
-    return lax.cond(over[0] > 0, with_second, first_only, bases, backs)
+    return lax.cond(jnp.max(over) > 0, with_second, first_only, bases, backs)
 
 
 def solution(mesh):

time: 49 us -> 47.7 us (0.973)
  Pallas kernels: 17.6 us -> 16.3 us
  waiting for transfers between devices: 3.41 us -> 2.81 us
  other arithmetic: 0 us -> 0.6 us
    reduce_max x0 -> x1, other arithmetic: none -> 0.6 us  [local(): return lax.cond(jnp.max(over) > 0, with_second, first_only, bases, backs)]
    ppermute x18, waiting for transfers between devices: 3.41 us -> 2.81 us  [swap(): return lax.ppermute(value, axis, [(i, i ^ k) for i in range(size)])]
    pallas_call x1, Pallas kernels: 7.53 us -> 6.97 us  [attend(): pl.pallas_call(functools.partial(attention_kernel, owned_total, hosts, ro...]
  transfers between devices with their start and end apart: 18 -> 18, of which waited for: 5 -> 5; matrix products, arithmetic and copies ran while one was open for 0% -> 1% of each run, Pallas kernels for 11% -> 12%
where the time goes in v4:
time: 47.7 us; the launch traced here: 47.6 us
  starting transfers between devices  27 us (57%)
  Pallas kernels  16.3 us (34%)
  waiting for transfers between devices  2.81 us (6%)
  between operations  0.79 us (2%)
  other arithmetic  0.6 us (1%)
    ppermute x18, starting transfers between devices, swap(): return lax.ppermute(value, axis, [(i, i ^ k) for i in range(size)])  27 us
    pallas_call x1, Pallas kernels, attend(): pl.pallas_call(functools.partial(attention_kernel, owned_total, hosts, ro...  6.97 us
    pallas_call x2, Pallas kernels, base_half(): pl.pallas_call(kernel, name=name, out_shape=out_shape, in_specs=[spec, pl...  5.54 us
    ppermute x18, waiting for transfers between devices, swap(): return lax.ppermute(value, axis, [(i, i ^ k) for i in range(size)])  2.81 us
    pallas_call x1, Pallas kernels, shrink(): pl.pallas_call(functools.partial(shrink_kernel, host_count, room), name='...  1.63 us
    pallas_call x1, Pallas kernels, expand(): pl.pallas_call(functools.partial(expand_kernel, len(parts), len(evens), h...  1.1 us
    pallas_call x1, Pallas kernels, finish(): pl.pallas_call(functools.partial(finish_kernel, len(bases), len(backs)),...  1.05 us
  transfers between devices with their start and end apart: 18, of which 5 were waited for; matrix products, arithmetic and copies ran while one was open for 1% of the time, Pallas kernels for 12%

profile of v4, /device:TPU:0, one launch (start us, length us, event | category | flops | bytes accessed | tf_op | source)
XLA Modules:
  0.0 47.6 jit_solution(11029138646150790753)
XLA Ops:
  0.0 7.0 %attend.1 = (bf16[64,1024]{1,0:T(8,128)(2,1)S(1)}, bf16[64,256]{1,0:T(8,128)(2,1)S(1)}, bf16[2048,1024]{1,0:T(8,128)(2,1)S(1)}, bf16[2048,1024]{1,0:T(8,128)(2,1...) custom-call(s32[8,64]{1,0:T(8,128)} %bitcast.36, ...), custom_call_target="tpu_custom_call" | custom-call | flops 268435456 | bytes 16777216 | tf_op jit(solution)/shard_map/attend/pallas_call | solution.py:223
  7.0 6.0 %collective-permute-start.3 = (bf16[168,128]{1,0:T(8,128)(2,1)S(1)}, bf16[168,128]{1,0:T(8,128)(2,1)S(1)}, u32[]{:S(2)}, u32[]{:S(2)}) collective-permute-start(bf16[168,128]{1,0:T(8,128)(2,1)S(1)} %get-tuple-element.144), channel_id=1, source_target_pairs={{0,28},{4,24},{8,20},{12,16},{16,12},{20,8},{24,4},{28,0},{1,29},{... | collective-permute-start | bytes 129032 | tf_op jit(solution)/shard_map/ppermute | solution.py:523
  13.0 0.2 collective-permute-start.4
  13.2 0.8 %collective-permute-start.5 = (bf16[168,128]{1,0:T(8,128)(2,1)S(1)}, bf16[168,128]{1,0:T(8,128)(2,1)S(1)}, u32[]{:S(2)}, u32[]{:S(2)}) collective-permute-start(bf16[168,128]{1,0:T(8,128)(2,1)S(1)} %get-tuple-element.146), channel_id=1, source_target_pairs={{0,20},{4,16},{8,28},{12,24},{16,4},{20,0},{24,12},{28,8},{1,21},{... | collective-permute-start | bytes 129032 | tf_op jit(solution)/shard_map/ppermute | solution.py:523
  14.0 2.0 %collective-permute-start.6 = (bf16[168,128]{1,0:T(8,128)(2,1)S(1)}, bf16[168,128]{1,0:T(8,128)(2,1)S(1)}, u32[]{:S(2)}, u32[]{:S(2)}) collective-permute-start(bf16[168,128]{1,0:T(8,128)(2,1)S(1)} %get-tuple-element.147), channel_id=1, source_target_pairs={{0,16},{4,20},{8,24},{12,28},{16,0},{20,4},{24,8},{28,12},{1,17},{... | collective-permute-start | bytes 129032 | tf_op jit(solution)/shard_map/ppermute | solution.py:523
  16.0 2.3 %collective-permute-start.7 = (bf16[168,128]{1,0:T(8,128)(2,1)S(1)}, bf16[168,128]{1,0:T(8,128)(2,1)S(1)}, u32[]{:S(2)}, u32[]{:S(2)}) collective-permute-start(bf16[168,128]{1,0:T(8,128)(2,1)S(1)} %get-tuple-element.148), channel_id=1, source_target_pairs={{0,12},{4,8},{8,4},{12,0},{16,28},{20,24},{24,20},{28,16},{1,13},{... | collective-permute-start | bytes 129032 | tf_op jit(solution)/shard_map/ppermute | solution.py:523
  18.3 0.0 collective-permute-done.3.refs_1_
  18.3 0.8 %collective-permute-start.8 = (bf16[168,128]{1,0:T(8,128)(2,1)S(1)}, bf16[168,128]{1,0:T(8,128)(2,1)S(1)}, u32[]{:S(2)}, u32[]{:S(2)}) collective-permute-start(bf16[168,128]{1,0:T(8,128)(2,1)S(1)} %get-tuple-element.149), channel_id=1, source_target_pairs={{0,8},{4,12},{8,0},{12,4},{16,24},{20,28},{24,16},{28,20},{1,9},{5... | collective-permute-start | bytes 129032 | tf_op jit(solution)/shard_map/ppermute | solution.py:523
  19.1 0.0 collective-permute-done.4.refs_2_
  19.1 0.4 collective-permute-start.9
  19.5 2.8 %base_odd.1.refs_9_ = bf16[128,1024]{1,0:T(8,128)(2,1)S(1)} custom-call(bf16[64,1024]{1,0:T(8,128)(2,1)S(1)} %get-tuple-element.151.attended_ref, bf16[1024,4096]{1,0:T(8,128)(2,1)} %weight_hbm.3), custom_call_target="tpu_custom_call" | custom-call | flops 268435456 | bytes 4194304 | tf_op jit(solution)/shard_map/base_odd/pallas_call | solution.py:316
  22.3 0.0 collective-permute-done.5.refs_3_
  22.3 0.0 collective-permute-done.6.refs_4_
  22.3 0.0 collective-permute-done.7.refs_5_
  22.3 0.0 collective-permute-done.8.refs_6_
  22.3 0.8 %collective-permute-done.9.refs_7_ = bf16[168,128]{1,0:T(8,128)(2,1)S(1)} collective-permute-done((bf16[168,128]{1,0:T(8,128)(2,1)S(1)}, bf16[168,128]{1,0:T(8,128)(2,1)S(1)}, u32[]{:S(2)}, u32[]{:S(2)}) %collective-permute-start.9) | collective-permute-done | bytes 43040 | tf_op jit(solution)/shard_map/ppermute | solution.py:523
  23.1 1.6 %shrink.1 = (bf16[80,128]{1,0:T(8,128)(2,1)S(1)}, bf16[1104,128]{1,0:T(8,128)(2,1)S(1)}, f32[160,128]{1,0:T(8,128)S(1)}, f32[8,128]{1,0:T(8,128)S(1)}) custom-call(bf16[168,128]{1,0:T(8,128)(2,1)S(1)} %get-tuple-element.152.refs_0_, bf16[168,128]{1,0:T(8,128)(2,1)S(1)} %collective-permute-done.3.refs_1_, ...), custom_call_target="tpu_custom_call" | custom-call | flops 671088640 | bytes 4194304 | tf_op jit(solution)/shard_map/shrink/pallas_call | solution.py:389
  24.8 0.1 collective-permute-start.10
  24.8 1.6 %collective-permute-start.12 = (bf16[80,128]{1,0:T(8,128)(2,1)S(1)}, bf16[80,128]{1,0:T(8,128)(2,1)S(1)}, u32[]{:S(2)}, u32[]{:S(2)}) collective-permute-start(bf16[80,128]{1,0:T(8,128)(2,1)S(1)} %get-tuple-element.168.refs_0_), channel_id=1, source_target_pairs={{0,3},{1,2},{2,1},{3,0},{4,7},{5,6},{6,5},{7,4},{8,11},{9,10},{10,... | collective-permute-start | bytes 61448 | tf_op jit(solution)/shard_map/ppermute | solution.py:523
  26.5 0.5 %collective-permute-start.11 = (bf16[80,128]{1,0:T(8,128)(2,1)S(1)}, bf16[80,128]{1,0:T(8,128)(2,1)S(1)}, u32[]{:S(2)}, u32[]{:S(2)}) collective-permute-start(bf16[80,128]{1,0:T(8,128)(2,1)S(1)} %get-tuple-element.168.refs_0_), channel_id=1, source_target_pairs={{0,2},{1,3},{2,0},{3,1},{4,6},{5,7},{6,4},{7,5},{8,10},{9,11},{10,... | collective-permute-start | bytes 61448 | tf_op jit(solution)/shard_map/ppermute | solution.py:523
  27.0 2.8 %base_even.1 = (bf16[64,1024]{1,0:T(8,128)(2,1)S(1)}, bf16[64,1024]{1,0:T(8,128)(2,1)S(1)}) custom-call(bf16[64,1024]{1,0:T(8,128)(2,1)S(1)} %get-tuple-element.151.attended_ref, bf16[1024,4096]{1,0:T(8,128)(2,1)} %weight_hbm.3), custom_call_target="tpu_custom_call" | custom-call | flops 268435456 | bytes 4194304 | tf_op jit(solution)/shard_map/base_even/pallas_call | solution.py:316
  29.8 0.0 copy-start
  29.8 0.0 copy-start.2
  29.8 0.0 copy-start.3
  29.8 0.0 collective-permute-done.12.refs_3_
  29.8 0.4 collective-permute-done.11.refs_2_
  30.3 0.0 collective-permute-done.10.refs_1_
  30.3 1.1 %expand.1 = (bf16[160,128]{1,0:T(8,128)(2,1)S(1)}, bf16[160,128]{1,0:T(8,128)(2,1)S(1)}, bf16[160,128]{1,0:T(8,128)(2,1)S(1)}, bf16[160,128]{1,0:T(8,128)(2,1)S(...) custom-call(bf16[80,128]{1,0:T(8,128)(2,1)S(1)} %get-tuple-element.1, ...), custom_call_target="tpu_custom_call" | custom-call | flops 671088640 | bytes 4194304 | tf_op jit(solution)/shard_map/expand/pallas_call | solution.py:464
  31.4 1.2 %collective-permute-start.13 = (bf16[64,1024]{1,0:T(8,128)(2,1)S(1)}, bf16[64,1024]{1,0:T(8,128)(2,1)S(1)}, u32[]{:S(2)}, u32[]{:S(2)}) collective-permute-start(bf16[64,1024]{1,0:T(8,128)(2,1)S(1)} %get-tuple-element.180), channel_id=1, source_target_pairs={{0,2},{1,3},{2,0},{3,1},{4,6},{5,7},{6,4},{7,5},{8,10},{9,11},{10,... | collective-permute-start | bytes 393224 | tf_op jit(solution)/shard_map/ppermute | solution.py:523
  32.5 3.9 %collective-permute-start.14 = (bf16[160,128]{1,0:T(8,128)(2,1)S(1)}, bf16[160,128]{1,0:T(8,128)(2,1)S(1)}, u32[]{:S(2)}, u32[]{:S(2)}) collective-permute-start(bf16[160,128]{1,0:T(8,128)(2,1)S(1)} %get-tuple-element.184), channel_id=1, source_target_pairs={{0,28},{4,24},{8,20},{12,16},{16,12},{20,8},{24,4},{28,0},{1,29},{... | collective-permute-start | bytes 122888 | tf_op jit(solution)/shard_map/ppermute | solution.py:523
  36.4 0.2 collective-permute-start.15
  36.6 1.0 %collective-permute-start.16 = (bf16[160,128]{1,0:T(8,128)(2,1)S(1)}, bf16[160,128]{1,0:T(8,128)(2,1)S(1)}, u32[]{:S(2)}, u32[]{:S(2)}) collective-permute-start(bf16[160,128]{1,0:T(8,128)(2,1)S(1)} %get-tuple-element.186), channel_id=1, source_target_pairs={{0,20},{4,16},{8,28},{12,24},{16,4},{20,0},{24,12},{28,8},{1,21},{... | collective-permute-start | bytes 122888 | tf_op jit(solution)/shard_map/ppermute | solution.py:523
  37.7 2.5 %collective-permute-start.17 = (bf16[160,128]{1,0:T(8,128)(2,1)S(1)}, bf16[160,128]{1,0:T(8,128)(2,1)S(1)}, u32[]{:S(2)}, u32[]{:S(2)}) collective-permute-start(bf16[160,128]{1,0:T(8,128)(2,1)S(1)} %get-tuple-element.187), channel_id=1, source_target_pairs={{0,16},{4,20},{8,24},{12,28},{16,0},{20,4},{24,8},{28,12},{1,17},{... | collective-permute-start | bytes 122888 | tf_op jit(solution)/shard_map/ppermute | solution.py:523
  40.2 0.0 collective-permute-done.13
  40.2 1.5 %collective-permute-start.18 = (bf16[160,128]{1,0:T(8,128)(2,1)S(1)}, bf16[160,128]{1,0:T(8,128)(2,1)S(1)}, u32[]{:S(2)}, u32[]{:S(2)}) collective-permute-start(bf16[160,128]{1,0:T(8,128)(2,1)S(1)} %get-tuple-element.188), channel_id=1, source_target_pairs={{0,12},{4,8},{8,4},{12,0},{16,28},{20,24},{24,20},{28,16},{1,13},{... | collective-permute-start | bytes 122888 | tf_op jit(solution)/shard_map/ppermute | solution.py:523
  41.7 0.0 collective-permute-done.14
  41.7 0.8 %collective-permute-start.19 = (bf16[160,128]{1,0:T(8,128)(2,1)S(1)}, bf16[160,128]{1,0:T(8,128)(2,1)S(1)}, u32[]{:S(2)}, u32[]{:S(2)}) collective-permute-start(bf16[160,128]{1,0:T(8,128)(2,1)S(1)} %get-tuple-element.189), channel_id=1, source_target_pairs={{0,8},{4,12},{8,0},{12,4},{16,24},{20,28},{24,16},{28,20},{1,9},{5... | collective-permute-start | bytes 122888 | tf_op jit(solution)/shard_map/ppermute | solution.py:523
  42.5 0.0 collective-permute-done.15
  42.5 1.2 %collective-permute-start.20 = (bf16[160,128]{1,0:T(8,128)(2,1)S(1)}, bf16[160,128]{1,0:T(8,128)(2,1)S(1)}, u32[]{:S(2)}, u32[]{:S(2)}) collective-permute-start(bf16[160,128]{1,0:T(8,128)(2,1)S(1)} %get-tuple-element.190), channel_id=1, source_target_pairs={{0,4},{4,0},{8,12},{12,8},{16,20},{20,16},{24,28},{28,24},{1,5},{5... | collective-permute-start | bytes 122888 | tf_op jit(solution)/shard_map/ppermute | solution.py:523
  43.7 0.6 %reduce_max.9 = f32[]{:T(128)} reduce(f32[8,128]{1,0:T(8,128)S(1)} %get-tuple-element.162, f32[]{:T(128)} %constant.47.clone.1), dimensions={0,1}, to_apply=%region_0.0 | reduce | flops 1023 | bytes 4104 | tf_op jit(solution)/shard_map/reduce_max | solution.py:632
  44.9 0.0 collective-permute-done.16
  44.9 0.0 collective-permute-done.17
  44.9 0.1 collective-permute-done.18
  45.1 0.6 %collective-permute-done.19 = bf16[160,128]{1,0:T(8,128)(2,1)S(1)} collective-permute-done((bf16[160,128]{1,0:T(8,128)(2,1)S(1)}, bf16[160,128]{1,0:T(8,128)(2,1)S(1)}, u32[]{:S(2)}, u32[]{:S(2)}) %collective-permute-start.19) | collective-permute-done | bytes 40992 | tf_op jit(solution)/shard_map/ppermute | solution.py:523
  45.7 0.8 %collective-permute-done.20 = bf16[160,128]{1,0:T(8,128)(2,1)S(1)} collective-permute-done((bf16[160,128]{1,0:T(8,128)(2,1)S(1)}, bf16[160,128]{1,0:T(8,128)(2,1)S(1)}, u32[]{:S(2)}, u32[]{:S(2)}) %collective-permute-start.20) | collective-permute-done | bytes 40992 | tf_op jit(solution)/shard_map/ppermute | solution.py:523
  46.5 0.0 copy-done
  46.5 1.1 %conditional.1 = (bf16[64,1024]{1,0:T(8,128)(2,1)}) conditional(s32[]{:T(128)} %convert_element_type.44, (bf16[64,256]{1,0:T(8,128)(2,1)S(1)}, bf16[64,1024]{1,0:T(8,128)(2,1)S(1)}, bf16[64,1024]{1,0:T(8,128)(2,1)S(1)}, bf16[64,1024]{1,0:T(8,128)(2,1)S(1)}, bf16[160,128]{1,0:T(8,128)(2,1)S(1)}, /*index=5*/bf16[160,128]{1,0:T(8,128)(2,1)S(1)}, ...), branch_computations={%region_1.0_spmd, %region_2.5_spmd} | conditional | flops 1109062016 | bytes 29252028 | solution.py:632
  46.5 1.0 %finish.2 = bf16[64,1024]{1,0:T(8,128)(2,1)} custom-call(bf16[64,256]{1,0:T(8,128)(2,1)S(1)} %get-tuple-element.66.place_ref, bf16[64,1024]{1,0:T(8,128)(2,1)S(1)} %get-tuple-element.67.residual_ref, bf16[64,1024]{1,0:T(8,128)(2,1)S(1)} %get-tuple-element.68.refs_0_, bf16[64,1024]{1,0:T(8,128)(2,1)S(1)} %get-tuple-element.69.refs_1_, ...), custom_call_target="tpu_custom_call" | custom-call | tf_op jit(solution)/shard_map/cond/branch_0_fun/finish/pallas_call | solution.py:508
  (2 shorter events, 0.0 us)
Async XLA Ops:
  7.0 11.3 %collective-permute-start.3 = (bf16[168,128]{1,0:T(8,128)(2,1)S(1)}, bf16[168,128]{1,0:T(8,128)(2,1)S(1)}, u32[]{:S(2)}, u32[]{:S(2)}) collective-permute-start(bf16[168,128]{1,0:T(8,128)(2,1)S(1)} %get-tuple-element.144), channel_id=1, source_target_pairs={{0,28},{4,24},{8,20},{12,16},{16,12},{20,8},{24,4},{28,0},{1,29},{... | collective-permute-start | bytes 129032 | tf_op jit(solution)/shard_map/ppermute | solution.py:523
  13.0 6.1 %collective-permute-start.4 = (bf16[168,128]{1,0:T(8,128)(2,1)S(1)}, bf16[168,128]{1,0:T(8,128)(2,1)S(1)}, u32[]{:S(2)}, u32[]{:S(2)}) collective-permute-start(bf16[168,128]{1,0:T(8,128)(2,1)S(1)} %get-tuple-element.145), channel_id=1, source_target_pairs={{0,24},{4,28},{8,16},{12,20},{16,8},{20,12},{24,0},{28,4},{1,25},{... | collective-permute-start | bytes 129032 | tf_op jit(solution)/shard_map/ppermute | solution.py:523
  13.2 9.1 %collective-permute-start.5 = (bf16[168,128]{1,0:T(8,128)(2,1)S(1)}, bf16[168,128]{1,0:T(8,128)(2,1)S(1)}, u32[]{:S(2)}, u32[]{:S(2)}) collective-permute-start(bf16[168,128]{1,0:T(8,128)(2,1)S(1)} %get-tuple-element.146), channel_id=1, source_target_pairs={{0,20},{4,16},{8,28},{12,24},{16,4},{20,0},{24,12},{28,8},{1,21},{... | collective-permute-start | bytes 129032 | tf_op jit(solution)/shard_map/ppermute | solution.py:523
  14.0 8.3 %collective-permute-start.6 = (bf16[168,128]{1,0:T(8,128)(2,1)S(1)}, bf16[168,128]{1,0:T(8,128)(2,1)S(1)}, u32[]{:S(2)}, u32[]{:S(2)}) collective-permute-start(bf16[168,128]{1,0:T(8,128)(2,1)S(1)} %get-tuple-element.147), channel_id=1, source_target_pairs={{0,16},{4,20},{8,24},{12,28},{16,0},{20,4},{24,8},{28,12},{1,17},{... | collective-permute-start | bytes 129032 | tf_op jit(solution)/shard_map/ppermute | solution.py:523
  16.0 6.3 %collective-permute-start.7 = (bf16[168,128]{1,0:T(8,128)(2,1)S(1)}, bf16[168,128]{1,0:T(8,128)(2,1)S(1)}, u32[]{:S(2)}, u32[]{:S(2)}) collective-permute-start(bf16[168,128]{1,0:T(8,128)(2,1)S(1)} %get-tuple-element.148), channel_id=1, source_target_pairs={{0,12},{4,8},{8,4},{12,0},{16,28},{20,24},{24,20},{28,16},{1,13},{... | collective-permute-start | bytes 129032 | tf_op jit(solution)/shard_map/ppermute | solution.py:523
  18.3 4.0 %collective-permute-start.8 = (bf16[168,128]{1,0:T(8,128)(2,1)S(1)}, bf16[168,128]{1,0:T(8,128)(2,1)S(1)}, u32[]{:S(2)}, u32[]{:S(2)}) collective-permute-start(bf16[168,128]{1,0:T(8,128)(2,1)S(1)} %get-tuple-element.149), channel_id=1, source_target_pairs={{0,8},{4,12},{8,0},{12,4},{16,24},{20,28},{24,16},{28,20},{1,9},{5... | collective-permute-start | bytes 129032 | tf_op jit(solution)/shard_map/ppermute | solution.py:523
  19.1 4.0 %collective-permute-start.9 = (bf16[168,128]{1,0:T(8,128)(2,1)S(1)}, bf16[168,128]{1,0:T(8,128)(2,1)S(1)}, u32[]{:S(2)}, u32[]{:S(2)}) collective-permute-start(bf16[168,128]{1,0:T(8,128)(2,1)S(1)} %get-tuple-element.150), channel_id=1, source_target_pairs={{0,4},{4,0},{8,12},{12,8},{16,20},{20,16},{24,28},{28,24},{1,5},{5... | collective-permute-start | bytes 129032 | tf_op jit(solution)/shard_map/ppermute | solution.py:523
  24.8 5.5 %collective-permute-start.10 = (bf16[1104,128]{1,0:T(8,128)(2,1)S(1)}, bf16[1104,128]{1,0:T(8,128)(2,1)S(1)}, u32[]{:S(2)}, u32[]{:S(2)}) collective-permute-start(bf16[1104,128]{1,0:T(8,128)(2,1)S(1)} %get-tuple-element.165), channel_id=1, source_target_pairs={{0,1},{1,0},{2,3},{3,2},{4,5},{5,4},{6,7},{7,6},{8,9},{9,8},{10,11... | collective-permute-start | bytes 847880 | tf_op jit(solution)/shard_map/ppermute | solution.py:523
  24.8 5.0 %collective-permute-start.12 = (bf16[80,128]{1,0:T(8,128)(2,1)S(1)}, bf16[80,128]{1,0:T(8,128)(2,1)S(1)}, u32[]{:S(2)}, u32[]{:S(2)}) collective-permute-start(bf16[80,128]{1,0:T(8,128)(2,1)S(1)} %get-tuple-element.168.refs_0_), channel_id=1, source_target_pairs={{0,3},{1,2},{2,1},{3,0},{4,7},{5,6},{6,5},{7,4},{8,11},{9,10},{10,... | collective-permute-start | bytes 61448 | tf_op jit(solution)/shard_map/ppermute | solution.py:523
  26.5 3.8 %collective-permute-start.11 = (bf16[80,128]{1,0:T(8,128)(2,1)S(1)}, bf16[80,128]{1,0:T(8,128)(2,1)S(1)}, u32[]{:S(2)}, u32[]{:S(2)}) collective-permute-start(bf16[80,128]{1,0:T(8,128)(2,1)S(1)} %get-tuple-element.168.refs_0_), channel_id=1, source_target_pairs={{0,2},{1,3},{2,0},{3,1},{4,6},{5,7},{6,4},{7,5},{8,10},{9,11},{10,... | collective-permute-start | bytes 61448 | tf_op jit(solution)/shard_map/ppermute | solution.py:523
  29.8 16.7 %copy-start = (s32[32]{0:T(128)S(1)}, s32[32]{0:T(128)}, u32[]{:S(2)}) copy-start(s32[32]{0:T(128)} %param.22) | copy-start | bytes 388
  29.8 16.7 %copy-start.2 = (bf16[64,1024]{1,0:T(8,128)(2,1)S(1)}, bf16[64,1024]{1,0:T(8,128)(2,1)}, u32[]{:S(2)}) copy-start(bf16[64,1024]{1,0:T(8,128)(2,1)} %param.21) | copy-start | bytes 393220
  29.8 16.7 %copy-start.3 = (s32[64,1]{0,1:T(1,128)S(1)}, s32[64,1]{0,1:T(1,128)}, u32[]{:S(2)}) copy-start(s32[64,1]{0,1:T(1,128)} %param.23) | copy-start | bytes 772
  31.4 8.8 %collective-permute-start.13 = (bf16[64,1024]{1,0:T(8,128)(2,1)S(1)}, bf16[64,1024]{1,0:T(8,128)(2,1)S(1)}, u32[]{:S(2)}, u32[]{:S(2)}) collective-permute-start(bf16[64,1024]{1,0:T(8,128)(2,1)S(1)} %get-tuple-element.180), channel_id=1, source_target_pairs={{0,2},{1,3},{2,0},{3,1},{4,6},{5,7},{6,4},{7,5},{8,10},{9,11},{10,... | collective-permute-start | bytes 393224 | tf_op jit(solution)/shard_map/ppermute | solution.py:523
  32.5 9.2 %collective-permute-start.14 = (bf16[160,128]{1,0:T(8,128)(2,1)S(1)}, bf16[160,128]{1,0:T(8,128)(2,1)S(1)}, u32[]{:S(2)}, u32[]{:S(2)}) collective-permute-start(bf16[160,128]{1,0:T(8,128)(2,1)S(1)} %get-tuple-element.184), channel_id=1, source_target_pairs={{0,28},{4,24},{8,20},{12,16},{16,12},{20,8},{24,4},{28,0},{1,29},{... | collective-permute-start | bytes 122888 | tf_op jit(solution)/shard_map/ppermute | solution.py:523
  36.4 6.1 %collective-permute-start.15 = (bf16[160,128]{1,0:T(8,128)(2,1)S(1)}, bf16[160,128]{1,0:T(8,128)(2,1)S(1)}, u32[]{:S(2)}, u32[]{:S(2)}) collective-permute-start(bf16[160,128]{1,0:T(8,128)(2,1)S(1)} %get-tuple-element.185), channel_id=1, source_target_pairs={{0,24},{4,28},{8,16},{12,20},{16,8},{20,12},{24,0},{28,4},{1,25},{... | collective-permute-start | bytes 122888 | tf_op jit(solution)/shard_map/ppermute | solution.py:523
  36.6 8.3 %collective-permute-start.16 = (bf16[160,128]{1,0:T(8,128)(2,1)S(1)}, bf16[160,128]{1,0:T(8,128)(2,1)S(1)}, u32[]{:S(2)}, u32[]{:S(2)}) collective-permute-start(bf16[160,128]{1,0:T(8,128)(2,1)S(1)} %get-tuple-element.186), channel_id=1, source_target_pairs={{0,20},{4,16},{8,28},{12,24},{16,4},{20,0},{24,12},{28,8},{1,21},{... | collective-permute-start | bytes 122888 | tf_op jit(solution)/shard_map/ppermute | solution.py:523
  37.7 7.3 %collective-permute-start.17 = (bf16[160,128]{1,0:T(8,128)(2,1)S(1)}, bf16[160,128]{1,0:T(8,128)(2,1)S(1)}, u32[]{:S(2)}, u32[]{:S(2)}) collective-permute-start(bf16[160,128]{1,0:T(8,128)(2,1)S(1)} %get-tuple-element.187), channel_id=1, source_target_pairs={{0,16},{4,20},{8,24},{12,28},{16,0},{20,4},{24,8},{28,12},{1,17},{... | collective-permute-start | bytes 122888 | tf_op jit(solution)/shard_map/ppermute | solution.py:523
  40.2 4.9 %collective-permute-start.18 = (bf16[160,128]{1,0:T(8,128)(2,1)S(1)}, bf16[160,128]{1,0:T(8,128)(2,1)S(1)}, u32[]{:S(2)}, u32[]{:S(2)}) collective-permute-start(bf16[160,128]{1,0:T(8,128)(2,1)S(1)} %get-tuple-element.188), channel_id=1, source_target_pairs={{0,12},{4,8},{8,4},{12,0},{16,28},{20,24},{24,20},{28,16},{1,13},{... | collective-permute-start | bytes 122888 | tf_op jit(solution)/shard_map/ppermute | solution.py:523
  41.7 4.0 %collective-permute-start.19 = (bf16[160,128]{1,0:T(8,128)(2,1)S(1)}, bf16[160,128]{1,0:T(8,128)(2,1)S(1)}, u32[]{:S(2)}, u32[]{:S(2)}) collective-permute-start(bf16[160,128]{1,0:T(8,128)(2,1)S(1)} %get-tuple-element.189), channel_id=1, source_target_pairs={{0,8},{4,12},{8,0},{12,4},{16,24},{20,28},{24,16},{28,20},{1,9},{5... | collective-permute-start | bytes 122888 | tf_op jit(solution)/shard_map/ppermute | solution.py:523
  42.5 4.0 %collective-permute-start.20 = (bf16[160,128]{1,0:T(8,128)(2,1)S(1)}, bf16[160,128]{1,0:T(8,128)(2,1)S(1)}, u32[]{:S(2)}, u32[]{:S(2)}) collective-permute-start(bf16[160,128]{1,0:T(8,128)(2,1)S(1)} %get-tuple-element.190), channel_id=1, source_target_pairs={{0,4},{4,0},{8,12},{12,8},{16,20},{20,16},{24,28},{28,24},{1,5},{5... | collective-permute-start | bytes 122888 | tf_op jit(solution)/shard_map/ppermute | solution.py:523

commit v5 on v4

--- a/solution.py
+++ b/solution.py
@@ -126,7 +126,10 @@
 
     def count(r, most):
         adapter = stock_ref[0, slot_ref[0, r]]
-        owner = lax.div(adapter, owned_total)
+        if owned_total & (owned_total - 1) == 0:
+            owner = lax.shift_right_logical(adapter, jnp.int32(owned_total.bit_length() - 1))
+        else:
+            owner = lax.div(adapter, owned_total)
         before = counts[owner]
         counts[owner] = before + 1
         block = block_of(owner ^ me, host_count)
@@ -139,7 +142,7 @@
         numbers[pl.ds(where, 1), :] = number.astype(jnp.float32)
         return jnp.maximum(most, before)
 
-    most = lax.fori_loop(0, row_count, count, jnp.int32(0))
+    most = lax.fori_loop(0, row_count, count, jnp.int32(0), unroll=8)
     place_ref[...] = places[...].astype(jnp.bfloat16)
     over = jnp.where(jnp.full((8, LANES), most, jnp.int32) >= room, 1.0, 0.0)
 

time: 47.7 us -> 47.7 us (level)
  no operation moved by 1% of the time
where the time goes in v5:
time: 47.7 us; the launch traced here: 47.6 us
  starting transfers between devices  27 us (57%)
  Pallas kernels  16.3 us (34%)
  waiting for transfers between devices  2.81 us (6%)
  between operations  0.79 us (2%)
  other arithmetic  0.6 us (1%)
    ppermute x18, starting transfers between devices, swap(): return lax.ppermute(value, axis, [(i, i ^ k) for i in range(size)])  27 us
    pallas_call x1, Pallas kernels, attend(): pl.pallas_call(functools.partial(attention_kernel, owned_total, hosts, ro...  6.96 us
    pallas_call x2, Pallas kernels, base_half(): pl.pallas_call(kernel, name=name, out_shape=out_shape, in_specs=[spec, pl...  5.54 us
    ppermute x18, waiting for transfers between devices, swap(): return lax.ppermute(value, axis, [(i, i ^ k) for i in range(size)])  2.81 us
    pallas_call x1, Pallas kernels, shrink(): pl.pallas_call(functools.partial(shrink_kernel, host_count, room), name='...  1.63 us
    pallas_call x1, Pallas kernels, expand(): pl.pallas_call(functools.partial(expand_kernel, len(parts), len(evens), h...  1.1 us
    pallas_call x1, Pallas kernels, finish(): pl.pallas_call(functools.partial(finish_kernel, len(bases), len(backs)),...  1.05 us
  transfers between devices with their start and end apart: 18, of which 5 were waited for; matrix products, arithmetic and copies ran while one was open for 1% of the time, Pallas kernels for 12%

profile of v5, /device:TPU:0, one launch (start us, length us, event | category | flops | bytes accessed | tf_op | source)
XLA Modules:
  0.0 47.6 jit_solution(15083235345421584070)
XLA Ops:
  0.0 7.0 %attend.1 = (bf16[64,1024]{1,0:T(8,128)(2,1)S(1)}, bf16[64,256]{1,0:T(8,128)(2,1)S(1)}, bf16[2048,1024]{1,0:T(8,128)(2,1)S(1)}, bf16[2048,1024]{1,0:T(8,128)(2,1...) custom-call(s32[8,64]{1,0:T(8,128)} %bitcast.36, ...), custom_call_target="tpu_custom_call" | custom-call | flops 268435456 | bytes 16777216 | tf_op jit(solution)/shard_map/attend/pallas_call | solution.py:226
  7.0 6.0 %collective-permute-start.3 = (bf16[168,128]{1,0:T(8,128)(2,1)S(1)}, bf16[168,128]{1,0:T(8,128)(2,1)S(1)}, u32[]{:S(2)}, u32[]{:S(2)}) collective-permute-start(bf16[168,128]{1,0:T(8,128)(2,1)S(1)} %get-tuple-element.144), channel_id=1, source_target_pairs={{0,28},{4,24},{8,20},{12,16},{16,12},{20,8},{24,4},{28,0},{1,29},{... | collective-permute-start | bytes 129032 | tf_op jit(solution)/shard_map/ppermute | solution.py:526
  13.0 0.2 collective-permute-start.4
  13.2 0.8 %collective-permute-start.5 = (bf16[168,128]{1,0:T(8,128)(2,1)S(1)}, bf16[168,128]{1,0:T(8,128)(2,1)S(1)}, u32[]{:S(2)}, u32[]{:S(2)}) collective-permute-start(bf16[168,128]{1,0:T(8,128)(2,1)S(1)} %get-tuple-element.146), channel_id=1, source_target_pairs={{0,20},{4,16},{8,28},{12,24},{16,4},{20,0},{24,12},{28,8},{1,21},{... | collective-permute-start | bytes 129032 | tf_op jit(solution)/shard_map/ppermute | solution.py:526
  14.0 2.0 %collective-permute-start.6 = (bf16[168,128]{1,0:T(8,128)(2,1)S(1)}, bf16[168,128]{1,0:T(8,128)(2,1)S(1)}, u32[]{:S(2)}, u32[]{:S(2)}) collective-permute-start(bf16[168,128]{1,0:T(8,128)(2,1)S(1)} %get-tuple-element.147), channel_id=1, source_target_pairs={{0,16},{4,20},{8,24},{12,28},{16,0},{20,4},{24,8},{28,12},{1,17},{... | collective-permute-start | bytes 129032 | tf_op jit(solution)/shard_map/ppermute | solution.py:526
  16.0 2.3 %collective-permute-start.7 = (bf16[168,128]{1,0:T(8,128)(2,1)S(1)}, bf16[168,128]{1,0:T(8,128)(2,1)S(1)}, u32[]{:S(2)}, u32[]{:S(2)}) collective-permute-start(bf16[168,128]{1,0:T(8,128)(2,1)S(1)} %get-tuple-element.148), channel_id=1, source_target_pairs={{0,12},{4,8},{8,4},{12,0},{16,28},{20,24},{24,20},{28,16},{1,13},{... | collective-permute-start | bytes 129032 | tf_op jit(solution)/shard_map/ppermute | solution.py:526
  18.3 0.0 collective-permute-done.3.refs_1_
  18.3 0.8 %collective-permute-start.8 = (bf16[168,128]{1,0:T(8,128)(2,1)S(1)}, bf16[168,128]{1,0:T(8,128)(2,1)S(1)}, u32[]{:S(2)}, u32[]{:S(2)}) collective-permute-start(bf16[168,128]{1,0:T(8,128)(2,1)S(1)} %get-tuple-element.149), channel_id=1, source_target_pairs={{0,8},{4,12},{8,0},{12,4},{16,24},{20,28},{24,16},{28,20},{1,9},{5... | collective-permute-start | bytes 129032 | tf_op jit(solution)/shard_map/ppermute | solution.py:526
  19.1 0.0 collective-permute-done.4.refs_2_
  19.1 0.4 collective-permute-start.9
  19.5 2.8 %base_odd.1.refs_9_ = bf16[128,1024]{1,0:T(8,128)(2,1)S(1)} custom-call(bf16[64,1024]{1,0:T(8,128)(2,1)S(1)} %get-tuple-element.151.attended_ref, bf16[1024,4096]{1,0:T(8,128)(2,1)} %weight_hbm.3), custom_call_target="tpu_custom_call" | custom-call | flops 268435456 | bytes 4194304 | tf_op jit(solution)/shard_map/base_odd/pallas_call | solution.py:319
  22.3 0.0 collective-permute-done.5.refs_3_
  22.3 0.0 collective-permute-done.6.refs_4_
  22.3 0.0 collective-permute-done.7.refs_5_
  22.3 0.0 collective-permute-done.8.refs_6_
  22.3 0.8 %collective-permute-done.9.refs_7_ = bf16[168,128]{1,0:T(8,128)(2,1)S(1)} collective-permute-done((bf16[168,128]{1,0:T(8,128)(2,1)S(1)}, bf16[168,128]{1,0:T(8,128)(2,1)S(1)}, u32[]{:S(2)}, u32[]{:S(2)}) %collective-permute-start.9) | collective-permute-done | bytes 43040 | tf_op jit(solution)/shard_map/ppermute | solution.py:526
  23.1 1.6 %shrink.1 = (bf16[80,128]{1,0:T(8,128)(2,1)S(1)}, bf16[1104,128]{1,0:T(8,128)(2,1)S(1)}, f32[160,128]{1,0:T(8,128)S(1)}, f32[8,128]{1,0:T(8,128)S(1)}) custom-call(bf16[168,128]{1,0:T(8,128)(2,1)S(1)} %get-tuple-element.152.refs_0_, bf16[168,128]{1,0:T(8,128)(2,1)S(1)} %collective-permute-done.3.refs_1_, ...), custom_call_target="tpu_custom_call" | custom-call | flops 671088640 | bytes 4194304 | tf_op jit(solution)/shard_map/shrink/pallas_call | solution.py:392
  24.8 0.1 collective-permute-start.10
  24.8 1.6 %collective-permute-start.12 = (bf16[80,128]{1,0:T(8,128)(2,1)S(1)}, bf16[80,128]{1,0:T(8,128)(2,1)S(1)}, u32[]{:S(2)}, u32[]{:S(2)}) collective-permute-start(bf16[80,128]{1,0:T(8,128)(2,1)S(1)} %get-tuple-element.168.refs_0_), channel_id=1, source_target_pairs={{0,3},{1,2},{2,1},{3,0},{4,7},{5,6},{6,5},{7,4},{8,11},{9,10},{10,... | collective-permute-start | bytes 61448 | tf_op jit(solution)/shard_map/ppermute | solution.py:526
  26.5 0.5 %collective-permute-start.11 = (bf16[80,128]{1,0:T(8,128)(2,1)S(1)}, bf16[80,128]{1,0:T(8,128)(2,1)S(1)}, u32[]{:S(2)}, u32[]{:S(2)}) collective-permute-start(bf16[80,128]{1,0:T(8,128)(2,1)S(1)} %get-tuple-element.168.refs_0_), channel_id=1, source_target_pairs={{0,2},{1,3},{2,0},{3,1},{4,6},{5,7},{6,4},{7,5},{8,10},{9,11},{10,... | collective-permute-start | bytes 61448 | tf_op jit(solution)/shard_map/ppermute | solution.py:526
  27.0 2.8 %base_even.1 = (bf16[64,1024]{1,0:T(8,128)(2,1)S(1)}, bf16[64,1024]{1,0:T(8,128)(2,1)S(1)}) custom-call(bf16[64,1024]{1,0:T(8,128)(2,1)S(1)} %get-tuple-element.151.attended_ref, bf16[1024,4096]{1,0:T(8,128)(2,1)} %weight_hbm.3), custom_call_target="tpu_custom_call" | custom-call | flops 268435456 | bytes 4194304 | tf_op jit(solution)/shard_map/base_even/pallas_call | solution.py:319
  29.8 0.0 copy-start
  29.8 0.0 copy-start.2
  29.8 0.0 copy-start.3
  29.8 0.0 collective-permute-done.12.refs_3_
  29.8 0.4 collective-permute-done.11.refs_2_
  30.2 0.0 collective-permute-done.10.refs_1_
  30.3 1.1 %expand.1 = (bf16[160,128]{1,0:T(8,128)(2,1)S(1)}, bf16[160,128]{1,0:T(8,128)(2,1)S(1)}, bf16[160,128]{1,0:T(8,128)(2,1)S(1)}, bf16[160,128]{1,0:T(8,128)(2,1)S(...) custom-call(bf16[80,128]{1,0:T(8,128)(2,1)S(1)} %get-tuple-element.1, ...), custom_call_target="tpu_custom_call" | custom-call | flops 671088640 | bytes 4194304 | tf_op jit(solution)/shard_map/expand/pallas_call | solution.py:467
  31.4 1.2 %collective-permute-start.13 = (bf16[64,1024]{1,0:T(8,128)(2,1)S(1)}, bf16[64,1024]{1,0:T(8,128)(2,1)S(1)}, u32[]{:S(2)}, u32[]{:S(2)}) collective-permute-start(bf16[64,1024]{1,0:T(8,128)(2,1)S(1)} %get-tuple-element.180), channel_id=1, source_target_pairs={{0,2},{1,3},{2,0},{3,1},{4,6},{5,7},{6,4},{7,5},{8,10},{9,11},{10,... | collective-permute-start | bytes 393224 | tf_op jit(solution)/shard_map/ppermute | solution.py:526
  32.5 3.9 %collective-permute-start.14 = (bf16[160,128]{1,0:T(8,128)(2,1)S(1)}, bf16[160,128]{1,0:T(8,128)(2,1)S(1)}, u32[]{:S(2)}, u32[]{:S(2)}) collective-permute-start(bf16[160,128]{1,0:T(8,128)(2,1)S(1)} %get-tuple-element.184), channel_id=1, source_target_pairs={{0,28},{4,24},{8,20},{12,16},{16,12},{20,8},{24,4},{28,0},{1,29},{... | collective-permute-start | bytes 122888 | tf_op jit(solution)/shard_map/ppermute | solution.py:526
  36.4 0.2 collective-permute-start.15
  36.6 1.0 %collective-permute-start.16 = (bf16[160,128]{1,0:T(8,128)(2,1)S(1)}, bf16[160,128]{1,0:T(8,128)(2,1)S(1)}, u32[]{:S(2)}, u32[]{:S(2)}) collective-permute-start(bf16[160,128]{1,0:T(8,128)(2,1)S(1)} %get-tuple-element.186), channel_id=1, source_target_pairs={{0,20},{4,16},{8,28},{12,24},{16,4},{20,0},{24,12},{28,8},{1,21},{... | collective-permute-start | bytes 122888 | tf_op jit(solution)/shard_map/ppermute | solution.py:526
  37.7 2.5 %collective-permute-start.17 = (bf16[160,128]{1,0:T(8,128)(2,1)S(1)}, bf16[160,128]{1,0:T(8,128)(2,1)S(1)}, u32[]{:S(2)}, u32[]{:S(2)}) collective-permute-start(bf16[160,128]{1,0:T(8,128)(2,1)S(1)} %get-tuple-element.187), channel_id=1, source_target_pairs={{0,16},{4,20},{8,24},{12,28},{16,0},{20,4},{24,8},{28,12},{1,17},{... | collective-permute-start | bytes 122888 | tf_op jit(solution)/shard_map/ppermute | solution.py:526
  40.2 0.0 collective-permute-done.13
  40.2 1.5 %collective-permute-start.18 = (bf16[160,128]{1,0:T(8,128)(2,1)S(1)}, bf16[160,128]{1,0:T(8,128)(2,1)S(1)}, u32[]{:S(2)}, u32[]{:S(2)}) collective-permute-start(bf16[160,128]{1,0:T(8,128)(2,1)S(1)} %get-tuple-element.188), channel_id=1, source_target_pairs={{0,12},{4,8},{8,4},{12,0},{16,28},{20,24},{24,20},{28,16},{1,13},{... | collective-permute-start | bytes 122888 | tf_op jit(solution)/shard_map/ppermute | solution.py:526
  41.7 0.0 collective-permute-done.14
  41.7 0.8 %collective-permute-start.19 = (bf16[160,128]{1,0:T(8,128)(2,1)S(1)}, bf16[160,128]{1,0:T(8,128)(2,1)S(1)}, u32[]{:S(2)}, u32[]{:S(2)}) collective-permute-start(bf16[160,128]{1,0:T(8,128)(2,1)S(1)} %get-tuple-element.189), channel_id=1, source_target_pairs={{0,8},{4,12},{8,0},{12,4},{16,24},{20,28},{24,16},{28,20},{1,9},{5... | collective-permute-start | bytes 122888 | tf_op jit(solution)/shard_map/ppermute | solution.py:526
  42.5 0.0 collective-permute-done.15
  42.5 1.2 %collective-permute-start.20 = (bf16[160,128]{1,0:T(8,128)(2,1)S(1)}, bf16[160,128]{1,0:T(8,128)(2,1)S(1)}, u32[]{:S(2)}, u32[]{:S(2)}) collective-permute-start(bf16[160,128]{1,0:T(8,128)(2,1)S(1)} %get-tuple-element.190), channel_id=1, source_target_pairs={{0,4},{4,0},{8,12},{12,8},{16,20},{20,16},{24,28},{28,24},{1,5},{5... | collective-permute-start | bytes 122888 | tf_op jit(solution)/shard_map/ppermute | solution.py:526
  43.7 0.6 %reduce_max.9 = f32[]{:T(128)} reduce(f32[8,128]{1,0:T(8,128)S(1)} %get-tuple-element.162, f32[]{:T(128)} %constant.47.clone.1), dimensions={0,1}, to_apply=%region_0.0 | reduce | flops 1023 | bytes 4104 | tf_op jit(solution)/shard_map/reduce_max | solution.py:635
  44.9 0.0 collective-permute-done.16
  44.9 0.0 collective-permute-done.17
  44.9 0.1 collective-permute-done.18
  45.1 0.6 %collective-permute-done.19 = bf16[160,128]{1,0:T(8,128)(2,1)S(1)} collective-permute-done((bf16[160,128]{1,0:T(8,128)(2,1)S(1)}, bf16[160,128]{1,0:T(8,128)(2,1)S(1)}, u32[]{:S(2)}, u32[]{:S(2)}) %collective-permute-start.19) | collective-permute-done | bytes 40992 | tf_op jit(solution)/shard_map/ppermute | solution.py:526
  45.7 0.8 %collective-permute-done.20 = bf16[160,128]{1,0:T(8,128)(2,1)S(1)} collective-permute-done((bf16[160,128]{1,0:T(8,128)(2,1)S(1)}, bf16[160,128]{1,0:T(8,128)(2,1)S(1)}, u32[]{:S(2)}, u32[]{:S(2)}) %collective-permute-start.20) | collective-permute-done | bytes 40992 | tf_op jit(solution)/shard_map/ppermute | solution.py:526
  46.5 0.0 copy-done
  46.5 1.1 %conditional.1 = (bf16[64,1024]{1,0:T(8,128)(2,1)}) conditional(s32[]{:T(128)} %convert_element_type.44, (bf16[64,256]{1,0:T(8,128)(2,1)S(1)}, bf16[64,1024]{1,0:T(8,128)(2,1)S(1)}, bf16[64,1024]{1,0:T(8,128)(2,1)S(1)}, bf16[64,1024]{1,0:T(8,128)(2,1)S(1)}, bf16[160,128]{1,0:T(8,128)(2,1)S(1)}, /*index=5*/bf16[160,128]{1,0:T(8,128)(2,1)S(1)}, ...), branch_computations={%region_1.0_spmd, %region_2.5_spmd} | conditional | flops 1109062016 | bytes 29252028 | solution.py:635
  46.5 1.0 %finish.2 = bf16[64,1024]{1,0:T(8,128)(2,1)} custom-call(bf16[64,256]{1,0:T(8,128)(2,1)S(1)} %get-tuple-element.66.place_ref, bf16[64,1024]{1,0:T(8,128)(2,1)S(1)} %get-tuple-element.67.residual_ref, bf16[64,1024]{1,0:T(8,128)(2,1)S(1)} %get-tuple-element.68.refs_0_, bf16[64,1024]{1,0:T(8,128)(2,1)S(1)} %get-tuple-element.69.refs_1_, ...), custom_call_target="tpu_custom_call" | custom-call | tf_op jit(solution)/shard_map/cond/branch_0_fun/finish/pallas_call | solution.py:511
  (2 shorter events, 0.0 us)
Async XLA Ops:
  7.0 11.3 %collective-permute-start.3 = (bf16[168,128]{1,0:T(8,128)(2,1)S(1)}, bf16[168,128]{1,0:T(8,128)(2,1)S(1)}, u32[]{:S(2)}, u32[]{:S(2)}) collective-permute-start(bf16[168,128]{1,0:T(8,128)(2,1)S(1)} %get-tuple-element.144), channel_id=1, source_target_pairs={{0,28},{4,24},{8,20},{12,16},{16,12},{20,8},{24,4},{28,0},{1,29},{... | collective-permute-start | bytes 129032 | tf_op jit(solution)/shard_map/ppermute | solution.py:526
  13.0 6.1 %collective-permute-start.4 = (bf16[168,128]{1,0:T(8,128)(2,1)S(1)}, bf16[168,128]{1,0:T(8,128)(2,1)S(1)}, u32[]{:S(2)}, u32[]{:S(2)}) collective-permute-start(bf16[168,128]{1,0:T(8,128)(2,1)S(1)} %get-tuple-element.145), channel_id=1, source_target_pairs={{0,24},{4,28},{8,16},{12,20},{16,8},{20,12},{24,0},{28,4},{1,25},{... | collective-permute-start | bytes 129032 | tf_op jit(solution)/shard_map/ppermute | solution.py:526
  13.2 9.1 %collective-permute-start.5 = (bf16[168,128]{1,0:T(8,128)(2,1)S(1)}, bf16[168,128]{1,0:T(8,128)(2,1)S(1)}, u32[]{:S(2)}, u32[]{:S(2)}) collective-permute-start(bf16[168,128]{1,0:T(8,128)(2,1)S(1)} %get-tuple-element.146), channel_id=1, source_target_pairs={{0,20},{4,16},{8,28},{12,24},{16,4},{20,0},{24,12},{28,8},{1,21},{... | collective-permute-start | bytes 129032 | tf_op jit(solution)/shard_map/ppermute | solution.py:526
  14.0 8.3 %collective-permute-start.6 = (bf16[168,128]{1,0:T(8,128)(2,1)S(1)}, bf16[168,128]{1,0:T(8,128)(2,1)S(1)}, u32[]{:S(2)}, u32[]{:S(2)}) collective-permute-start(bf16[168,128]{1,0:T(8,128)(2,1)S(1)} %get-tuple-element.147), channel_id=1, source_target_pairs={{0,16},{4,20},{8,24},{12,28},{16,0},{20,4},{24,8},{28,12},{1,17},{... | collective-permute-start | bytes 129032 | tf_op jit(solution)/shard_map/ppermute | solution.py:526
  16.0 6.3 %collective-permute-start.7 = (bf16[168,128]{1,0:T(8,128)(2,1)S(1)}, bf16[168,128]{1,0:T(8,128)(2,1)S(1)}, u32[]{:S(2)}, u32[]{:S(2)}) collective-permute-start(bf16[168,128]{1,0:T(8,128)(2,1)S(1)} %get-tuple-element.148), channel_id=1, source_target_pairs={{0,12},{4,8},{8,4},{12,0},{16,28},{20,24},{24,20},{28,16},{1,13},{... | collective-permute-start | bytes 129032 | tf_op jit(solution)/shard_map/ppermute | solution.py:526
  18.3 4.0 %collective-permute-start.8 = (bf16[168,128]{1,0:T(8,128)(2,1)S(1)}, bf16[168,128]{1,0:T(8,128)(2,1)S(1)}, u32[]{:S(2)}, u32[]{:S(2)}) collective-permute-start(bf16[168,128]{1,0:T(8,128)(2,1)S(1)} %get-tuple-element.149), channel_id=1, source_target_pairs={{0,8},{4,12},{8,0},{12,4},{16,24},{20,28},{24,16},{28,20},{1,9},{5... | collective-permute-start | bytes 129032 | tf_op jit(solution)/shard_map/ppermute | solution.py:526
  19.1 4.0 %collective-permute-start.9 = (bf16[168,128]{1,0:T(8,128)(2,1)S(1)}, bf16[168,128]{1,0:T(8,128)(2,1)S(1)}, u32[]{:S(2)}, u32[]{:S(2)}) collective-permute-start(bf16[168,128]{1,0:T(8,128)(2,1)S(1)} %get-tuple-element.150), channel_id=1, source_target_pairs={{0,4},{4,0},{8,12},{12,8},{16,20},{20,16},{24,28},{28,24},{1,5},{5... | collective-permute-start | bytes 129032 | tf_op jit(solution)/shard_map/ppermute | solution.py:526
  24.8 5.5 %collective-permute-start.10 = (bf16[1104,128]{1,0:T(8,128)(2,1)S(1)}, bf16[1104,128]{1,0:T(8,128)(2,1)S(1)}, u32[]{:S(2)}, u32[]{:S(2)}) collective-permute-start(bf16[1104,128]{1,0:T(8,128)(2,1)S(1)} %get-tuple-element.165), channel_id=1, source_target_pairs={{0,1},{1,0},{2,3},{3,2},{4,5},{5,4},{6,7},{7,6},{8,9},{9,8},{10,11... | collective-permute-start | bytes 847880 | tf_op jit(solution)/shard_map/ppermute | solution.py:526
  24.8 5.0 %collective-permute-start.12 = (bf16[80,128]{1,0:T(8,128)(2,1)S(1)}, bf16[80,128]{1,0:T(8,128)(2,1)S(1)}, u32[]{:S(2)}, u32[]{:S(2)}) collective-permute-start(bf16[80,128]{1,0:T(8,128)(2,1)S(1)} %get-tuple-element.168.refs_0_), channel_id=1, source_target_pairs={{0,3},{1,2},{2,1},{3,0},{4,7},{5,6},{6,5},{7,4},{8,11},{9,10},{10,... | collective-permute-start | bytes 61448 | tf_op jit(solution)/shard_map/ppermute | solution.py:526
  26.5 3.8 %collective-permute-start.11 = (bf16[80,128]{1,0:T(8,128)(2,1)S(1)}, bf16[80,128]{1,0:T(8,128)(2,1)S(1)}, u32[]{:S(2)}, u32[]{:S(2)}) collective-permute-start(bf16[80,128]{1,0:T(8,128)(2,1)S(1)} %get-tuple-element.168.refs_0_), channel_id=1, source_target_pairs={{0,2},{1,3},{2,0},{3,1},{4,6},{5,7},{6,4},{7,5},{8,10},{9,11},{10,... | collective-permute-start | bytes 61448 | tf_op jit(solution)/shard_map/ppermute | solution.py:526
  29.8 16.7 %copy-start = (s32[32]{0:T(128)S(1)}, s32[32]{0:T(128)}, u32[]{:S(2)}) copy-start(s32[32]{0:T(128)} %param.22) | copy-start | bytes 388
  29.8 16.7 %copy-start.2 = (bf16[64,1024]{1,0:T(8,128)(2,1)S(1)}, bf16[64,1024]{1,0:T(8,128)(2,1)}, u32[]{:S(2)}) copy-start(bf16[64,1024]{1,0:T(8,128)(2,1)} %param.21) | copy-start | bytes 393220
  29.8 16.7 %copy-start.3 = (s32[64,1]{0,1:T(1,128)S(1)}, s32[64,1]{0,1:T(1,128)}, u32[]{:S(2)}) copy-start(s32[64,1]{0,1:T(1,128)} %param.23) | copy-start | bytes 772
  31.4 8.8 %collective-permute-start.13 = (bf16[64,1024]{1,0:T(8,128)(2,1)S(1)}, bf16[64,1024]{1,0:T(8,128)(2,1)S(1)}, u32[]{:S(2)}, u32[]{:S(2)}) collective-permute-start(bf16[64,1024]{1,0:T(8,128)(2,1)S(1)} %get-tuple-element.180), channel_id=1, source_target_pairs={{0,2},{1,3},{2,0},{3,1},{4,6},{5,7},{6,4},{7,5},{8,10},{9,11},{10,... | collective-permute-start | bytes 393224 | tf_op jit(solution)/shard_map/ppermute | solution.py:526
  32.5 9.2 %collective-permute-start.14 = (bf16[160,128]{1,0:T(8,128)(2,1)S(1)}, bf16[160,128]{1,0:T(8,128)(2,1)S(1)}, u32[]{:S(2)}, u32[]{:S(2)}) collective-permute-start(bf16[160,128]{1,0:T(8,128)(2,1)S(1)} %get-tuple-element.184), channel_id=1, source_target_pairs={{0,28},{4,24},{8,20},{12,16},{16,12},{20,8},{24,4},{28,0},{1,29},{... | collective-permute-start | bytes 122888 | tf_op jit(solution)/shard_map/ppermute | solution.py:526
  36.4 6.1 %collective-permute-start.15 = (bf16[160,128]{1,0:T(8,128)(2,1)S(1)}, bf16[160,128]{1,0:T(8,128)(2,1)S(1)}, u32[]{:S(2)}, u32[]{:S(2)}) collective-permute-start(bf16[160,128]{1,0:T(8,128)(2,1)S(1)} %get-tuple-element.185), channel_id=1, source_target_pairs={{0,24},{4,28},{8,16},{12,20},{16,8},{20,12},{24,0},{28,4},{1,25},{... | collective-permute-start | bytes 122888 | tf_op jit(solution)/shard_map/ppermute | solution.py:526
  36.6 8.3 %collective-permute-start.16 = (bf16[160,128]{1,0:T(8,128)(2,1)S(1)}, bf16[160,128]{1,0:T(8,128)(2,1)S(1)}, u32[]{:S(2)}, u32[]{:S(2)}) collective-permute-start(bf16[160,128]{1,0:T(8,128)(2,1)S(1)} %get-tuple-element.186), channel_id=1, source_target_pairs={{0,20},{4,16},{8,28},{12,24},{16,4},{20,0},{24,12},{28,8},{1,21},{... | collective-permute-start | bytes 122888 | tf_op jit(solution)/shard_map/ppermute | solution.py:526
  37.7 7.3 %collective-permute-start.17 = (bf16[160,128]{1,0:T(8,128)(2,1)S(1)}, bf16[160,128]{1,0:T(8,128)(2,1)S(1)}, u32[]{:S(2)}, u32[]{:S(2)}) collective-permute-start(bf16[160,128]{1,0:T(8,128)(2,1)S(1)} %get-tuple-element.187), channel_id=1, source_target_pairs={{0,16},{4,20},{8,24},{12,28},{16,0},{20,4},{24,8},{28,12},{1,17},{... | collective-permute-start | bytes 122888 | tf_op jit(solution)/shard_map/ppermute | solution.py:526
  40.2 4.9 %collective-permute-start.18 = (bf16[160,128]{1,0:T(8,128)(2,1)S(1)}, bf16[160,128]{1,0:T(8,128)(2,1)S(1)}, u32[]{:S(2)}, u32[]{:S(2)}) collective-permute-start(bf16[160,128]{1,0:T(8,128)(2,1)S(1)} %get-tuple-element.188), channel_id=1, source_target_pairs={{0,12},{4,8},{8,4},{12,0},{16,28},{20,24},{24,20},{28,16},{1,13},{... | collective-permute-start | bytes 122888 | tf_op jit(solution)/shard_map/ppermute | solution.py:526
  41.7 4.0 %collective-permute-start.19 = (bf16[160,128]{1,0:T(8,128)(2,1)S(1)}, bf16[160,128]{1,0:T(8,128)(2,1)S(1)}, u32[]{:S(2)}, u32[]{:S(2)}) collective-permute-start(bf16[160,128]{1,0:T(8,128)(2,1)S(1)} %get-tuple-element.189), channel_id=1, source_target_pairs={{0,8},{4,12},{8,0},{12,4},{16,24},{20,28},{24,16},{28,20},{1,9},{5... | collective-permute-start | bytes 122888 | tf_op jit(solution)/shard_map/ppermute | solution.py:526
  42.5 4.0 %collective-permute-start.20 = (bf16[160,128]{1,0:T(8,128)(2,1)S(1)}, bf16[160,128]{1,0:T(8,128)(2,1)S(1)}, u32[]{:S(2)}, u32[]{:S(2)}) collective-permute-start(bf16[160,128]{1,0:T(8,128)(2,1)S(1)} %get-tuple-element.190), channel_id=1, source_target_pairs={{0,4},{4,0},{8,12},{12,8},{16,20},{20,16},{24,28},{28,24},{1,5},{5... | collective-permute-start | bytes 122888 | tf_op jit(solution)/shard_map/ppermute | solution.py:526
